TPU v7x, 32 devices: a whole 2x2x4 slice. The times are simulated.
32 devices in a mesh: expert: 4 (over y, core), shard: 8 (over z, x).
Axes of the slice: x: 2, y: 2, z: 4, core: 2. Of those that a mesh axis runs over, the one named last changes fastest.
Arguments:
- inputs: bfloat16 [2, 4096, 1536], P(None, ('expert', 'shard')), may hold values from -6 to 6
- cotangent: bfloat16 [2, 4096, 1536], P(None, ('expert', 'shard')), may hold values from -6 to 6
- lengths: int32 [2, 32, 3], P(None, ('expert', 'shard')), may hold values from 1 to 64, 128 in all within a row
- routes: int32 [2, 4096, 8], P(None, ('expert', 'shard')), may hold values from 0 to 39, all different within a row; in each aligned block of 128 rows (0 to 127, 128 to 255, ..., all dimensions but the last counted through in order) at most 40 rows name the same one
- norm_gain_one: bfloat16 [1536], P(('expert', 'shard')), may hold values from 0.5 to 1.5
- w_query: bfloat16 [1536, 1536], P(('expert', 'shard')), may hold values from -0.15625 to 0.15625
- key_projection_weight: bfloat16 [1536, 512], P(('expert', 'shard')), may hold values from -0.15625 to 0.15625
- value_projection_weight: bfloat16 [1536, 512], P(('expert', 'shard')), may hold values from -0.15625 to 0.15625
- w_out: bfloat16 [1536, 1536], P(('expert', 'shard')), may hold values from -0.4375 to 0.4375
- norm_gain_two: bfloat16 [1536], P(('expert', 'shard')), may hold values from 0.5 to 1.5
- w_router: bfloat16 [1536, 40], P(('expert', 'shard')), may hold values from -0.078125 to 0.078125
- w_gate: bfloat16 [40, 1536, 512], P('expert', 'shard'), may hold values from -0.15625 to 0.15625
- w_up: bfloat16 [40, 1536, 512], P('expert', 'shard'), may hold values from -0.15625 to 0.15625
- w_down: bfloat16 [40, 512, 1536], P('expert', 'shard'), may hold values from -0.5 to 0.5
Outputs:
- outputs: bfloat16 [2, 4096, 1536], P(None, ('expert', 'shard'))
- grad_inputs: float32 [2, 4096, 1536], P(None, ('expert', 'shard'))
- grad_norm_gain_one: float32 [1536], P(('expert', 'shard'))
- grad_w_query: float32 [1536, 1536], P(('expert', 'shard'))
- grad_w_key: float32 [1536, 512], P(('expert', 'shard'))
- grad_w_value: float32 [1536, 512], P(('expert', 'shard'))
- grad_w_out: float32 [1536, 1536], P(('expert', 'shard'))
- grad_norm_gain_two: float32 [1536], P(('expert', 'shard'))
- grad_w_router: float32 [1536, 40], P(('expert', 'shard'))
- grad_w_gate: float32 [40, 1536, 512], P('expert', 'shard')
- grad_w_up: float32 [40, 1536, 512], P('expert', 'shard')
- grad_w_down: float32 [40, 512, 1536], P('expert', 'shard')
Inputs may be any that keep to these rules, and one draw needn't show every extreme that they name: `routes`: in the rows of one device in one micro-batch no expert is named more than 40 times, a bound that some devices reach for some expert; each row names 8 different experts. The 3 lengths of one device in one micro-batch sum to 128, the largest being exactly 64.
All inputs are finite; a program needn't handle non-finite values.
Results may differ from a plain program's by a relative error of at most 0.015.
Values may be sent and summed in bfloat16 or wider, within the bound.
No kernel may reach another device: no remote copies, remote signals or barrier semaphores. Data moves between devices by JAX's collectives and lax.ppermute only.
A program may use at most 384 MiB of HBM per device.

v0:
```python
import math

import jax
import jax.numpy as jnp
from jax import lax
from jax.sharding import PartitionSpec as P

MODEL_WIDTH = 1536
QUERY_HEADS = 24
KEY_VALUE_HEADS = 8
HEAD_SIZE = 64
E = 40
TOPK = 8
CAP = 40


epsilon = 1e-05


def for_sending(array):
    return jax.tree.map(lambda a: a.astype(jnp.bfloat16) if a.dtype == jnp.float32 else a, array)


def positions(lengths, count_of_tokens):
    seq_ends = jnp.cumsum(lengths)
    starts = seq_ends - lengths
    token_index = jnp.arange(count_of_tokens, dtype=jnp.int32)
    segment = jnp.sum((token_index[:, None] >= seq_ends[None, :]).astype(jnp.int32), axis=1)
    choose = segment[:, None] == jnp.arange(lengths.shape[0], dtype=jnp.int32)[None, :]
    offset = jnp.sum(jnp.where(choose, starts[None, :], 0), axis=1)
    return (segment, token_index - offset)


def rotary_embedding(values_in, token_position, direction):
    half_size = values_in.shape[-1] // 2
    frequency = jnp.exp(jnp.arange(half_size, dtype=jnp.float32) * (-math.log(10000.0) / half_size))
    angles = token_position.astype(jnp.float32)[..., None] * frequency
    cosine = jnp.cos(angles)[..., None, :]
    sine_part = jnp.sin(angles)[..., None, :]
    first_half = values_in[..., :half_size]
    second_half = values_in[..., half_size:]
    return jnp.concatenate(
        [
            first_half * cosine - direction * second_half * sine_part,
            second_half * cosine + direction * first_half * sine_part,
        ],
        axis=-1,
    )


def slot_positions(routes, experts_total):
    flat_routes = routes.reshape(routes.shape[:-2] + (-1,))
    onehot = (flat_routes[..., None] == jnp.arange(experts_total, dtype=jnp.int32)).astype(
        jnp.int32
    )
    before = jnp.cumsum(onehot, axis=-2) - onehot
    return jnp.sum(before * onehot, axis=-1).reshape(routes.shape)


def attention_scores(query_rows_rotated, projected_key_rows, allowed, score_scale):
    scores = (
        jnp.einsum(
            "qkgd,skd->kgqs",
            query_rows_rotated,
            projected_key_rows,
            preferred_element_type=jnp.float32,
        )
        * score_scale
    )
    return jnp.where(allowed, scores, -1000000000.0)


def norm_back(grad_normed, values_in, inverse_root, gain):
    scaled = grad_normed * gain
    grad_gain = jnp.sum(grad_normed * values_in * inverse_root, axis=0)
    cubed = inverse_root * inverse_root * inverse_root
    grad_values = inverse_root * scaled - values_in * cubed * jnp.mean(
        scaled * values_in, axis=-1, keepdims=True
    )
    return (grad_values, grad_gain)


def add_into(earlier, term):
    if earlier is None:
        return term
    return earlier + term


def micro_step(
    inputs, cotangent, lengths, routes, attn_whole, expert_whole, attn_before, expert_before
):
    gain_one, w_query, key_projection_weight, value_projection_weight, w_out, gain_two, w_router = (
        attn_whole
    )
    w_gate, w_up, w_down = expert_whole
    count_of_tokens = inputs.shape[0]
    local_count = w_gate.shape[0]
    groups = lax.axis_size("expert")
    query_per_group = QUERY_HEADS // KEY_VALUE_HEADS
    score_scale = 1.0 / math.sqrt(HEAD_SIZE)
    act_rows = inputs.astype(jnp.float32)
    r_one = lax.rsqrt(jnp.mean(act_rows * act_rows, axis=-1, keepdims=True) + epsilon)
    gain_first = gain_one.astype(jnp.float32)
    normalized_input = (act_rows * r_one * gain_first).astype(jnp.bfloat16)
    query_pre = jnp.dot(normalized_input, w_query, preferred_element_type=jnp.float32)
    key_before_rotation = jnp.dot(
        normalized_input, key_projection_weight, preferred_element_type=jnp.float32
    )
    projected_value_rows = (
        jnp.dot(normalized_input, value_projection_weight, preferred_element_type=jnp.float32)
        .astype(jnp.bfloat16)
        .reshape(count_of_tokens, KEY_VALUE_HEADS, HEAD_SIZE)
    )
    segment, token_position = positions(lengths, count_of_tokens)
    query_rows_rotated = (
        rotary_embedding(
            query_pre.reshape(count_of_tokens, QUERY_HEADS, HEAD_SIZE), token_position, 1.0
        )
        .astype(jnp.bfloat16)
        .reshape(count_of_tokens, KEY_VALUE_HEADS, query_per_group, HEAD_SIZE)
    )
    projected_key_rows = rotary_embedding(
        key_before_rotation.reshape(count_of_tokens, KEY_VALUE_HEADS, HEAD_SIZE),
        token_position,
        1.0,
    ).astype(jnp.bfloat16)
    token_index = jnp.arange(count_of_tokens, dtype=jnp.int32)
    allowed = (segment[:, None] == segment[None, :]) & (
        token_index[:, None] >= token_index[None, :]
    )
    scores = attention_scores(query_rows_rotated, projected_key_rows, allowed, score_scale)
    row_max = jnp.max(scores, axis=-1, keepdims=True)
    shifted = jnp.exp(scores - row_max)
    row_total = jnp.sum(shifted, axis=-1, keepdims=True)
    log_total = row_max + jnp.log(row_total)
    probs_low = (shifted / row_total).astype(jnp.bfloat16)
    mixed = jnp.einsum(
        "kgqs,skd->qkgd", probs_low, projected_value_rows, preferred_element_type=jnp.float32
    )
    mixed = mixed.reshape(count_of_tokens, QUERY_HEADS * HEAD_SIZE).astype(jnp.bfloat16)
    resid = act_rows + jnp.dot(mixed, w_out, preferred_element_type=jnp.float32)
    r_two = lax.rsqrt(jnp.mean(resid * resid, axis=-1, keepdims=True) + epsilon)
    gain_second = gain_two.astype(jnp.float32)
    normed_two = (resid * r_two * gain_second).astype(jnp.bfloat16)
    logits = jnp.dot(normed_two, w_router, preferred_element_type=jnp.float32)
    chance = jax.nn.softmax(logits, axis=-1)
    onehot_routes = (routes[..., None] == jnp.arange(E, dtype=jnp.int32)).astype(jnp.float32)
    picked = jnp.sum(onehot_routes * chance[:, None, :], axis=-1)
    picked_total = jnp.sum(picked, axis=-1, keepdims=True)
    gate_weights = picked / picked_total
    slot_index = slot_positions(routes, E)
    target = (routes * CAP + slot_index).reshape(-1)
    outbound = (
        jnp.zeros((E * CAP, MODEL_WIDTH), jnp.bfloat16)
        .at[target]
        .set(jnp.repeat(normed_two, TOPK, axis=0))
    )
    arrived = lax.all_to_all(
        outbound.reshape(groups, local_count * CAP, MODEL_WIDTH),
        "expert",
        split_axis=0,
        concat_axis=0,
        tiled=True,
    )
    arrived = arrived.reshape(groups, local_count, CAP, MODEL_WIDTH)
    gate_part = jnp.einsum("slcd,ldf->slcf", arrived, w_gate, preferred_element_type=jnp.float32)
    up_part = jnp.einsum("slcd,ldf->slcf", arrived, w_up, preferred_element_type=jnp.float32)
    sigmoid_gate = jax.nn.sigmoid(gate_part)
    active = (gate_part * sigmoid_gate * up_part).astype(jnp.bfloat16)
    result = jnp.einsum(
        "slcf,lfd->slcd", active, w_down, preferred_element_type=jnp.float32
    ).astype(jnp.bfloat16)
    returned_rows = lax.all_to_all(
        result.reshape(groups, local_count * CAP, MODEL_WIDTH),
        "expert",
        split_axis=0,
        concat_axis=0,
        tiled=True,
    )
    returned = (
        returned_rows.reshape(E * CAP, MODEL_WIDTH)[target]
        .reshape(count_of_tokens, TOPK, MODEL_WIDTH)
        .astype(jnp.float32)
    )
    output = resid + jnp.sum(gate_weights[..., None] * returned, axis=1)
    grad_final = cotangent.astype(jnp.float32)
    grad_returned = (gate_weights[..., None] * grad_final[:, None, :]).astype(jnp.bfloat16)
    grad_gates = jnp.sum(returned * grad_final[:, None, :], axis=-1)
    outbound_grad = (
        jnp.zeros((E * CAP, MODEL_WIDTH), jnp.bfloat16)
        .at[target]
        .set(grad_returned.reshape(-1, MODEL_WIDTH))
    )
    arrived_grad = lax.all_to_all(
        outbound_grad.reshape(groups, local_count * CAP, MODEL_WIDTH),
        "expert",
        split_axis=0,
        concat_axis=0,
        tiled=True,
    )
    arrived_grad = arrived_grad.reshape(groups, local_count, CAP, MODEL_WIDTH)
    grad_active = jnp.einsum(
        "slcd,lfd->slcf", arrived_grad, w_down, preferred_element_type=jnp.float32
    )
    grad_w_down = add_into(
        expert_before[2],
        jnp.einsum("slcf,slcd->lfd", active, arrived_grad, preferred_element_type=jnp.float32),
    )
    grad_gate = (
        grad_active * up_part * sigmoid_gate * (1.0 + gate_part * (1.0 - sigmoid_gate))
    ).astype(jnp.bfloat16)
    grad_up = (grad_active * gate_part * sigmoid_gate).astype(jnp.bfloat16)
    grad_w_gate = add_into(
        expert_before[0],
        jnp.einsum("slcd,slcf->ldf", arrived, grad_gate, preferred_element_type=jnp.float32),
    )
    grad_w_up = add_into(
        expert_before[1],
        jnp.einsum("slcd,slcf->ldf", arrived, grad_up, preferred_element_type=jnp.float32),
    )
    grad_in = jnp.einsum("slcf,ldf->slcd", grad_gate, w_gate, preferred_element_type=jnp.float32)
    grad_in = (
        grad_in + jnp.einsum("slcf,ldf->slcd", grad_up, w_up, preferred_element_type=jnp.float32)
    ).astype(jnp.bfloat16)
    grad_back = lax.all_to_all(
        grad_in.reshape(groups, local_count * CAP, MODEL_WIDTH),
        "expert",
        split_axis=0,
        concat_axis=0,
        tiled=True,
    )
    grad_back = (
        grad_back.reshape(E * CAP, MODEL_WIDTH)[target]
        .reshape(count_of_tokens, TOPK, MODEL_WIDTH)
        .astype(jnp.float32)
    )
    grad_picked = (
        grad_gates - jnp.sum(grad_gates * gate_weights, axis=-1, keepdims=True)
    ) / picked_total
    grad_chance = jnp.sum(onehot_routes * grad_picked[..., None], axis=1)
    grad_logits = (
        chance * (grad_chance - jnp.sum(chance * grad_chance, axis=-1, keepdims=True))
    ).astype(jnp.bfloat16)
    grad_w_router = add_into(
        attn_before[6],
        jnp.einsum("nd,ne->de", normed_two, grad_logits, preferred_element_type=jnp.float32),
    )
    grad_normed_two = jnp.sum(grad_back, axis=1) + jnp.einsum(
        "ne,de->nd", grad_logits, w_router, preferred_element_type=jnp.float32
    )
    grad_resid, grad_gain_two = norm_back(grad_normed_two, resid, r_two, gain_second)
    grad_gain_two = add_into(attn_before[5], grad_gain_two)
    grad_resid = grad_final + grad_resid
    grad_att = grad_resid.astype(jnp.bfloat16)
    grad_w_out = add_into(
        attn_before[4], jnp.einsum("nf,nd->fd", mixed, grad_att, preferred_element_type=jnp.float32)
    )
    mixed_gradient = jnp.einsum(
        "nd,fd->nf", grad_att, w_out, preferred_element_type=jnp.float32
    ).astype(jnp.bfloat16)
    mixed_gradient = mixed_gradient.reshape(
        count_of_tokens, KEY_VALUE_HEADS, query_per_group, HEAD_SIZE
    )
    probs_again = jnp.exp(
        attention_scores(query_rows_rotated, projected_key_rows, allowed, score_scale) - log_total
    )
    grad_probs = jnp.einsum(
        "qkgd,skd->kgqs", mixed_gradient, projected_value_rows, preferred_element_type=jnp.float32
    )
    value_input_gradient = jnp.einsum(
        "kgqs,qkgd->skd", probs_low, mixed_gradient, preferred_element_type=jnp.float32
    )
    value_input_gradient = value_input_gradient.reshape(
        count_of_tokens, KEY_VALUE_HEADS * HEAD_SIZE
    ).astype(jnp.bfloat16)
    grad_scores = (
        probs_again * (grad_probs - jnp.sum(probs_again * grad_probs, axis=-1, keepdims=True))
    ).astype(jnp.bfloat16)
    grad_query = (
        jnp.einsum(
            "kgqs,skd->qkgd", grad_scores, projected_key_rows, preferred_element_type=jnp.float32
        )
        * score_scale
    )
    key_gradient_rows = (
        jnp.einsum(
            "kgqs,qkgd->skd", grad_scores, query_rows_rotated, preferred_element_type=jnp.float32
        )
        * score_scale
    )
    grad_query_pre = (
        rotary_embedding(
            grad_query.reshape(count_of_tokens, QUERY_HEADS, HEAD_SIZE), token_position, -1.0
        )
        .reshape(count_of_tokens, QUERY_HEADS * HEAD_SIZE)
        .astype(jnp.bfloat16)
    )
    grad_key_pre = (
        rotary_embedding(key_gradient_rows, token_position, -1.0)
        .reshape(count_of_tokens, KEY_VALUE_HEADS * HEAD_SIZE)
        .astype(jnp.bfloat16)
    )
    grad_w_query = add_into(
        attn_before[1],
        jnp.einsum(
            "nd,nf->df", normalized_input, grad_query_pre, preferred_element_type=jnp.float32
        ),
    )
    grad_w_key = add_into(
        attn_before[2],
        jnp.einsum("nd,nf->df", normalized_input, grad_key_pre, preferred_element_type=jnp.float32),
    )
    grad_w_value = add_into(
        attn_before[3],
        jnp.einsum(
            "nd,nf->df", normalized_input, value_input_gradient, preferred_element_type=jnp.float32
        ),
    )
    grad_normed = jnp.einsum(
        "nf,df->nd", grad_query_pre, w_query, preferred_element_type=jnp.float32
    )
    grad_normed = grad_normed + jnp.einsum(
        "nf,df->nd", grad_key_pre, key_projection_weight, preferred_element_type=jnp.float32
    )
    grad_normed = grad_normed + jnp.einsum(
        "nf,df->nd",
        value_input_gradient,
        value_projection_weight,
        preferred_element_type=jnp.float32,
    )
    grad_rows, grad_gain_one = norm_back(grad_normed, act_rows, r_one, gain_first)
    grad_gain_one = add_into(attn_before[0], grad_gain_one)
    grad_rows = grad_resid + grad_rows
    attn_grad = (
        grad_gain_one,
        grad_w_query,
        grad_w_key,
        grad_w_value,
        grad_w_out,
        grad_gain_two,
        grad_w_router,
    )
    expert_grad = (grad_w_gate, grad_w_up, grad_w_down)
    return (output.astype(jnp.bfloat16), grad_rows, attn_grad, expert_grad)


def body(
    inputs,
    cotangent,
    lengths,
    routes,
    norm_gain_one,
    w_query,
    key_projection_weight,
    value_projection_weight,
    w_out,
    norm_gain_two,
    w_router,
    w_gate,
    w_up,
    w_down,
):
    attn_whole = (
        lax.all_gather(norm_gain_one, ("expert", "shard"), axis=0, tiled=True),
        lax.all_gather(w_query, ("expert", "shard"), axis=0, tiled=True),
        lax.all_gather(key_projection_weight, ("expert", "shard"), axis=0, tiled=True),
        lax.all_gather(value_projection_weight, ("expert", "shard"), axis=0, tiled=True),
        lax.all_gather(w_out, ("expert", "shard"), axis=0, tiled=True),
        lax.all_gather(norm_gain_two, ("expert", "shard"), axis=0, tiled=True),
        lax.all_gather(w_router, ("expert", "shard"), axis=0, tiled=True),
    )
    expert_whole = (
        lax.all_gather(w_gate, "shard", axis=1, tiled=True),
        lax.all_gather(w_up, "shard", axis=1, tiled=True),
        lax.all_gather(w_down, "shard", axis=1, tiled=True),
    )
    outputs = []
    grad_inputs = []
    empty_attn = (None,) * 7
    empty_expert = (None,) * 3
    attn_sums = empty_attn
    expert_sums = empty_expert
    for micro_index in range(inputs.shape[0]):
        output, grad_rows, attn_sums, expert_sums = micro_step(
            inputs[micro_index],
            cotangent[micro_index],
            lengths[micro_index, 0],
            routes[micro_index],
            attn_whole,
            expert_whole,
            attn_sums,
            expert_sums,
        )
        outputs.append(output)
        grad_inputs.append(grad_rows)
    attn_sums = lax.psum_scatter(
        tuple(attn_sums), ("expert", "shard"), scatter_dimension=0, tiled=True
    )
    expert_sums = jax.tree.map(
        lambda part: part.astype(jnp.float32),
        lax.psum_scatter(for_sending(tuple(expert_sums)), "shard", scatter_dimension=1, tiled=True),
    )
    return (jnp.stack(outputs), jnp.stack(grad_inputs)) + tuple(attn_sums) + tuple(expert_sums)


def solution(mesh):
    return jax.shard_map(
        body,
        mesh=mesh,
        in_specs=(
            P(None, ("expert", "shard"), None),
            P(None, ("expert", "shard"), None),
            P(None, ("expert", "shard"), None),
            P(None, ("expert", "shard"), None),
            P(("expert", "shard")),
            P(("expert", "shard"), None),
            P(("expert", "shard"), None),
            P(("expert", "shard"), None),
            P(("expert", "shard"), None),
            P(("expert", "shard")),
            P(("expert", "shard"), None),
            P("expert", "shard", None),
            P("expert", "shard", None),
            P("expert", "shard", None),
        ),
        out_specs=(
            P(None, ("expert", "shard"), None),
            P(None, ("expert", "shard"), None),
            P(("expert", "shard")),
            P(("expert", "shard"), None),
            P(("expert", "shard"), None),
            P(("expert", "shard"), None),
            P(("expert", "shard"), None),
            P(("expert", "shard")),
            P(("expert", "shard"), None),
            P("expert", "shard", None),
            P("expert", "shard", None),
            P("expert", "shard", None),
        ),
        check_vma=False,
    )
```

profile of v0, /device:TPU:1, one launch (start us, length us, event | category | flops | bytes accessed | tf_op | source)
XLA Modules:
  0.0 2659.1 jit_solution(13211037078474270568)
XLA Ops:
  13.1 40.7 %all-reduce.5 = (bf16[1536]{0:T(1024)(128)(2,1)S(1)}, bf16[1536]{0:T(1024)(128)(2,1)S(1)}) all-reduce(bf16[1536]{0:T(1024)(128)(2,1)S(1)} %dynamic-update-slice, bf16[1536]{0:T(1024)(128)(2,1)S(1)} %dynamic-update-slice.1), channel_id=1, replica_groups=mesh['expert'=4,'shard'=8] {'expert','shard'}, use_global_device_ids=true, to_apply=%add | all-reduce | flops 3072 | bytes 12288
  54.1 11.3 reduce-window.29
  70.8 55.0 %all-gather.11.cloned.1.call-done = bf16[1536,512]{1,0:T(8,128)(2,1)} async-done(((bf16[48,512]{1,0:T(8,128)(2,1)}), bf16[1536,512]{1,0:T(8,128)(2,1)}) %all-gather.11.cloned.1.call-update) | async-done | bytes 1572880 | tf_op jit(solution)/shard_map/all_gather | solution.py:366
  128.2 63.2 %all-gather.13.cloned.1.call-done = bf16[1536,1536]{1,0:T(8,128)(2,1)} async-done(((bf16[48,1536]{1,0:T(8,128)(2,1)}), bf16[1536,1536]{1,0:T(8,128)(2,1)}) %all-gather.13.cloned.1.call-update) | async-done | bytes 4718608 | tf_op jit(solution)/shard_map/all_gather | solution.py:365
  205.0 51.7 %all-gather.15.cloned.1.call-done = bf16[1536,1536]{1,0:T(8,128)(2,1)} async-done(((bf16[48,1536]{1,0:T(8,128)(2,1)}), bf16[1536,1536]{1,0:T(8,128)(2,1)}) %all-gather.15.cloned.1.call-update) | async-done | bytes 4718608 | tf_op jit(solution)/shard_map/all_gather | solution.py:368
  275.2 65.8 %all-gather = bf16[32,48,40]{1,2,0:T(8,128)(2,1)S(1)} all-gather(bf16[1,48,40]{1,2,0:T(8,128)(2,1)S(1)} %bitcast.627), channel_id=1, replica_groups=mesh['expert'=4,'shard'=8] {'expert','shard'}, dimensions={0}, use_global_device_ids=true | all-gather | bytes 126720 | tf_op jit(solution)/shard_map/all_gather | solution.py:370
  343.1 8.9 scatter_custom_fusion.2
  352.0 12.5 all-to-all-start.4
  364.7 11.3 reduce-window.38
  376.5 98.1 %all-gather.19.cloned.1.call-done = bf16[10,1536,512]{2,1,0:T(8,128)(2,1)} async-done(((bf16[10,192,512]{2,1,0:T(8,128)(2,1)}), bf16[10,1536,512]{2,1,0:T(8,128)(2,1)}) %all-gather.19.cloned.1.call-update) | async-done | bytes 15728656 | tf_op jit(solution)/shard_map/all_gather | solution.py:374
  474.6 11.7 fusion.17
  486.3 203.4 %all-gather.17.cloned.1.call-done = bf16[10,1536,512]{2,1,0:T(8,128)(2,1)} async-done(((bf16[10,192,512]{2,1,0:T(8,128)(2,1)}), bf16[10,1536,512]{2,1,0:T(8,128)(2,1)}) %all-gather.17.cloned.1.call-update) | async-done | bytes 15728656 | tf_op jit(solution)/shard_map/all_gather | solution.py:373
  689.8 11.8 fusion.25
  701.6 203.4 %all-gather.21.cloned.1.call-done = bf16[10,512,1536]{2,1,0:T(8,128)(2,1)} async-done(((bf16[10,64,1536]{2,1,0:T(8,128)(2,1)}), bf16[10,512,1536]{2,1,0:T(8,128)(2,1)}) %all-gather.21.cloned.1.call-update) | async-done | bytes 15728656 | tf_op jit(solution)/shard_map/all_gather | solution.py:375
  905.0 12.9 fusion.63
  917.8 9.3 convert_bitcast_fusion.1
  938.9 14.4 fusion.13
  953.3 13.0 fusion.50
  971.2 20.2 all-to-all-done.1
  1007.1 9.7 gather_fusion
  1022.0 30.6 %all-to-all-done.5 = bf16[4,400,1536]{2,1,0:T(8,128)(2,1)} async-done(((bf16[4,400,1536]{2,1,0:T(8,128)(2,1)}), bf16[4,400,1536]{2,1,0:T(8,128)(2,1)}, u32[]{:S(2)}, u32[]{:S(2)}) %all-to-all-start.5) | async-done | bytes 4915232 | tf_op jit(solution)/shard_map/all_to_all | solution.py:225
  1052.7 9.7 gather_fusion.2
  1082.8 8.9 scatter_custom_fusion.3
  1091.7 44.5 %all-to-all-done.2 = bf16[4,400,1536]{2,1,0:T(8,128)(2,1)} async-done(((bf16[4,400,1536]{2,1,0:T(8,128)(2,1)}), bf16[4,400,1536]{2,1,0:T(8,128)(2,1)}, u32[]{:S(2)}, u32[]{:S(2)}) %all-to-all-start.2) | async-done | bytes 4915232 | tf_op jit(solution)/shard_map/all_to_all | solution.py:158
  1142.5 11.7 fusion.15
  1154.3 11.7 fusion.23
  1166.0 31.6 %all-to-all-done.6 = bf16[4,400,1536]{2,1,0:T(8,128)(2,1)} async-done(((bf16[4,400,1536]{2,1,0:T(8,128)(2,1)}), bf16[4,400,1536]{2,1,0:T(8,128)(2,1)}, u32[]{:S(2)}, u32[]{:S(2)}) %all-to-all-start.6) | async-done | bytes 4915232 | tf_op jit(solution)/shard_map/all_to_all | solution.py:194
  1197.6 12.9 fusion.58
  1228.0 15.0 fusion.43
  1243.9 39.2 %all-to-all-done.3 = bf16[4,400,1536]{2,1,0:T(8,128)(2,1)} async-done(((bf16[4,400,1536]{2,1,0:T(8,128)(2,1)}), bf16[4,400,1536]{2,1,0:T(8,128)(2,1)}, u32[]{:S(2)}, u32[]{:S(2)}) %all-to-all-start.3) | async-done | bytes 4915232 | tf_op jit(solution)/shard_map/all_to_all | solution.py:173
  1283.1 9.7 gather_fusion.1
  1303.5 20.0 fusion
  1324.9 15.5 fusion.96
  1340.3 20.6 fusion.2
  1362.4 15.6 fusion.93
  1377.9 19.8 fusion.1
  1399.2 14.5 fusion.11
  1413.6 12.4 fusion.53
  1437.2 55.1 %all-to-all-done.7 = bf16[4,400,1536]{2,1,0:T(8,128)(2,1)} async-done(((bf16[4,400,1536]{2,1,0:T(8,128)(2,1)}), bf16[4,400,1536]{2,1,0:T(8,128)(2,1)}, u32[]{:S(2)}, u32[]{:S(2)}) %all-to-all-start.7) | async-done | bytes 4915232 | tf_op jit(solution)/shard_map/all_to_all | solution.py:225
  1492.3 10.1 gather_fusion.3
  1561.8 41.2 %all-reduce.4 = (f32[1536]{0:T(1024)}, f32[1536]{0:T(1024)}) all-reduce(f32[1536]{0:T(1024)} %add.282, f32[1536]{0:T(1024)S(1)} %copy-done.101), channel_id=2, replica_groups=mesh['expert'=4,'shard'=8] {'expert','shard'}, use_global_device_ids=true, to_apply=%region_52.53.clone | all-reduce | flops 3072 | bytes 24576
  1613.0 38.3 %reduce-scatter.23.cloned.1.call-done = bf16[10,64,1536]{2,1,0:T(8,128)(2,1)} async-done(((bf16[10,512,1536]{2,1,0:T(8,128)(2,1)}), bf16[10,64,1536]{2,1,0:T(8,128)(2,1)}) %reduce-scatter.23.cloned.1.call-update) | async-done | bytes 1966096 | tf_op jit(solution)/shard_map/reduce_scatter | solution.py:401
  1655.3 249.5 %reduce-scatter.19.cloned.1.call-done = bf16[10,192,512]{2,1,0:T(8,128)(2,1)} async-done(((bf16[10,1536,512]{2,1,0:T(8,128)(2,1)}), bf16[10,192,512]{2,1,0:T(8,128)(2,1)}) %reduce-scatter.19.cloned.1.call-update) | async-done | bytes 1966096 | tf_op jit(solution)/shard_map/reduce_scatter | solution.py:401
  1908.8 249.8 %reduce-scatter.21.cloned.1.call-done = bf16[10,192,512]{2,1,0:T(8,128)(2,1)} async-done(((bf16[10,1536,512]{2,1,0:T(8,128)(2,1)}), bf16[10,192,512]{2,1,0:T(8,128)(2,1)}) %reduce-scatter.21.cloned.1.call-update) | async-done | bytes 1966096 | tf_op jit(solution)/shard_map/reduce_scatter | solution.py:401
  2162.6 100.7 %reduce-scatter.15.cloned.1.call-done = f32[48,512]{1,0:T(8,128)} async-done(((f32[1536,512]{1,0:T(8,128)}), f32[48,512]{1,0:T(8,128)}) %reduce-scatter.15.cloned.1.call-update) | async-done | bytes 98320 | tf_op jit(solution)/shard_map/reduce_scatter | solution.py:396
  2263.3 106.5 %reduce-scatter.13.cloned.1.call-done = f32[48,512]{1,0:T(8,128)} async-done(((f32[1536,512]{1,0:T(8,128)}), f32[48,512]{1,0:T(8,128)}) %reduce-scatter.13.cloned.1.call-update) | async-done | bytes 98320 | tf_op jit(solution)/shard_map/reduce_scatter | solution.py:396
  2369.8 140.7 %reduce-scatter.17.cloned.1.call-done = f32[48,1536]{1,0:T(8,128)} async-done(((f32[1536,1536]{1,0:T(8,128)}), f32[48,1536]{1,0:T(8,128)}) %reduce-scatter.17.cloned.1.call-update) | async-done | bytes 294928 | tf_op jit(solution)/shard_map/reduce_scatter | solution.py:396
  2510.5 141.9 %reduce-scatter.11.cloned.1.call-done = f32[48,1536]{1,0:T(8,128)} async-done(((f32[1536,1536]{1,0:T(8,128)}), f32[48,1536]{1,0:T(8,128)}) %reduce-scatter.11.cloned.1.call-update) | async-done | bytes 294928 | tf_op jit(solution)/shard_map/reduce_scatter | solution.py:396
  (488 shorter events, 237.0 us)
Async XLA Ops:
  7.2 61.6 %all-gather.9.cloned.1.call-start = ((), (), s32[]{:S(2)}) async-start(), calls=%async_computation.16 | async-start | bytes 1622016 | tf_op jit(solution)/shard_map/all_gather | solution.py:367
  8.0 117.8 %all-gather.11.cloned.1.call-start = ((), (), s32[]{:S(2)}) async-start(), calls=%async_computation.17 | async-start | bytes 1622016 | tf_op jit(solution)/shard_map/all_gather | solution.py:366
  8.7 182.6 %all-gather.13.cloned.1.call-start = ((), (), s32[]{:S(2)}) async-start(), calls=%async_computation.18 | async-start | bytes 4866048 | tf_op jit(solution)/shard_map/all_gather | solution.py:365
  9.4 247.3 %all-gather.15.cloned.1.call-start = ((), (), s32[]{:S(2)}) async-start(), calls=%async_computation.19 | async-start | bytes 4866048 | tf_op jit(solution)/shard_map/all_gather | solution.py:368
  10.0 464.6 %all-gather.19.cloned.1.call-start = ((), (), s32[]{:S(2)}) async-start(), calls=%async_computation.21 | async-start | bytes 17694720 | tf_op jit(solution)/shard_map/all_gather | solution.py:374
  10.6 55.6 %copy-start = (bf16[2,128,1536]{2,1,0:T(8,128)(2,1)S(1)}, bf16[2,128,1536]{2,1,0:T(8,128)(2,1)}, u32[]{:S(2)}) copy-start(bf16[2,128,1536]{2,1,0:T(8,128)(2,1)} %param.14) | copy-start | bytes 2359300
  10.6 679.1 %all-gather.17.cloned.1.call-start = ((), (), s32[]{:S(2)}) async-start(), calls=%async_computation.20 | async-start | bytes 17694720 | tf_op jit(solution)/shard_map/all_gather | solution.py:373
  11.2 893.8 %all-gather.21.cloned.1.call-start = ((), (), s32[]{:S(2)}) async-start(), calls=%async_computation.22 | async-start | bytes 17694720 | tf_op jit(solution)/shard_map/all_gather | solution.py:375
  53.9 944.4 %copy-start.51 = (f32[1536]{0:T(1024)}, f32[1536]{0:T(1024)S(1)}, u32[]{:S(2)}) copy-start(f32[1536]{0:T(1024)S(1)} %convert_element_type.368) | copy-start | bytes 18436
  53.9 1010.7 %copy-start.88 = (f32[1536]{0:T(1024)}, f32[1536]{0:T(1024)S(1)}, u32[]{:S(2)}) copy-start(f32[1536]{0:T(1024)S(1)} %convert_element_type.380) | copy-start | bytes 18436
  67.0 131.0 %copy-start.102 = (f32[128]{0:T(128)}, f32[128]{0:T(128)S(1)}, u32[]{:S(2)}) copy-start(f32[128]{0:T(128)S(1)} %get-tuple-element.113) | copy-start | bytes 1540
  67.0 931.2 %copy-start.105 = (f32[128]{0:T(128)}, f32[128]{0:T(128)S(1)}, u32[]{:S(2)}) copy-start(f32[128]{0:T(128)S(1)} %get-tuple-element.86) | copy-start | bytes 1540
  67.9 133.9 %copy-start.77 = (f32[128,32]{0,1:T(8,128)}, f32[128,32]{0,1:T(8,128)S(1)}, u32[]{:S(2)}) copy-start(f32[128,32]{0,1:T(8,128)S(1)} %get-tuple-element.75) | copy-start | bytes 49156
  67.9 934.2 %copy-start.74 = (f32[128,32]{0,1:T(8,128)}, f32[128,32]{0,1:T(8,128)S(1)}, u32[]{:S(2)}) copy-start(f32[128,32]{0,1:T(8,128)S(1)} %get-tuple-element.88) | copy-start | bytes 49156
  70.8 133.1 %copy-start.57 = (bf16[128,512]{0,1:T(8,128)(2,1)}, bf16[128,512]{0,1:T(8,128)(2,1)S(1)}, u32[]{:S(2)}) copy-start(bf16[128,512]{0,1:T(8,128)(2,1)S(1)} %copy.183) | copy-start | bytes 393220
  127.5 70.5 %copy-start.50 = (bf16[512,1536]{1,0:T(8,128)(2,1)}, bf16[512,1536]{1,0:T(8,128)(2,1)S(1)}, u32[]{:S(2)}) copy-start(bf16[512,1536]{1,0:T(8,128)(2,1)S(1)} %copy.184) | copy-start | bytes 4718596
  128.2 73.8 %copy-start.80 = (bf16[128,8,32]{0,2,1:T(8,128)(2,1)}, bf16[128,8,32]{0,2,1:T(8,128)(2,1)S(1)}, u32[]{:S(2)}) copy-start(bf16[128,8,32]{0,2,1:T(8,128)(2,1)S(1)} %get-tuple-element.62) | copy-start | bytes 196612
  128.2 73.8 %copy-start.82 = (bf16[128,8,32]{0,2,1:T(8,128)(2,1)}, bf16[128,8,32]{0,2,1:T(8,128)(2,1)S(1)}, u32[]{:S(2)}) copy-start(bf16[128,8,32]{0,2,1:T(8,128)(2,1)S(1)} %get-tuple-element.63) | copy-start | bytes 196612
  202.4 57.5 %copy-start.90 = (f32[8,3,128]{2,1,0:T(4,128)}, f32[8,3,128]{2,1,0:T(4,128)S(1)}, u32[]{:S(2)}) copy-start(f32[8,3,128]{2,1,0:T(4,128)S(1)} %get-tuple-element.94) | copy-start | bytes 36868
  203.5 56.4 %copy-start.91 = (f32[8,3,128]{2,1,0:T(4,128)}, f32[8,3,128]{2,1,0:T(4,128)S(1)}, u32[]{:S(2)}) copy-start(f32[8,3,128]{2,1,0:T(4,128)S(1)} %fusion.106) | copy-start | bytes 36868
  205.0 56.0 %copy-start.26 = (bf16[8,64,3,128]{3,1,2,0:T(8,128)(2,1)}, bf16[8,64,3,128]{3,1,2,0:T(8,128)(2,1)S(1)}, u32[]{:S(2)}) copy-start(bf16[8,64,3,128]{3,1,2,0:T(8,128)(2,1)S(1)} %convolution_convert_fusion.3) | copy-start | bytes 1179652
  261.0 81.5 %copy-start.24 = (bf16[128,1536]{1,0:T(8,128)(2,1)}, bf16[128,1536]{1,0:T(8,128)(2,1)S(1)}, u32[]{:S(2)}) copy-start(bf16[128,1536]{1,0:T(8,128)(2,1)S(1)} %multiply_convert_fusion.1) | copy-start | bytes 1179652
  269.8 71.6 %copy-start.35 = (bf16[2,128,1536]{2,1,0:T(8,128)(2,1)S(1)}, bf16[2,128,1536]{2,1,0:T(8,128)(2,1)}, u32[]{:S(2)}) copy-start(bf16[2,128,1536]{2,1,0:T(8,128)(2,1)} %param.15) | copy-start | bytes 2359300
  269.9 82.1 %all-to-all-start = ((bf16[4,400,1536]{2,1,0:T(8,128)(2,1)}), bf16[4,400,1536]{2,1,0:T(8,128)(2,1)}, u32[]{:S(2)}, u32[]{:S(2)}) async-start(bf16[4,400,1536]{2,1,0:T(8,128)(2,1)} %bitcast.573), calls=%async_computation | async-start | bytes 9830400 | tf_op jit(solution)/shard_map/all_to_all | solution.py:158
  352.0 349.6 %all-to-all-start.4 = ((bf16[4,400,1536]{2,1,0:T(8,128)(2,1)}), bf16[4,400,1536]{2,1,0:T(8,128)(2,1)}, u32[]{:S(2)}, u32[]{:S(2)}) async-start(bf16[4,400,1536]{2,1,0:T(8,128)(2,1)} %bitcast.570), calls=%async_computation.4 | async-start | bytes 9830400 | tf_op jit(solution)/shard_map/all_to_all | solution.py:194
  917.8 21.0 copy-start.42
  929.8 61.6 %all-to-all-start.1 = ((bf16[4,400,1536]{2,1,0:T(8,128)(2,1)}), bf16[4,400,1536]{2,1,0:T(8,128)(2,1)}, u32[]{:S(2)}, u32[]{:S(2)}) async-start(bf16[4,400,1536]{2,1,0:T(8,128)(2,1)} %bitcast.574), calls=%async_computation.1 | async-start | bytes 9830400 | tf_op jit(solution)/shard_map/all_to_all | solution.py:173
  936.7 146.1 %copy-start.108 = (s32[1024,1]{0,1:T(1,128)}, s32[1024,1]{0,1:T(1,128)S(1)}, u32[]{:S(2)}) copy-start(s32[1024,1]{0,1:T(1,128)S(1)} %compare_select_fusion) | copy-start | bytes 12292
  991.4 61.3 %all-to-all-start.5 = ((bf16[4,400,1536]{2,1,0:T(8,128)(2,1)}), bf16[4,400,1536]{2,1,0:T(8,128)(2,1)}, u32[]{:S(2)}, u32[]{:S(2)}) async-start(bf16[4,400,1536]{2,1,0:T(8,128)(2,1)} %bitcast.572), calls=%async_computation.5 | async-start | bytes 9830400 | tf_op jit(solution)/shard_map/all_to_all | solution.py:225
  1075.1 61.1 %all-to-all-start.2 = ((bf16[4,400,1536]{2,1,0:T(8,128)(2,1)}), bf16[4,400,1536]{2,1,0:T(8,128)(2,1)}, u32[]{:S(2)}, u32[]{:S(2)}) async-start(bf16[4,400,1536]{2,1,0:T(8,128)(2,1)} %bitcast.575), calls=%async_computation.2 | async-start | bytes 9830400 | tf_op jit(solution)/shard_map/all_to_all | solution.py:158
  1081.4 54.9 %copy-start.73 = (f32[128,40]{0,1:T(8,128)}, f32[128,40]{0,1:T(8,128)S(1)}, u32[]{:S(2)}) copy-start(f32[128,40]{0,1:T(8,128)S(1)} %get-tuple-element.106) | copy-start | bytes 61444
  1082.7 53.5 %copy-start.72 = (f32[128,8]{1,0:T(8,128)}, f32[128,8]{1,0:T(8,128)S(1)}, u32[]{:S(2)}) copy-start(f32[128,8]{1,0:T(8,128)S(1)} %copy.199) | copy-start | bytes 12292
  1136.3 61.4 %all-to-all-start.6 = ((bf16[4,400,1536]{2,1,0:T(8,128)(2,1)}), bf16[4,400,1536]{2,1,0:T(8,128)(2,1)}, u32[]{:S(2)}, u32[]{:S(2)}) async-start(bf16[4,400,1536]{2,1,0:T(8,128)(2,1)} %bitcast.571), calls=%async_computation.6 | async-start | bytes 9830400 | tf_op jit(solution)/shard_map/all_to_all | solution.py:194
  1222.0 61.1 %all-to-all-start.3 = ((bf16[4,400,1536]{2,1,0:T(8,128)(2,1)}), bf16[4,400,1536]{2,1,0:T(8,128)(2,1)}, u32[]{:S(2)}, u32[]{:S(2)}) async-start(bf16[4,400,1536]{2,1,0:T(8,128)(2,1)} %bitcast.576), calls=%async_computation.3 | async-start | bytes 9830400 | tf_op jit(solution)/shard_map/all_to_all | solution.py:173
  1228.0 383.6 %reduce-scatter.25.cloned.1.call-start = ((), (), s32[]{:S(2)}) async-start(), calls=%async_computation.30 | async-start | bytes 811008
  1228.0 15.0 copy-start.25
  1228.0 15.0 copy-start.99
  1303.4 347.9 %reduce-scatter.23.cloned.1.call-start = ((), (), s32[]{:S(2)}) async-start(), calls=%async_computation.29 | async-start | bytes 17694720 | tf_op jit(solution)/shard_map/reduce_scatter | solution.py:401
  1323.4 16.9 copy-start.46
  1323.4 581.3 %reduce-scatter.19.cloned.1.call-start = ((), (), s32[]{:S(2)}) async-start(), calls=%async_computation.27 | async-start | bytes 17694720 | tf_op jit(solution)/shard_map/reduce_scatter | solution.py:401
  1361.0 797.6 %reduce-scatter.21.cloned.1.call-start = ((), (), s32[]{:S(2)}) async-start(), calls=%async_computation.28 | async-start | bytes 17694720 | tf_op jit(solution)/shard_map/reduce_scatter | solution.py:401
  1431.1 61.2 %all-to-all-start.7 = ((bf16[4,400,1536]{2,1,0:T(8,128)(2,1)}), bf16[4,400,1536]{2,1,0:T(8,128)(2,1)}, u32[]{:S(2)}, u32[]{:S(2)}) async-start(bf16[4,400,1536]{2,1,0:T(8,128)(2,1)} %bitcast.577), calls=%async_computation.7 | async-start | bytes 9830400 | tf_op jit(solution)/shard_map/all_to_all | solution.py:225
  1437.2 826.1 %reduce-scatter.15.cloned.1.call-start = ((), (), s32[]{:S(2)}) async-start(), calls=%async_computation.25 | async-start | bytes 3244032 | tf_op jit(solution)/shard_map/reduce_scatter | solution.py:396
  1522.1 847.7 %reduce-scatter.13.cloned.1.call-start = ((), (), s32[]{:S(2)}) async-start(), calls=%async_computation.24 | async-start | bytes 3244032 | tf_op jit(solution)/shard_map/reduce_scatter | solution.py:396
  1531.7 978.7 %reduce-scatter.17.cloned.1.call-start = ((), (), s32[]{:S(2)}) async-start(), calls=%async_computation.26 | async-start | bytes 9732096 | tf_op jit(solution)/shard_map/reduce_scatter | solution.py:396
  1539.4 1112.9 %reduce-scatter.11.cloned.1.call-start = ((), (), s32[]{:S(2)}) async-start(), calls=%async_computation.23 | async-start | bytes 9732096 | tf_op jit(solution)/shard_map/reduce_scatter | solution.py:396
  1558.2 48.5 %copy-start.49 = (bf16[1,128,1536]{2,1,0:T(8,128)(2,1)S(1)}, bf16[1,128,1536]{2,1,0:T(8,128)(2,1)}, u32[]{:S(2)}) copy-start(bf16[1,128,1536]{2,1,0:T(8,128)(2,1)} %get-tuple-element.54) | copy-start | bytes 1179652
  1558.9 49.8 %copy-start.14 = (f32[128,1536]{1,0:T(8,128)S(1)}, f32[128,1536]{1,0:T(8,128)}, u32[]{:S(2)}) copy-start(f32[128,1536]{1,0:T(8,128)} %copy-done.12) | copy-start | bytes 2359300
  (108 other events, 371.8 us)
Sparse Core Ops, SparseCore 0:
  11.0 57.7 all-gather.8
  71.8 53.9 all-gather.10
  128.8 62.5 all-gather.12
  194.2 62.4 all-gather.14
  258.8 215.7 all-gather.18
  476.6 213.0 all-gather.16
  691.9 212.9 all-gather.20
  1303.5 91.3 reduce-scatter.24
  1398.5 252.7 reduce-scatter.22
  1654.7 250.0 reduce-scatter.18
  1908.4 250.1 reduce-scatter.20
  2164.4 98.7 reduce-scatter.14
  2269.3 100.4 reduce-scatter.12
  2376.1 134.3 reduce-scatter.16
  2517.8 134.5 reduce-scatter.10
where the time goes:
time: 2670 us; the launch traced here: 2660 us
  waiting for transfers between devices  1930 us (72%)
  matrix products  318 us (12%)
  blocking collectives  148 us (6%)
  local copies, waits for them, and re-layouts  105 us (4%)
  other arithmetic  88.1 us (3%)
  starting transfers between devices  55.5 us (2%)
    reduce_scatter x3, waiting for transfers between devices, body(): lax.psum_scatter(for_sending(tuple(expert_sums)), 'shard', scatter_dimens...  538 us
    reduce_scatter x4, waiting for transfers between devices, body(): lax.psum_scatter(tuple(attn_sums), ('expert', 'shard'), scatter_dimension...  490 us
    all_gather x1, waiting for transfers between devices, body(): lax.all_gather(w_gate, 'shard', axis=1, tiled=True)  203 us
    all_gather x1, waiting for transfers between devices, body(): lax.all_gather(w_down, 'shard', axis=1, tiled=True)  203 us
    all_gather x1, waiting for transfers between devices, body(): lax.all_gather(w_up, 'shard', axis=1, tiled=True)  98.1 us
    all_to_all x2, waiting for transfers between devices, micro_step(): lax.all_to_all(grad_in.reshape(groups, local_count * CAP, MODEL_WIDTH), '...  85.8 us
    unnamed x2, blocking collectives  81.9 us
    all_gather x1, blocking collectives, body(): lax.all_gather(w_router, ('expert', 'shard'), axis=0, tiled=True)  65.8 us
  transfers between devices with their start and end apart: 23, of which 20 were waited for; matrix products, arithmetic and copies ran while one was open for 15% of the time, Pallas kernels for 0%

commit v1 on v0

v1 whole, which is shorter than its diff:
```python
import math

import jax
import jax.numpy as jnp
from jax import lax
from jax.sharding import Mesh, PartitionSpec as P

MODEL_WIDTH = 1536
QUERY_HEADS = 24
KEY_VALUE_HEADS = 8
HEAD_SIZE = 64
E = 40
TOPK = 8
SLICES = 4
LANES = 128

ALL = ("y", "c", "z", "x")
epsilon = 1e-05
F32 = jnp.float32
BF16 = jnp.bfloat16


def ring_step(array, axis):
    size = lax.axis_size(axis)
    return lax.ppermute(array, axis, [(i, (i + 1) % size) for i in range(size)])


def ring_gather(block, axis):
    blocks = [block]
    for _ in range(lax.axis_size(axis) - 1):
        blocks.append(ring_step(blocks[-1], axis))
    return blocks


def ring_sum(parts, axis, kind):
    total = parts[1]
    for part in parts[2:] + parts[:1]:
        total = (ring_step(total, axis).astype(F32) + part.astype(F32)).astype(kind)
    return total


def gather_group(block):
    chunks = []
    for own in ring_gather(block, "z"):
        rows = jnp.stack(ring_gather(own, "y"))
        chunks.append(jnp.concatenate(ring_gather(rows, "c")))
    return chunks


def sum_chunk(chunk, kind):
    halves = chunk.reshape((2, lax.axis_size("y")) + chunk.shape[1:])
    rows = ring_sum([halves[0], halves[1]], "c", kind)
    return ring_sum([rows[i] for i in range(rows.shape[0])], "y", kind)


def placed_gather(block, axis, position):
    size, index = lax.axis_size(axis), lax.axis_index(axis)
    whole = jnp.zeros(block.shape[:position] + (size,) + block.shape[position:], block.dtype)
    for step, part in enumerate(ring_gather(block, axis)):
        whole = lax.dynamic_update_index_in_dim(whole, part, (index - step) % size, position)
    return whole


def positions(lengths, count_of_tokens):
    seq_ends = jnp.cumsum(lengths, axis=-1)
    starts = seq_ends - lengths
    token_index = jnp.arange(count_of_tokens, dtype=jnp.int32)
    segment = jnp.sum((token_index[:, None] >= seq_ends[..., None, :]).astype(jnp.int32), axis=-1)
    choose = segment[..., None] == jnp.arange(lengths.shape[-1], dtype=jnp.int32)
    offset = jnp.sum(jnp.where(choose, starts[..., None, :], 0), axis=-1)
    return (segment, token_index - offset)


def rotary_embedding(values_in, token_position, direction):
    half_size = values_in.shape[-1] // 2
    frequency = jnp.exp(jnp.arange(half_size, dtype=F32) * (-math.log(10000.0) / half_size))
    angles = token_position.astype(F32)[..., None] * frequency
    cosine = jnp.cos(angles)[..., None, :]
    sine_part = jnp.sin(angles)[..., None, :]
    first_half = values_in[..., :half_size]
    second_half = values_in[..., half_size:]
    return jnp.concatenate(
        [
            first_half * cosine - direction * second_half * sine_part,
            second_half * cosine + direction * first_half * sine_part,
        ],
        axis=-1,
    )


def norm_back(grad_normed, values_in, inverse_root, gain):
    scaled = grad_normed * gain
    grad_gain = jnp.sum(grad_normed * values_in * inverse_root, axis=0)
    cubed = inverse_root * inverse_root * inverse_root
    grad_values = inverse_root * scaled - values_in * cubed * jnp.mean(
        scaled * values_in, axis=-1, keepdims=True
    )
    return (grad_values, grad_gain)


def dot(left, right, dims=((1,), (0,))):
    return lax.dot_general(left, right, (dims, ((), ())), preferred_element_type=F32)


def expert_chunk(rows_and_gates, grad_rows, w_in, w_back, local_count):
    count = rows_and_gates.shape[0]
    rows = rows_and_gates[:, :MODEL_WIDTH]
    high = rows_and_gates[:, MODEL_WIDTH : MODEL_WIDTH + E].astype(F32)
    low = rows_and_gates[:, MODEL_WIDTH + E : MODEL_WIDTH + 2 * E].astype(F32)
    group = lax.axis_index("y") * lax.axis_size("c") + lax.axis_index("c")
    gates = lax.dynamic_slice_in_dim(high + low, group * local_count, local_count, axis=1)
    gates = gates[..., None]
    hidden = dot(rows, w_in).reshape(count, local_count, 2, -1)
    gate_part, up_part = hidden[:, :, 0], hidden[:, :, 1]
    grad_plain = dot(grad_rows, w_back, ((1,), (1,))).reshape(gate_part.shape)
    sigmoid_gate = jax.nn.sigmoid(gate_part)
    active = gate_part * sigmoid_gate * up_part
    grad_gates = jnp.sum(active * grad_plain, axis=-1)
    weighted = (gates * active).astype(BF16).reshape(count, -1)
    grad_active = gates * grad_plain
    grad_gate = grad_active * up_part * sigmoid_gate * (1.0 + gate_part * (1.0 - sigmoid_gate))
    grad_up = grad_active * gate_part * sigmoid_gate
    grad_hidden = jnp.stack([grad_gate, grad_up], axis=2).astype(BF16).reshape(count, -1)
    result = dot(weighted, w_back).astype(BF16)
    grad_in = dot(grad_hidden, w_in, ((1,), (1,))).astype(BF16)
    return result, grad_in, grad_gates, weighted, grad_hidden


def body(
    inputs,
    cotangent,
    lengths,
    routes,
    norm_gain_one,
    w_query,
    key_projection_weight,
    value_projection_weight,
    w_out,
    norm_gain_two,
    w_router,
    w_gate,
    w_up,
    w_down,
):
    micro, block, _ = inputs.shape
    count = micro * block
    local_count = w_gate.shape[0]
    y_size, z_size, x_size = lax.axis_size("y"), lax.axis_size("z"), lax.axis_size("x")
    group = lax.axis_index("y") * lax.axis_size("c") + lax.axis_index("c")
    query_per_group = QUERY_HEADS // KEY_VALUE_HEADS
    kv_width = KEY_VALUE_HEADS * HEAD_SIZE
    score_scale = 1.0 / math.sqrt(HEAD_SIZE)

    small = jnp.concatenate([w_router, norm_gain_one[:, None], norm_gain_two[:, None]], axis=1)
    small = jnp.pad(small, ((0, 0), (0, LANES - small.shape[1])))
    mine = jnp.concatenate(
        [w_query, key_projection_weight, value_projection_weight, small], axis=1
    )
    whole = lax.all_gather(mine, ALL, axis=0, tiled=True)
    w_qkv = whole[:, : MODEL_WIDTH + 2 * kv_width]
    small = whole[:, MODEL_WIDTH + 2 * kv_width :]
    w_router = small[:, :E]
    gain_first = small[:, E].astype(F32)
    gain_second = small[:, E + 1].astype(F32)
    w_out = lax.all_gather(w_out, ALL, axis=0, tiled=True)

    w_in = jnp.stack([w_gate, w_up])
    own_rows = w_in.shape[2]
    w_in = w_in.reshape(2, local_count, own_rows, z_size, -1)
    hidden_slice = w_in.shape[-1]
    w_in = w_in.transpose(3, 2, 1, 0, 4).reshape(z_size, own_rows, -1)
    w_in = lax.all_to_all(w_in, "z", 0, 0, tiled=True)
    w_in = placed_gather(w_in, "x", 1).reshape(MODEL_WIDTH, -1)
    w_back = placed_gather(w_down, "x", 1).reshape(-1, MODEL_WIDTH)

    act_rows = inputs.reshape(count, MODEL_WIDTH).astype(F32)
    grad_final_low = cotangent.reshape(count, MODEL_WIDTH)
    grad_final = grad_final_low.astype(F32)
    grad_chunks = gather_group(grad_final_low)
    r_one = lax.rsqrt(jnp.mean(act_rows * act_rows, axis=-1, keepdims=True) + epsilon)
    normalized_input = (act_rows * r_one * gain_first).astype(BF16)
    qkv = dot(normalized_input, w_qkv)
    segment, token_position = positions(lengths[:, 0], block)
    query_pre = qkv[:, :MODEL_WIDTH].reshape(micro, block, QUERY_HEADS, HEAD_SIZE)
    key_pre = qkv[:, MODEL_WIDTH : MODEL_WIDTH + kv_width]
    key_pre = key_pre.reshape(micro, block, KEY_VALUE_HEADS, HEAD_SIZE)
    values = qkv[:, MODEL_WIDTH + kv_width :].astype(BF16)
    values = values.reshape(micro, block, KEY_VALUE_HEADS, HEAD_SIZE)
    query = rotary_embedding(query_pre, token_position, 1.0).astype(BF16)
    query = query.reshape(micro, block, KEY_VALUE_HEADS, query_per_group, HEAD_SIZE)
    keys = rotary_embedding(key_pre, token_position, 1.0).astype(BF16)
    token_index = jnp.arange(block, dtype=jnp.int32)
    allowed = (segment[:, :, None] == segment[:, None, :]) & (
        token_index[:, None] >= token_index[None, :]
    )
    scores = jnp.einsum("bqkgd,bskd->bkgqs", query, keys, preferred_element_type=F32)
    scores = jnp.where(allowed[:, None, None], scores * score_scale, -1000000000.0)
    probs = jax.nn.softmax(scores, axis=-1)
    probs_low = probs.astype(BF16)
    mixed = jnp.einsum("bkgqs,bskd->bqkgd", probs_low, values, preferred_element_type=F32)
    mixed = mixed.reshape(count, MODEL_WIDTH).astype(BF16)
    resid = act_rows + dot(mixed, w_out)

    r_two = lax.rsqrt(jnp.mean(resid * resid, axis=-1, keepdims=True) + epsilon)
    normed_two = (resid * r_two * gain_second).astype(BF16)
    chance = jax.nn.softmax(dot(normed_two, w_router), axis=-1)
    choice = routes.reshape(count, TOPK)
    chosen = jnp.any(choice[..., None] == jnp.arange(E, dtype=jnp.int32), axis=1).astype(F32)
    picked = chance * chosen
    picked_total = jnp.sum(picked, axis=-1, keepdims=True)
    gates = picked / picked_total

    high = lax.reduce_precision(gates, 8, 7)
    low = gates - high
    spare = jnp.zeros((count, LANES - 2 * E), BF16)
    sent = jnp.concatenate([normed_two, high.astype(BF16), low.astype(BF16), spare], axis=1)
    sent_chunks = gather_group(sent)
    results, grads_in, grads_gates, weighted, grad_hidden = [], [], [], [], []
    for sent_chunk, grad_chunk in zip(sent_chunks, grad_chunks):
        parts = expert_chunk(
            sent_chunk.reshape(-1, sent_chunk.shape[-1]),
            grad_chunk.reshape(-1, MODEL_WIDTH),
            w_in,
            w_back,
            local_count,
        )
        shape = (-1, count, MODEL_WIDTH)
        results.append(sum_chunk(parts[0].reshape(shape), BF16))
        grads_in.append(sum_chunk(parts[1].reshape(shape), BF16))
        spread = jnp.zeros((parts[2].shape[0], E), F32)
        spread = lax.dynamic_update_slice(spread, parts[2], (0, group * local_count))
        grads_gates.append(sum_chunk(spread.reshape(-1, count, E), F32))
        weighted.append(parts[3])
        grad_hidden.append(parts[4])
    outputs = resid + ring_sum(results, "z", F32)
    grad_experts = ring_sum(grads_in, "z", F32)
    grad_gates = ring_sum(grads_gates, "z", F32)

    all_rows = jnp.concatenate(sent_chunks).reshape(-1, sent.shape[1])[:, :MODEL_WIDTH]
    all_grads = jnp.concatenate(grad_chunks).reshape(-1, MODEL_WIDTH)
    grad_w_in = dot(all_rows, jnp.concatenate(grad_hidden), ((0,), (0,))).astype(BF16)
    grad_w_back = dot(jnp.concatenate(weighted), all_grads, ((0,), (0,))).astype(BF16)
    x_index = lax.axis_index("x")

    def sum_x(parts, position, kind):
        ordered = [
            lax.dynamic_index_in_dim(parts, (x_index - step) % x_size, position, keepdims=False)
            for step in range(x_size)
        ]
        return ring_sum(ordered, "x", kind)

    grad_w_in = sum_x(grad_w_in.reshape(z_size, x_size, own_rows, -1), 1, BF16)
    grad_w_in = lax.all_to_all(grad_w_in, "z", 0, 0, tiled=True)
    grad_w_in = grad_w_in.reshape(z_size, own_rows, local_count, 2, hidden_slice)
    grad_w_in = grad_w_in.transpose(3, 2, 1, 0, 4).reshape(2, local_count, own_rows, -1)
    grad_w_in = grad_w_in.astype(F32)
    grad_w_down = sum_x(grad_w_back.reshape(local_count, x_size, -1, MODEL_WIDTH), 1, F32)

    grad_picked = grad_gates * chosen
    grad_picked = grad_picked - chosen * jnp.sum(grad_gates * gates, axis=-1, keepdims=True)
    grad_chance = grad_picked / picked_total
    grad_logits = (
        chance * (grad_chance - jnp.sum(chance * grad_chance, axis=-1, keepdims=True))
    ).astype(BF16)
    grad_w_router = dot(normed_two, grad_logits, ((0,), (0,)))
    grad_normed_two = grad_experts + dot(grad_logits, w_router, ((1,), (1,)))
    grad_resid, grad_gain_two = norm_back(grad_normed_two, resid, r_two, gain_second)
    grad_resid = grad_final + grad_resid

    grad_att = grad_resid.astype(BF16)
    grad_w_out = dot(mixed, grad_att, ((0,), (0,))).astype(BF16)
    grad_w_out = lax.psum_scatter(grad_w_out, ALL, scatter_dimension=0, tiled=True)
    grad_mixed = dot(grad_att, w_out, ((1,), (1,))).astype(BF16).reshape(query.shape)
    grad_probs = jnp.einsum("bqkgd,bskd->bkgqs", grad_mixed, values, preferred_element_type=F32)
    grad_value_pre = jnp.einsum(
        "bkgqs,bqkgd->bskd", probs_low, grad_mixed, preferred_element_type=F32
    )
    grad_value_pre = grad_value_pre.reshape(count, kv_width).astype(BF16)
    grad_scores = (
        probs * (grad_probs - jnp.sum(probs * grad_probs, axis=-1, keepdims=True))
    ).astype(BF16)
    grad_query = jnp.einsum("bkgqs,bskd->bqkgd", grad_scores, keys, preferred_element_type=F32)
    grad_keys = jnp.einsum("bkgqs,bqkgd->bskd", grad_scores, query, preferred_element_type=F32)
    grad_query_pre = rotary_embedding(
        (grad_query * score_scale).reshape(query_pre.shape), token_position, -1.0
    )
    grad_key_pre = rotary_embedding(grad_keys * score_scale, token_position, -1.0)
    grad_qkv = jnp.concatenate(
        [
            grad_query_pre.reshape(count, MODEL_WIDTH).astype(BF16),
            grad_key_pre.reshape(count, kv_width).astype(BF16),
            grad_value_pre,
        ],
        axis=1,
    )
    grad_w_qkv = dot(normalized_input, grad_qkv, ((0,), (0,))).astype(BF16)
    grad_normed = dot(grad_qkv, w_qkv, ((1,), (1,)))
    grad_rows, grad_gain_one = norm_back(grad_normed, act_rows, r_one, gain_first)
    grad_rows = grad_resid + grad_rows

    grad_small = jnp.concatenate(
        [grad_w_router, grad_gain_one[:, None], grad_gain_two[:, None]], axis=1
    )
    grad_small = jnp.pad(grad_small, ((0, 0), (0, LANES - grad_small.shape[1])))
    grad_mine = jnp.concatenate([grad_w_qkv, grad_small.astype(BF16)], axis=1)
    grad_mine = lax.psum_scatter(grad_mine, ALL, scatter_dimension=0, tiled=True).astype(F32)
    grad_small = grad_mine[:, MODEL_WIDTH + 2 * kv_width :]
    return (
        outputs.astype(BF16).reshape(inputs.shape),
        grad_rows.reshape(inputs.shape),
        grad_small[:, E],
        grad_mine[:, :MODEL_WIDTH],
        grad_mine[:, MODEL_WIDTH : MODEL_WIDTH + kv_width],
        grad_mine[:, MODEL_WIDTH + kv_width : MODEL_WIDTH + 2 * kv_width],
        grad_w_out.astype(F32),
        grad_small[:, E + 1],
        grad_small[:, :E],
        grad_w_in[0],
        grad_w_in[1],
        grad_w_down,
    )


def solution(mesh):
    experts, shards = mesh.shape["expert"], mesh.shape["shard"]
    split = Mesh(
        mesh.devices.reshape(experts // 2, 2, SLICES, shards // SLICES), ("y", "c", "z", "x")
    )
    groups, within = ("y", "c"), ("z", "x")
    tokens = P(None, ALL, None)
    rows = P(ALL, None)
    expert = P(groups, within, None)
    return jax.shard_map(
        body,
        mesh=split,
        in_specs=(tokens,) * 4
        + (P(ALL), rows, rows, rows, rows, P(ALL), rows, expert, expert, expert),
        out_specs=(tokens, tokens, P(ALL), rows, rows, rows, rows, P(ALL), rows)
        + (expert, expert, expert),
        check_vma=False,
    )
```

time: 2670 us -> 1270 us (0.48)
  waiting for transfers between devices: 1930 us -> 486 us
  local copies, waits for them, and re-layouts: 105 us -> 262 us
  blocking collectives: 148 us -> 0 us
  matrix products: 318 us -> 272 us
  other arithmetic: 88.1 us -> 131 us
  starting transfers between devices: 55.5 us -> 92.3 us
    reduce_scatter x7 -> x2, waiting for transfers between devices: 1030 us -> 83.3 us  [the longest x1 83.3 us: body(): lax.psum_scatter(grad_mine, ALL, scatter_dimension=0, tiled=True)]
    all_gather x7 -> x2, waiting for transfers between devices: 676 us -> 0.02 us  [the longest x1 0.02 us: body(): w_out = lax.all_gather(w_out, ALL, axis=0, tiled=True)]
    ppermute x0 -> x59, waiting for transfers between devices: none -> 380 us  [ring_step(): return lax.ppermute(array, axis, [(i, (i + 1) % size) for i in range(size)])]
    all_to_all x8 -> x2, waiting for transfers between devices: 221 us -> 22.9 us  [the longest x1 22.9 us: body(): grad_w_in = lax.all_to_all(grad_w_in, 'z', 0, 0, tiled=True)]
    unnamed x2 -> x0, blocking collectives: 81.9 us -> none
    ppermute x0 -> x59, starting transfers between devices: none -> 81.7 us  [ring_step(): return lax.ppermute(array, axis, [(i, (i + 1) % size) for i in range(size)])]
    all_gather x1 -> x0, blocking collectives: 65.8 us -> none  [body(): lax.all_gather(w_router, ('expert', 'shard'), axis=0, tiled=True)]
    slice x4 -> x32, local copies, waits for them, and re-layouts: 0.43 us -> 62.7 us  [the longest x4 31.4 us: expert_chunk(): gate_part, up_part = (hidden[:, :, 0], hidden[:, :, 1])]
  transfers between devices with their start and end apart: 23 -> 65, of which waited for: 20 -> 23; matrix products, arithmetic and copies ran while one was open for 15% -> 51% of each run, Pallas kernels for 0% -> 0%
where the time goes in v1:
time: 1270 us; the launch traced here: 1260 us
  waiting for transfers between devices  486 us (38%)
  matrix products  272 us (21%)
  local copies, waits for them, and re-layouts  262 us (21%)
  other arithmetic  131 us (10%)
  starting transfers between devices  92.3 us (7%)
  between operations  16.5 us (1%)
    ppermute x59, waiting for transfers between devices, ring_step(): return lax.ppermute(array, axis, [(i, (i + 1) % size) for i in range(size)])  380 us
    dot_general x27, matrix products, dot(): lax.dot_general(left, right, (dims, ((), ())), preferred_element_type=F32)  263 us
    reduce_scatter x1, waiting for transfers between devices, body(): lax.psum_scatter(grad_mine, ALL, scatter_dimension=0, tiled=True)  83.3 us
    ppermute x59, starting transfers between devices, ring_step(): return lax.ppermute(array, axis, [(i, (i + 1) % size) for i in range(size)])  81.7 us
    unnamed x312, local copies, waits for them, and re-layouts  42.6 us
    dot_general x3, local copies, waits for them, and re-layouts, dot(): lax.dot_general(left, right, (dims, ((), ())), preferred_element_type=F32)  36.7 us
    slice x4, local copies, waits for them, and re-layouts, expert_chunk(): gate_part, up_part = (hidden[:, :, 0], hidden[:, :, 1])  31.4 us
  transfers between devices with their start and end apart: 65, of which 23 were waited for; matrix products, arithmetic and copies ran while one was open for 51% of the time, Pallas kernels for 0%

profile of v1, /device:TPU:1, one launch (start us, length us, event | category | flops | bytes accessed | tf_op | source)
XLA Modules:
  0.0 1260.0 jit_solution(16510237388817773280)
XLA Ops:
  30.3 13.3 %maximum_bitcast_fusion = bf16[4,192,10,2,128]{4,3,2,1,0:T(2,128)(2,1)} fusion(bf16[1,10,192,4,128]{4,0,1,2,3:T(2,128)(2,1)} %copy.204, bf16[1,10,192,4,128]{4,0,1,2,3:T(2,128)(2,1)} %copy.203), kind=kLoop, calls=%fused_computation.138 | loop fusion | flops 7864320 | bytes 7864320 | tf_op jit(solution)/shard_map/transpose | solution.py:171
  43.6 9.7 reshape.480
  78.8 84.7 %collective-permute-done.30 = bf16[256,1536]{1,0:T(8,128)(2,1)S(1)} collective-permute-done((bf16[256,1536]{1,0:T(8,128)(2,1)S(1)}, bf16[256,1536]{1,0:T(8,128)(2,1)S(1)}, u32[]{:S(2)}, u32[]{:S(2)}) %collective-permute-start.30) | collective-permute-done | bytes 786464 | tf_op jit(solution)/shard_map/ppermute | solution.py:25
  167.6 21.5 %collective-permute-start.36 = (bf16[256,1536]{1,0:T(8,128)(2,1)S(1)}, bf16[256,1536]{1,0:T(8,128)(2,1)S(1)}, u32[]{:S(2)}, u32[]{:S(2)}) collective-permute-start(bf16[256,1536]{1,0:T(8,128)(2,1)S(1)} %collective-permute-done.30), channel_id=1, source_target_pairs={{0,2},{2,4},{4,6},{6,0},{1,3},{3,5},{5,7},{7,1},{8,10},{10,12},{12... | collective-permute-start | bytes 2359304 | tf_op jit(solution)/shard_map/ppermute | solution.py:25
  191.5 20.8 %collective-permute-done.36 = bf16[256,1536]{1,0:T(8,128)(2,1)S(1)} collective-permute-done((bf16[256,1536]{1,0:T(8,128)(2,1)S(1)}, bf16[256,1536]{1,0:T(8,128)(2,1)S(1)}, u32[]{:S(2)}, u32[]{:S(2)}) %collective-permute-start.36) | collective-permute-done | bytes 786464 | tf_op jit(solution)/shard_map/ppermute | solution.py:25
  219.8 19.3 %collective-permute-done.37 = bf16[256,1536]{1,0:T(8,128)(2,1)S(1)} collective-permute-done((bf16[256,1536]{1,0:T(8,128)(2,1)S(1)}, bf16[256,1536]{1,0:T(8,128)(2,1)S(1)}, u32[]{:S(2)}, u32[]{:S(2)}) %collective-permute-start.37) | collective-permute-done | bytes 786464 | tf_op jit(solution)/shard_map/ppermute | solution.py:25
  258.9 5.7 fusion.33
  305.9 9.0 collective-permute-done.20
  319.6 23.0 %collective-permute-done.3 = bf16[4,192,2560]{2,1,0:T(8,128)(2,1)} collective-permute-done((bf16[4,192,2560]{2,1,0:T(8,128)(2,1)}, bf16[4,192,2560]{2,1,0:T(8,128)(2,1)}, u32[]{:S(2)}, u32[]{:S(2)}) %collective-permute-start.3) | collective-permute-done | bytes 3932192 | tf_op jit(solution)/shard_map/ppermute | solution.py:25
  346.8 16.6 %dot_general.111 = bf16[10,2,128,1536]{2,1,0,3:T(2,128)(2,1)} reshape(bf16[2560,1536]{0,1:T(8,128)(2,1)} %bitcast.27) | data formatting | bytes 15728640 | tf_op jit(solution)/shard_map/dot_general | solution.py:102
  363.4 19.9 %copy.253 = bf16[10,2,128,1536]{3,2,0,1:T(8,128)(2,1)} copy(bf16[10,2,128,1536]{2,1,0,3:T(2,128)(2,1)} %dot_general.111) | data formatting | bytes 15728640 | tf_op jit(solution)/shard_map/dot_general | solution.py:102
  390.1 13.1 %collective-permute-done.1 = bf16[256,1664]{1,0:T(8,128)(2,1)S(1)} collective-permute-done((bf16[256,1664]{1,0:T(8,128)(2,1)}, bf16[256,1664]{1,0:T(8,128)(2,1)S(1)}, u32[]{:S(2)}, u32[]{:S(2)}) %collective-permute-start.1) | collective-permute-done | bytes 852000 | tf_op jit(solution)/shard_map/ppermute | solution.py:25
  409.1 12.4 collective-permute-done.9
  430.3 11.8 fusion.93
  442.1 7.3 multiply_reduce_fusion
  454.9 7.4 convolution_convert_fusion.6
  468.9 12.6 %convolution_convert_fusion.2 = bf16[1024,1536]{1,0:T(8,128)(2,1)S(1)} fusion(bf16[1024,2560]{0,1:T(8,128)(2,1)S(1)} %bitcast.761, bf16[1536,2560]{1,0:T(8,128)(2,1)} %bitcast.26), kind=kOutput, calls=%fused_computation.143 | convolution fusion | flops 8054636544 | bytes 16252928 | tf_op jit(solution)/shard_map/dot_general | solution.py:102
  494.2 11.2 fusion.26
  505.8 14.6 %multiply_reduce_fusion.3 = (f32[1024,10]{0,1:T(8,128)S(1)}, bf16[1024,10,128]{0,2,1:T(8,128)(2,1)}, f32[1024,10,128]{0,2,1:T(8,128)}) fusion(f32[1024,10,2,128]{0,3,2,1:T(8,128)} %fusion.26, f32[1024,10]{0,1:T(8,128)S(1)} %copy.202, bf16[1024,1536,1]{1,0,2:T(8,128)(2,1)} %bitcast.793, bf16[10,128,1536]{2,1,0:T(8,128)(2,1)} %bitcast.778), kind=kOutput, calls=%fused_computation.132 | convolution fusion | flops 4038318080 | bytes 25509888 | tf_op jit(solution)/shard_map/dot_general | solution.py:102
  526.0 7.4 convolution_convert_fusion.9
  539.3 12.6 convolution_convert_fusion.5
  574.1 11.2 fusion.95
  585.7 14.6 %multiply_reduce_fusion.2 = (f32[1024,10]{0,1:T(8,128)S(1)}, bf16[1024,10,128]{0,2,1:T(8,128)(2,1)}, f32[1024,10,128]{0,2,1:T(8,128)}) fusion(f32[1024,10,2,128]{0,3,1,2:T(8,128)} %fusion.95, f32[1024,10]{0,1:T(8,128)S(1)} %copy.211, bf16[1024,1536,1]{1,0,2:T(8,128)(2,1)} %bitcast.792, bf16[10,128,1536]{2,1,0:T(8,128)(2,1)} %bitcast.780), kind=kOutput, calls=%fused_computation.131 | convolution fusion | flops 4038318080 | bytes 25509888 | tf_op jit(solution)/shard_map/dot_general | solution.py:102
  604.3 7.3 convolution_convert_fusion.8
  617.6 12.8 %convolution_convert_fusion.4 = bf16[1024,1536]{1,0:T(8,128)(2,1)S(1)} fusion(bf16[1024,2560]{0,1:T(8,128)(2,1)S(1)} %bitcast.765, bf16[1536,2560]{1,0:T(8,128)(2,1)} %bitcast.26), kind=kOutput, calls=%fused_computation.145 | convolution fusion | flops 8054636544 | bytes 16252928 | tf_op jit(solution)/shard_map/dot_general | solution.py:102
  653.0 11.2 fusion.94
  666.4 12.3 multiply_reduce_fusion.1
  685.0 6.9 fusion.75
  693.2 13.7 %convolution_convert_fusion.3 = bf16[1024,1536]{1,0:T(8,128)(2,1)} fusion(bf16[1024,2560]{0,1:T(8,128)(2,1)S(1)} %bitcast.767, bf16[1536,2560]{1,0:T(8,128)(2,1)} %bitcast.26), kind=kOutput, calls=%fused_computation.144 | convolution fusion | flops 8054636544 | bytes 16252928 | tf_op jit(solution)/shard_map/dot_general | solution.py:102
  709.7 41.5 %fusion.11 = bf16[1536,2560]{1,0:T(8,128)(2,1)} fusion(bf16[1024,2560]{0,1:T(8,128)(2,1)} %bitcast.768, bf16[1024,2560]{0,1:T(8,128)(2,1)} %bitcast.766, bf16[1024,2560]{0,1:T(8,128)(2,1)} %bitcast.764, bf16[1024,2560]{0,1:T(8,128)(2,1)} %bitcast.762, bf16[4096,1664]{1,0:T(8,128)(2,1)} %bitcast.814), kind=kOutput, calls=%fused_computation.12 | convolution fusion | flops 32300072960 | bytes 41418752 | tf_op jit(solution)/shard_map/dot_general | solution.py:102
  768.3 11.0 collective-permute-done.7
  786.3 9.8 collective-permute-done.29
  804.8 12.3 collective-permute-done.40
  818.0 50.1 %collective-permute-done.35 = f32[256,1536]{1,0:T(8,128)S(1)} collective-permute-done((f32[256,1536]{1,0:T(8,128)S(1)}, f32[256,1536]{1,0:T(8,128)S(1)}, u32[]{:S(2)}, u32[]{:S(2)}) %collective-permute-start.35) | collective-permute-done | bytes 1572896 | tf_op jit(solution)/shard_map/ppermute | solution.py:25
  876.1 10.1 collective-permute-done.45
  886.3 18.5 %collective-permute-done.41 = f32[256,1536]{1,0:T(8,128)S(1)} collective-permute-done((f32[256,1536]{1,0:T(8,128)S(1)}, f32[256,1536]{1,0:T(8,128)S(1)}, u32[]{:S(2)}, u32[]{:S(2)}) %collective-permute-start.41) | collective-permute-done | bytes 1572896 | tf_op jit(solution)/shard_map/ppermute | solution.py:25
  906.7 31.8 %collective-permute-done.19 = f32[256,1536]{1,0:T(8,128)S(1)} collective-permute-done((f32[256,1536]{1,0:T(8,128)S(1)}, f32[256,1536]{1,0:T(8,128)S(1)}, u32[]{:S(2)}, u32[]{:S(2)}) %collective-permute-start.19) | collective-permute-done | bytes 1572896 | tf_op jit(solution)/shard_map/ppermute | solution.py:25
  971.9 10.7 fusion.176
  987.8 11.8 fusion.60
  999.6 10.4 fusion.178
  1015.2 11.6 fusion.50
  1037.2 22.3 %fusion.28 = bf16[1280,1536]{1,0:T(8,128)(2,1)S(1)} fusion(bf16[4096,1536]{1,0:T(8,128)(2,1)} %bitcast.815, bf16[1024,1280]{0,1:T(8,128)(2,1)} %get-tuple-element.167, bf16[1024,1280]{0,1:T(8,128)(2,1)} %get-tuple-element.168, bf16[1024,1280]{0,1:T(8,128)(2,1)} %get-tuple-element.170, bf16[1024,1280]{0,1:T(8,128)(2,1)S(1)} %copy-done.55), kind=kOutput, calls=%fused_computation.32 | convolution fusion | flops 16150036480 | bytes 27000832 | tf_op jit(solution)/shard_map/dot_general | solution.py:102
  1061.0 41.0 %collective-permute-done.58 = bf16[10,64,1536]{2,1,0:T(8,128)(2,1)S(1)} collective-permute-done((bf16[10,64,1536]{2,1,0:T(8,128)(2,1)S(1)}, bf16[10,64,1536]{2,1,0:T(8,128)(2,1)S(1)}, u32[]{:S(2)}, u32[]{:S(2)}) %collective-permute-start.58) | collective-permute-done | bytes 1966112 | tf_op jit(solution)/shard_map/ppermute | solution.py:25
  1106.1 22.9 %all-to-all-done.1 = bf16[4,192,2560]{2,1,0:T(8,128)(2,1)} async-done(((bf16[4,192,2560]{2,1,0:T(8,128)(2,1)}), bf16[4,192,2560]{2,1,0:T(8,128)(2,1)}, u32[]{:S(2)}, u32[]{:S(2)}) %all-to-all-start.1) | async-done | bytes 3932192 | tf_op jit(solution)/shard_map/all_to_all | solution.py:253
  1129.1 9.7 reshape.520
  1138.8 8.6 copy.317
  1151.4 5.4 squeeze.224
  1163.8 83.3 %reduce-scatter.3.cloned.1.call-done = bf16[48,2688]{1,0:T(8,128)(2,1)} async-done(((bf16[1536,2688]{1,0:T(8,128)(2,1)}), bf16[48,2688]{1,0:T(8,128)(2,1)}) %reduce-scatter.3.cloned.1.call-update) | async-done | bytes 258064 | tf_op jit(solution)/shard_map/reduce_scatter | solution.py:306
  (649 shorter events, 376.7 us)
Async XLA Ops:
  7.2 249.7 %all-gather.3.cloned.1.call-start = ((), (), s32[]{:S(2)}) async-start(), calls=%async_computation.4 | async-start | bytes 8515584 | tf_op jit(solution)/shard_map/all_gather | solution.py:159
  9.8 56.5 %collective-permute-start.24 = (bf16[256,1536]{1,0:T(8,128)(2,1)}, bf16[256,1536]{1,0:T(8,128)(2,1)S(1)}, u32[]{:S(2)}, u32[]{:S(2)}) collective-permute-start(bf16[256,1536]{1,0:T(8,128)(2,1)} %bitcast.704), channel_id=1, source_target_pairs={{0,2},{2,4},{4,6},{6,0},{1,3},{3,5},{5,7},{7,1},{8,10},{10,12},{12... | collective-permute-start | bytes 2359304 | tf_op jit(solution)/shard_map/ppermute | solution.py:25
  12.0 62.9 %collective-permute-start.42 = (bf16[256,1536]{1,0:T(8,128)(2,1)}, bf16[256,1536]{1,0:T(8,128)(2,1)S(1)}, u32[]{:S(2)}, u32[]{:S(2)}) collective-permute-start(bf16[256,1536]{1,0:T(8,128)(2,1)} %bitcast.705), channel_id=1, source_target_pairs={{0,16},{16,0},{1,17},{17,1},{2,18},{18,2},{3,19},{19,3},{4,20},{20... | collective-permute-start | bytes 2359304 | tf_op jit(solution)/shard_map/ppermute | solution.py:25
  53.4 202.3 %all-to-all-start = ((bf16[4,192,2560]{2,1,0:T(8,128)(2,1)}), bf16[4,192,2560]{2,1,0:T(8,128)(2,1)}, u32[]{:S(2)}, u32[]{:S(2)}) async-start(bf16[4,192,2560]{2,1,0:T(8,128)(2,1)} %reshape.480), calls=%async_computation | async-start | bytes 7864320 | tf_op jit(solution)/shard_map/all_to_all | solution.py:172
  58.3 227.5 %all-gather.5.cloned.1.call-start = ((), (), s32[]{:S(2)}) async-start(), calls=%async_computation.5 | async-start | bytes 4866048 | tf_op jit(solution)/shard_map/all_gather | solution.py:165
  58.4 130.7 %collective-permute-start.4 = (bf16[10,64,1536]{2,1,0:T(8,128)(2,1)}, bf16[10,64,1536]{2,1,0:T(8,128)(2,1)}, u32[]{:S(2)}, u32[]{:S(2)}) collective-permute-start(bf16[10,64,1536]{2,1,0:T(8,128)(2,1)} %param.27), channel_id=1, source_target_pairs={{0,1},{1,0},{2,3},{3,2},{4,5},{5,4},{6,7},{7,6},{8,9},{9,8},{10,11... | collective-permute-start | bytes 5898248 | tf_op jit(solution)/shard_map/ppermute | solution.py:25
  59.7 1102.5 %reduce-scatter.5.cloned.1.call-start = ((), (), s32[]{:S(2)}) async-start(), calls=%async_computation.7 | async-start | bytes 4866048 | tf_op jit(solution)/shard_map/reduce_scatter | solution.py:272
  66.3 97.3 %collective-permute-start.30 = (bf16[256,1536]{1,0:T(8,128)(2,1)S(1)}, bf16[256,1536]{1,0:T(8,128)(2,1)S(1)}, u32[]{:S(2)}, u32[]{:S(2)}) collective-permute-start(bf16[256,1536]{1,0:T(8,128)(2,1)S(1)} %collective-permute-done.24), channel_id=1, source_target_pairs={{0,2},{2,4},{4,6},{6,0},{1,3},{3,5},{5,7},{7,1},{8,10},{10,12},{12... | collective-permute-start | bytes 2359304 | tf_op jit(solution)/shard_map/ppermute | solution.py:25
  67.6 96.2 %collective-permute-start.25 = (bf16[256,1536]{1,0:T(8,128)(2,1)S(1)}, bf16[256,1536]{1,0:T(8,128)(2,1)}, u32[]{:S(2)}, u32[]{:S(2)}) collective-permute-start(bf16[256,1536]{1,0:T(8,128)(2,1)S(1)} %collective-permute-done.24), channel_id=1, source_target_pairs={{0,16},{16,0},{1,17},{17,1},{2,18},{18,2},{3,19},{19,3},{4,20},{20... | collective-permute-start | bytes 2359304 | tf_op jit(solution)/shard_map/ppermute | solution.py:25
  75.0 138.5 %collective-permute-start.43 = (bf16[2,256,1536]{2,1,0:T(8,128)(2,1)S(1)}, bf16[2,256,1536]{2,1,0:T(8,128)(2,1)S(1)}, u32[]{:S(2)}, u32[]{:S(2)}) collective-permute-start(bf16[2,256,1536]{2,1,0:T(8,128)(2,1)S(1)} %pad_maximum_fusion.15), channel_id=1, source_target_pairs={{0,8},{8,0},{1,9},{9,1},{2,10},{10,2},{3,11},{11,3},{4,12},{12,4},... | collective-permute-start | bytes 4718600 | tf_op jit(solution)/shard_map/ppermute | solution.py:25
  165.0 75.9 %collective-permute-start.26 = (bf16[2,256,1536]{2,1,0:T(8,128)(2,1)S(1)}, bf16[2,256,1536]{2,1,0:T(8,128)(2,1)S(1)}, u32[]{:S(2)}, u32[]{:S(2)}) collective-permute-start(bf16[2,256,1536]{2,1,0:T(8,128)(2,1)S(1)} %pad_maximum_fusion.12), channel_id=1, source_target_pairs={{0,8},{8,0},{1,9},{9,1},{2,10},{10,2},{3,11},{11,3},{4,12},{12,4},... | collective-permute-start | bytes 4718600 | tf_op jit(solution)/shard_map/ppermute | solution.py:25
  167.6 44.8 %collective-permute-start.36 = (bf16[256,1536]{1,0:T(8,128)(2,1)S(1)}, bf16[256,1536]{1,0:T(8,128)(2,1)S(1)}, u32[]{:S(2)}, u32[]{:S(2)}) collective-permute-start(bf16[256,1536]{1,0:T(8,128)(2,1)S(1)} %collective-permute-done.30), channel_id=1, source_target_pairs={{0,2},{2,4},{4,6},{6,0},{1,3},{3,5},{5,7},{7,1},{8,10},{10,12},{12... | collective-permute-start | bytes 2359304 | tf_op jit(solution)/shard_map/ppermute | solution.py:25
  191.1 56.2 %collective-permute-start.32 = (bf16[2,256,1536]{2,1,0:T(8,128)(2,1)S(1)}, bf16[2,256,1536]{2,1,0:T(8,128)(2,1)S(1)}, u32[]{:S(2)}, u32[]{:S(2)}) collective-permute-start(bf16[2,256,1536]{2,1,0:T(8,128)(2,1)S(1)} %pad_maximum_fusion.13), channel_id=1, source_target_pairs={{0,8},{8,0},{1,9},{9,1},{2,10},{10,2},{3,11},{11,3},{4,12},{12,4},... | collective-permute-start | bytes 4718600 | tf_op jit(solution)/shard_map/ppermute | solution.py:25
  255.7 86.9 %collective-permute-start.3 = (bf16[4,192,2560]{2,1,0:T(8,128)(2,1)}, bf16[4,192,2560]{2,1,0:T(8,128)(2,1)}, u32[]{:S(2)}, u32[]{:S(2)}) collective-permute-start(bf16[4,192,2560]{2,1,0:T(8,128)(2,1)} %all-to-all-done), channel_id=1, source_target_pairs={{0,1},{1,0},{2,3},{3,2},{4,5},{5,4},{6,7},{7,6},{8,9},{9,8},{10,11... | collective-permute-start | bytes 11796488 | tf_op jit(solution)/shard_map/ppermute | solution.py:25
  316.4 109.6 %collective-permute-start.21 = (bf16[2,256,1664]{2,1,0:T(8,128)(2,1)}, bf16[2,256,1664]{2,1,0:T(8,128)(2,1)}, u32[]{:S(2)}, u32[]{:S(2)}) collective-permute-start(bf16[2,256,1664]{2,1,0:T(8,128)(2,1)} %pad_maximum_fusion.11), channel_id=1, source_target_pairs={{0,8},{8,0},{1,9},{9,1},{2,10},{10,2},{3,11},{11,3},{4,12},{12,4},... | collective-permute-start | bytes 5111816 | tf_op jit(solution)/shard_map/ppermute | solution.py:25
  318.5 66.1 %collective-permute-start.8 = (bf16[256,1664]{1,0:T(8,128)(2,1)}, bf16[256,1664]{1,0:T(8,128)(2,1)S(1)}, u32[]{:S(2)}, u32[]{:S(2)}) collective-permute-start(bf16[256,1664]{1,0:T(8,128)(2,1)} %collective-permute-done), channel_id=1, source_target_pairs={{0,2},{2,4},{4,6},{6,0},{1,3},{3,5},{5,7},{7,1},{8,10},{10,12},{12... | collective-permute-start | bytes 2555912 | tf_op jit(solution)/shard_map/ppermute | solution.py:25
  384.6 36.9 %collective-permute-start.9 = (bf16[256,1664]{1,0:T(8,128)(2,1)S(1)}, bf16[256,1664]{1,0:T(8,128)(2,1)S(1)}, u32[]{:S(2)}, u32[]{:S(2)}) collective-permute-start(bf16[256,1664]{1,0:T(8,128)(2,1)S(1)} %collective-permute-done.8), channel_id=1, source_target_pairs={{0,16},{16,0},{1,17},{17,1},{2,18},{18,2},{3,19},{19,3},{4,20},{20... | collective-permute-start | bytes 2555912 | tf_op jit(solution)/shard_map/ppermute | solution.py:25
  385.8 38.9 %collective-permute-start.14 = (bf16[256,1664]{1,0:T(8,128)(2,1)S(1)}, bf16[256,1664]{1,0:T(8,128)(2,1)S(1)}, u32[]{:S(2)}, u32[]{:S(2)}) collective-permute-start(bf16[256,1664]{1,0:T(8,128)(2,1)S(1)} %collective-permute-done.8), channel_id=1, source_target_pairs={{0,2},{2,4},{4,6},{6,0},{1,3},{3,5},{5,7},{7,1},{8,10},{10,12},{12... | collective-permute-start | bytes 2555912 | tf_op jit(solution)/shard_map/ppermute | solution.py:25
  406.1 86.1 %collective-permute-start.2 = (bf16[2,256,1664]{2,1,0:T(8,128)(2,1)}, bf16[2,256,1664]{2,1,0:T(8,128)(2,1)}, u32[]{:S(2)}, u32[]{:S(2)}) collective-permute-start(bf16[2,256,1664]{2,1,0:T(8,128)(2,1)} %pad_maximum_fusion.8), channel_id=1, source_target_pairs={{0,8},{8,0},{1,9},{9,1},{2,10},{10,2},{3,11},{11,3},{4,12},{12,4},... | collective-permute-start | bytes 5111816 | tf_op jit(solution)/shard_map/ppermute | solution.py:25
  423.0 148.4 %collective-permute-start.10 = (bf16[2,256,1664]{2,1,0:T(8,128)(2,1)}, bf16[2,256,1664]{2,1,0:T(8,128)(2,1)}, u32[]{:S(2)}, u32[]{:S(2)}) collective-permute-start(bf16[2,256,1664]{2,1,0:T(8,128)(2,1)} %pad_maximum_fusion.9), channel_id=1, source_target_pairs={{0,8},{8,0},{1,9},{9,1},{2,10},{10,2},{3,11},{11,3},{4,12},{12,4},... | collective-permute-start | bytes 5111816 | tf_op jit(solution)/shard_map/ppermute | solution.py:25
  424.7 65.7 %collective-permute-start.15 = (bf16[256,1664]{1,0:T(8,128)(2,1)S(1)}, bf16[256,1664]{1,0:T(8,128)(2,1)S(1)}, u32[]{:S(2)}, u32[]{:S(2)}) collective-permute-start(bf16[256,1664]{1,0:T(8,128)(2,1)S(1)} %collective-permute-done.14), channel_id=1, source_target_pairs={{0,16},{16,0},{1,17},{17,1},{2,18},{18,2},{3,19},{19,3},{4,20},{20... | collective-permute-start | bytes 2555912 | tf_op jit(solution)/shard_map/ppermute | solution.py:25
  454.8 34.7 %collective-permute-start.55 = (f32[2,256,40]{2,1,0:T(8,128)S(1)}, f32[2,256,40]{2,1,0:T(8,128)S(1)}, u32[]{:S(2)}, u32[]{:S(2)}) collective-permute-start(f32[2,256,40]{2,1,0:T(8,128)S(1)} %bitcast.810), channel_id=1, source_target_pairs={{0,8},{8,0},{1,9},{9,1},{2,10},{10,2},{3,11},{11,3},{4,12},{12,4},... | collective-permute-start | bytes 245768 | tf_op jit(solution)/shard_map/ppermute | solution.py:25
  464.1 99.5 %collective-permute-start.22 = (bf16[2,256,1536]{2,1,0:T(8,128)(2,1)}, bf16[2,256,1536]{2,1,0:T(8,128)(2,1)}, u32[]{:S(2)}, u32[]{:S(2)}) collective-permute-start(bf16[2,256,1536]{2,1,0:T(8,128)(2,1)} %bitcast.68), channel_id=1, source_target_pairs={{0,8},{8,0},{1,9},{9,1},{2,10},{10,2},{3,11},{11,3},{4,12},{12,4},... | collective-permute-start | bytes 4718600 | tf_op jit(solution)/shard_map/ppermute | solution.py:25
  489.5 77.0 %collective-permute-start.44 = (bf16[2,256,1536]{2,1,0:T(8,128)(2,1)}, bf16[2,256,1536]{2,1,0:T(8,128)(2,1)}, u32[]{:S(2)}, u32[]{:S(2)}) collective-permute-start(bf16[2,256,1536]{2,1,0:T(8,128)(2,1)} %bitcast.115), channel_id=1, source_target_pairs={{0,8},{8,0},{1,9},{9,1},{2,10},{10,2},{3,11},{11,3},{4,12},{12,4},... | collective-permute-start | bytes 4718600 | tf_op jit(solution)/shard_map/ppermute | solution.py:25
  491.7 158.7 %collective-permute-start.16 = (bf16[2,256,1664]{2,1,0:T(8,128)(2,1)}, bf16[2,256,1664]{2,1,0:T(8,128)(2,1)}, u32[]{:S(2)}, u32[]{:S(2)}) collective-permute-start(bf16[2,256,1664]{2,1,0:T(8,128)(2,1)} %pad_maximum_fusion.10), channel_id=1, source_target_pairs={{0,8},{8,0},{1,9},{9,1},{2,10},{10,2},{3,11},{11,3},{4,12},{12,4},... | collective-permute-start | bytes 5111816 | tf_op jit(solution)/shard_map/ppermute | solution.py:25
  525.8 31.8 %collective-permute-start.46 = (f32[2,256,40]{2,1,0:T(8,128)S(1)}, f32[2,256,40]{2,1,0:T(8,128)S(1)}, u32[]{:S(2)}, u32[]{:S(2)}) collective-permute-start(f32[2,256,40]{2,1,0:T(8,128)S(1)} %bitcast.811), channel_id=1, source_target_pairs={{0,8},{8,0},{1,9},{9,1},{2,10},{10,2},{3,11},{11,3},{4,12},{12,4},... | collective-permute-start | bytes 245768 | tf_op jit(solution)/shard_map/ppermute | solution.py:25
  562.3 80.8 %collective-permute-start.5 = (bf16[2,256,1536]{2,1,0:T(8,128)(2,1)}, bf16[2,256,1536]{2,1,0:T(8,128)(2,1)}, u32[]{:S(2)}, u32[]{:S(2)}) collective-permute-start(bf16[2,256,1536]{2,1,0:T(8,128)(2,1)} %bitcast.35), channel_id=1, source_target_pairs={{0,8},{8,0},{1,9},{9,1},{2,10},{10,2},{3,11},{11,3},{4,12},{12,4},... | collective-permute-start | bytes 4718600 | tf_op jit(solution)/shard_map/ppermute | solution.py:25
  563.7 83.8 %collective-permute-start.27 = (bf16[2,256,1536]{2,1,0:T(8,128)(2,1)}, bf16[2,256,1536]{2,1,0:T(8,128)(2,1)}, u32[]{:S(2)}, u32[]{:S(2)}) collective-permute-start(bf16[2,256,1536]{2,1,0:T(8,128)(2,1)} %bitcast.82), channel_id=1, source_target_pairs={{0,8},{8,0},{1,9},{9,1},{2,10},{10,2},{3,11},{11,3},{4,12},{12,4},... | collective-permute-start | bytes 4718600 | tf_op jit(solution)/shard_map/ppermute | solution.py:25
  566.6 72.2 %collective-permute-start.48 = (f32[256,40]{1,0:T(8,128)S(1)}, f32[256,40]{1,0:T(8,128)}, u32[]{:S(2)}, u32[]{:S(2)}) collective-permute-start(f32[256,40]{1,0:T(8,128)S(1)} %fusion.161), channel_id=1, source_target_pairs={{0,2},{2,4},{4,6},{6,0},{1,3},{3,5},{5,7},{7,1},{8,10},{10,12},{12... | collective-permute-start | bytes 122888 | tf_op jit(solution)/shard_map/ppermute | solution.py:25
  604.2 32.0 %collective-permute-start.49 = (f32[2,256,40]{2,1,0:T(8,128)S(1)}, f32[2,256,40]{2,1,0:T(8,128)S(1)}, u32[]{:S(2)}, u32[]{:S(2)}) collective-permute-start(f32[2,256,40]{2,1,0:T(8,128)S(1)} %bitcast.812), channel_id=1, source_target_pairs={{0,8},{8,0},{1,9},{9,1},{2,10},{10,2},{3,11},{11,3},{4,12},{12,4},... | collective-permute-start | bytes 245768 | tf_op jit(solution)/shard_map/ppermute | solution.py:25
  638.8 124.0 %collective-permute-start.11 = (bf16[2,256,1536]{2,1,0:T(8,128)(2,1)}, bf16[2,256,1536]{2,1,0:T(8,128)(2,1)}, u32[]{:S(2)}, u32[]{:S(2)}) collective-permute-start(bf16[2,256,1536]{2,1,0:T(8,128)(2,1)} %bitcast.46), channel_id=1, source_target_pairs={{0,8},{8,0},{1,9},{9,1},{2,10},{10,2},{3,11},{11,3},{4,12},{12,4},... | collective-permute-start | bytes 4718600 | tf_op jit(solution)/shard_map/ppermute | solution.py:25
  641.0 125.0 %collective-permute-start.33 = (bf16[2,256,1536]{2,1,0:T(8,128)(2,1)}, bf16[2,256,1536]{2,1,0:T(8,128)(2,1)}, u32[]{:S(2)}, u32[]{:S(2)}) collective-permute-start(bf16[2,256,1536]{2,1,0:T(8,128)(2,1)} %bitcast.93), channel_id=1, source_target_pairs={{0,8},{8,0},{1,9},{9,1},{2,10},{10,2},{3,11},{11,3},{4,12},{12,4},... | collective-permute-start | bytes 4718600 | tf_op jit(solution)/shard_map/ppermute | solution.py:25
  646.0 111.2 %collective-permute-start.6 = (bf16[256,1536]{1,0:T(8,128)(2,1)}, bf16[256,1536]{1,0:T(8,128)(2,1)}, u32[]{:S(2)}, u32[]{:S(2)}) collective-permute-start(bf16[256,1536]{1,0:T(8,128)(2,1)} %slice_bitcast_fusion.23), channel_id=1, source_target_pairs={{0,16},{16,0},{1,17},{17,1},{2,18},{18,2},{3,19},{19,3},{4,20},{20... | collective-permute-start | bytes 2359304 | tf_op jit(solution)/shard_map/ppermute | solution.py:25
  650.5 110.1 %collective-permute-start.28 = (bf16[256,1536]{1,0:T(8,128)(2,1)}, bf16[256,1536]{1,0:T(8,128)(2,1)}, u32[]{:S(2)}, u32[]{:S(2)}) collective-permute-start(bf16[256,1536]{1,0:T(8,128)(2,1)} %slice_bitcast_fusion.15), channel_id=1, source_target_pairs={{0,16},{16,0},{1,17},{17,1},{2,18},{18,2},{3,19},{19,3},{4,20},{20... | collective-permute-start | bytes 2359304 | tf_op jit(solution)/shard_map/ppermute | solution.py:25
  756.7 44.0 %collective-permute-start.39 = (bf16[2,256,1536]{2,1,0:T(8,128)(2,1)S(1)}, bf16[2,256,1536]{2,1,0:T(8,128)(2,1)S(1)}, u32[]{:S(2)}, u32[]{:S(2)}) collective-permute-start(bf16[2,256,1536]{2,1,0:T(8,128)(2,1)S(1)} %bitcast.797), channel_id=1, source_target_pairs={{0,8},{8,0},{1,9},{9,1},{2,10},{10,2},{3,11},{11,3},{4,12},{12,4},... | collective-permute-start | bytes 4718600 | tf_op jit(solution)/shard_map/ppermute | solution.py:25
  761.9 34.2 %collective-permute-start.29 = (bf16[256,1536]{1,0:T(8,128)(2,1)S(1)}, bf16[256,1536]{1,0:T(8,128)(2,1)S(1)}, u32[]{:S(2)}, u32[]{:S(2)}) collective-permute-start(bf16[256,1536]{1,0:T(8,128)(2,1)S(1)} %fusion.111), channel_id=1, source_target_pairs={{0,2},{2,4},{4,6},{6,0},{1,3},{3,5},{5,7},{7,1},{8,10},{10,12},{12... | collective-permute-start | bytes 2359304 | tf_op jit(solution)/shard_map/ppermute | solution.py:25
  767.8 32.0 %collective-permute-start.34 = (bf16[256,1536]{1,0:T(8,128)(2,1)S(1)}, bf16[256,1536]{1,0:T(8,128)(2,1)S(1)}, u32[]{:S(2)}, u32[]{:S(2)}) collective-permute-start(bf16[256,1536]{1,0:T(8,128)(2,1)S(1)} %slice_bitcast_fusion.13), channel_id=1, source_target_pairs={{0,16},{16,0},{1,17},{17,1},{2,18},{18,2},{3,19},{19,3},{4,20},{20... | collective-permute-start | bytes 2359304 | tf_op jit(solution)/shard_map/ppermute | solution.py:25
  799.8 68.9 %collective-permute-start.13 = (f32[256,1536]{1,0:T(8,128)S(1)}, f32[256,1536]{1,0:T(8,128)S(1)}, u32[]{:S(2)}, u32[]{:S(2)}) collective-permute-start(f32[256,1536]{1,0:T(8,128)S(1)} %convert_add_fusion.21), channel_id=1, source_target_pairs={{0,2},{2,4},{4,6},{6,0},{1,3},{3,5},{5,7},{7,1},{8,10},{10,12},{12... | collective-permute-start | bytes 4718600 | tf_op jit(solution)/shard_map/ppermute | solution.py:25
  800.7 67.4 %collective-permute-start.35 = (f32[256,1536]{1,0:T(8,128)S(1)}, f32[256,1536]{1,0:T(8,128)S(1)}, u32[]{:S(2)}, u32[]{:S(2)}) collective-permute-start(f32[256,1536]{1,0:T(8,128)S(1)} %convert_add_fusion.19), channel_id=1, source_target_pairs={{0,2},{2,4},{4,6},{6,0},{1,3},{3,5},{5,7},{7,1},{8,10},{10,12},{12... | collective-permute-start | bytes 4718600 | tf_op jit(solution)/shard_map/ppermute | solution.py:25
  803.3 69.3 %collective-permute-start.56 = (f32[256,40]{1,0:T(8,128)S(1)}, f32[256,40]{1,0:T(8,128)S(1)}, u32[]{:S(2)}, u32[]{:S(2)}) collective-permute-start(f32[256,40]{1,0:T(8,128)S(1)} %copy-done.91), channel_id=1, source_target_pairs={{0,16},{16,0},{1,17},{17,1},{2,18},{18,2},{3,19},{19,3},{4,20},{20... | collective-permute-start | bytes 122888 | tf_op jit(solution)/shard_map/ppermute | solution.py:25
  803.8 64.8 %collective-permute-start.18 = (bf16[256,1536]{1,0:T(8,128)(2,1)S(1)}, bf16[256,1536]{1,0:T(8,128)(2,1)S(1)}, u32[]{:S(2)}, u32[]{:S(2)}) collective-permute-start(bf16[256,1536]{1,0:T(8,128)(2,1)S(1)} %slice_bitcast_fusion.19), channel_id=1, source_target_pairs={{0,16},{16,0},{1,17},{17,1},{2,18},{18,2},{3,19},{19,3},{4,20},{20... | collective-permute-start | bytes 2359304 | tf_op jit(solution)/shard_map/ppermute | solution.py:25
  817.1 89.5 %collective-permute-start.23 = (bf16[256,1536]{1,0:T(8,128)(2,1)S(1)}, bf16[256,1536]{1,0:T(8,128)(2,1)S(1)}, u32[]{:S(2)}, u32[]{:S(2)}) collective-permute-start(bf16[256,1536]{1,0:T(8,128)(2,1)S(1)} %copy-done.68), channel_id=1, source_target_pairs={{0,16},{16,0},{1,17},{17,1},{2,18},{18,2},{3,19},{19,3},{4,20},{20... | collective-permute-start | bytes 2359304 | tf_op jit(solution)/shard_map/ppermute | solution.py:25
  868.6 36.2 %collective-permute-start.41 = (f32[256,1536]{1,0:T(8,128)S(1)}, f32[256,1536]{1,0:T(8,128)S(1)}, u32[]{:S(2)}, u32[]{:S(2)}) collective-permute-start(f32[256,1536]{1,0:T(8,128)S(1)} %convert_add_fusion.18), channel_id=1, source_target_pairs={{0,2},{2,4},{4,6},{6,0},{1,3},{3,5},{5,7},{7,1},{8,10},{10,12},{12... | collective-permute-start | bytes 4718600 | tf_op jit(solution)/shard_map/ppermute | solution.py:25
  869.0 69.5 %collective-permute-start.19 = (f32[256,1536]{1,0:T(8,128)S(1)}, f32[256,1536]{1,0:T(8,128)S(1)}, u32[]{:S(2)}, u32[]{:S(2)}) collective-permute-start(f32[256,1536]{1,0:T(8,128)S(1)} %convert_add_fusion.20), channel_id=1, source_target_pairs={{0,2},{2,4},{4,6},{6,0},{1,3},{3,5},{5,7},{7,1},{8,10},{10,12},{12... | collective-permute-start | bytes 4718600 | tf_op jit(solution)/shard_map/ppermute | solution.py:25
  873.9 152.8 %collective-permute-start.57 = (bf16[4,192,2560]{2,1,0:T(8,128)(2,1)}, bf16[4,192,2560]{2,1,0:T(8,128)(2,1)}, u32[]{:S(2)}, u32[]{:S(2)}) collective-permute-start(bf16[4,192,2560]{2,1,0:T(8,128)(2,1)} %dynamic-slice_bitcast_fusion), channel_id=1, source_target_pairs={{0,1},{1,0},{2,3},{3,2},{4,5},{5,4},{6,7},{7,6},{8,9},{9,8},{10,11... | collective-permute-start | bytes 11796488 | tf_op jit(solution)/shard_map/ppermute | solution.py:25
  951.8 295.3 %reduce-scatter.3.cloned.1.call-start = ((), (), s32[]{:S(2)}) async-start(), calls=%async_computation.6 | async-start | bytes 8515584 | tf_op jit(solution)/shard_map/reduce_scatter | solution.py:306
  1031.8 97.2 %all-to-all-start.1 = ((bf16[4,192,2560]{2,1,0:T(8,128)(2,1)}), bf16[4,192,2560]{2,1,0:T(8,128)(2,1)}, u32[]{:S(2)}, u32[]{:S(2)}) async-start(bf16[4,192,2560]{2,1,0:T(8,128)(2,1)} %fusion.25), calls=%async_computation.3 | async-start | bytes 7864320 | tf_op jit(solution)/shard_map/all_to_all | solution.py:253
  1059.6 42.4 %collective-permute-start.58 = (bf16[10,64,1536]{2,1,0:T(8,128)(2,1)S(1)}, bf16[10,64,1536]{2,1,0:T(8,128)(2,1)S(1)}, u32[]{:S(2)}, u32[]{:S(2)}) collective-permute-start(bf16[10,64,1536]{2,1,0:T(8,128)(2,1)S(1)} %dynamic-slice_bitcast_fusion.1), channel_id=1, source_target_pairs={{0,1},{1,0},{2,3},{3,2},{4,5},{5,4},{6,7},{7,6},{8,9},{9,8},{10,11... | collective-permute-start | bytes 5898248 | tf_op jit(solution)/shard_map/ppermute | solution.py:25
  (159 other events, 2150.5 us)
Sparse Core Ops, SparseCore 0:
  11.6 108.0 all-gather.2
  122.6 120.9 all-gather.4
  952.0 160.6 reduce-scatter.4
  1119.4 127.6 reduce-scatter.2

commit v2 on v1

v2 whole, which is shorter than its diff:
```python
import functools
import itertools
import math

import jax
import jax.numpy as jnp
from jax import lax
from jax.experimental import pallas as pl
from jax.experimental.pallas import tpu as pltpu
from jax.sharding import Mesh, PartitionSpec as P

MODEL_WIDTH = 1536
QUERY_HEADS = 24
KEY_VALUE_HEADS = 8
HEAD_SIZE = 64
QUERY_PER_GROUP = QUERY_HEADS // KEY_VALUE_HEADS
E = 40
TOPK = 8
SLICES = 4
LANES = 128
VMEM_BYTES = 60 * 1024 * 1024

ALL = ("y", "c", "z", "x")
epsilon = 1e-05
F32 = jnp.float32
BF16 = jnp.bfloat16


def dot(left, right, dims=((1,), (0,))):
    return lax.dot_general(left, right, (dims, ((), ())), preferred_element_type=F32)


def sync(*values):
    return lax.optimization_barrier(values)


def ring_step(array, axis):
    size = lax.axis_size(axis)
    return lax.ppermute(array, axis, [(i, (i + 1) % size) for i in range(size)])


def ring_gather(block, axis):
    blocks = [block]
    for _ in range(lax.axis_size(axis) - 1):
        blocks.append(ring_step(blocks[-1], axis))
    return blocks


def ring_sum(parts, axis, kind):
    total = parts[1]
    for part in list(parts[2:]) + [parts[0]]:
        total = ring_step(total, axis).astype(F32) + part.astype(F32)
        total = total.astype(kind if part is parts[0] else part.dtype)
    return total


def index_at(axis, step):
    return (lax.axis_index(axis) - step) % lax.axis_size(axis)


def move_kernel(moves, count_in, count_out, place_ref, *refs):
    sources, targets = refs[:count_in], refs[count_in : count_in + count_out]
    held, sems = refs[count_in + count_out : -1], refs[-1]
    copies = [[] for _ in targets]
    for number, (source, from_index, target, to_index) in enumerate(moves):
        picked = [
            tuple(place_ref[i[0]] if isinstance(i, tuple) else i for i in index)
            for index in (from_index, to_index)
        ]
        copy = pltpu.make_async_copy(
            sources[source].at[picked[0]], held[target].at[picked[1]], sems.at[number]
        )
        copy.start()
        copies[target].append(copy)
    out = []
    for target, arriving in enumerate(copies):
        for copy in arriving:
            copy.wait()
        out.append(
            pltpu.make_async_copy(held[target], targets[target], sems.at[len(moves) + target])
        )
        out[-1].start()
    for copy in out:
        copy.wait()


def move(moves, places, sources, shapes, name):
    anywhere = pl.BlockSpec(memory_space=pl.ANY)
    total = sum(math.prod(s.shape) * s.dtype.itemsize for s in shapes)
    return pl.pallas_call(
        functools.partial(move_kernel, moves, len(sources), len(shapes)),
        in_specs=[pl.BlockSpec(memory_space=pltpu.SMEM)] + [anywhere] * len(sources),
        out_specs=[anywhere] * len(shapes),
        out_shape=shapes,
        scratch_shapes=[pltpu.VMEM(s.shape, s.dtype) for s in shapes]
        + [pltpu.SemaphoreType.DMA((len(moves) + len(shapes),))],
        compiler_params=pltpu.CompilerParams(vmem_limit_bytes=VMEM_BYTES // 3),
        cost_estimate=pl.CostEstimate(flops=0, bytes_accessed=2 * total, transcendentals=0),
        name=name,
    )(jnp.stack(places).astype(jnp.int32), *sources)


def places_of(axes):
    places, where = [], {}
    for axis in axes:
        for step in range(lax.axis_size(axis)):
            where[axis, step] = (len(places),)
            places.append(index_at(axis, step))
    return places, where


def place_weights(gathers):
    places, where = places_of(("y", "z", "x"))
    sizes = [lax.axis_size(axis) for axis in ("y", "z", "x")]
    moves, sources, shapes = [], [], []
    for number, blocks in enumerate(gathers):
        for (y_step, z_first, x_step), part in blocks.items():
            for i in range(part.shape[0]):
                spot = (where["y", y_step], slice(None), where["z", z_first + i], where["x", x_step])
                moves.append((len(sources), (i,), number, spot))
            sources.append(part)
        shape = (sizes[0], 2) + tuple(sizes[1:]) + sources[-1].shape[2:]
        shapes.append(jax.ShapeDtypeStruct(shape, sources[-1].dtype))
    whole = move(moves, places, sources, shapes, "place_weights")
    return [part.reshape(-1, part.shape[-1]) for part in whole]


def pick_weights(grad, first, second, with_core):
    sizes = {axis: lax.axis_size(axis) for axis in ("y", "z", "x")}
    core = (2,) if with_core else ()
    shape = (sizes["y"],) + core + (sizes["z"], sizes["x"], -1, grad.shape[-1])
    grad = grad.reshape(shape)
    places, where = places_of(("y", "z", "x"))
    moves = []
    for y_step, z_step, x_step in itertools.product(
        range(sizes["y"]), range(sizes["z"]), range(sizes["x"])
    ):
        spot = [where["y", y_step], where["z", z_step], where["x", x_step]]
        if with_core:
            spot.insert(1, slice(None))
        steps = {"y": y_step, "x": x_step}
        moves.append((0, tuple(spot), steps[second], (steps[first], z_step)))
    tail = core + grad.shape[-2:]
    shape = jax.ShapeDtypeStruct((sizes[first], sizes["z"]) + tail, grad.dtype)
    return move(moves, places, [grad], [shape] * sizes[second], "pick_weights")


def sum_along(parts, axis, kind=BF16):
    return ring_sum([parts[i] for i in range(parts.shape[0])], axis, kind)


def pack_kernel(gate_ref, up_ref, out_ref):
    width = out_ref.shape[-1] // 2
    for z in range(out_ref.shape[0]):
        out_ref[z, :, :width] = gate_ref[0, :, z * width : (z + 1) * width]
        out_ref[z, :, width:] = up_ref[0, :, z * width : (z + 1) * width]


def pack_experts(w_gate, w_up, first, last, slices):
    rows, hidden = w_gate.shape[1:]
    spec = pl.BlockSpec((1, rows, hidden), lambda e: (first + e, 0, 0))
    width = 2 * hidden // slices
    return pl.pallas_call(
        pack_kernel,
        grid=(last - first,),
        in_specs=[spec, spec],
        out_specs=pl.BlockSpec((slices, rows, width), lambda e: (0, 0, e)),
        out_shape=jax.ShapeDtypeStruct((slices, rows, (last - first) * width), w_gate.dtype),
        name="pack_experts",
    )(w_gate, w_up)


def unpack_kernel(counts, slices, place_ref, *refs):
    parts, (gate_ref, up_ref) = refs[:-2], refs[-2:]
    expert = pl.program_id(0)
    width = gate_ref.shape[-1] // slices
    first = 0
    for which, count in enumerate(counts):

        @pl.when((expert >= first) & (expert < first + count))
        def _(which=which, first=first):
            start = pl.multiple_of((expert - first) * 2 * width, 2 * width)
            for step in range(slices):
                both = parts[which * slices + step][:, pl.ds(start, 2 * width)].astype(F32)
                spot = pl.multiple_of(place_ref[step] * width, width)
                gate_ref[0, :, pl.ds(spot, width)] = both[:, :width]
                up_ref[0, :, pl.ds(spot, width)] = both[:, width:]

        first = first + count


def unpack_experts(parts, counts):
    places, _ = places_of(("z",))
    slices, local_count = len(parts[0]), sum(counts)
    rows, columns = parts[0][0].shape
    hidden = columns // (2 * counts[0]) * slices
    flat = [part for half in parts for part in half]
    spec = pl.BlockSpec((1, rows, hidden), lambda e: (e, 0, 0))
    whole = [pl.BlockSpec(part.shape, lambda e: (0, 0)) for part in flat]
    shape = jax.ShapeDtypeStruct((local_count, rows, hidden), F32)
    return pl.pallas_call(
        functools.partial(unpack_kernel, counts, slices),
        grid=(local_count,),
        in_specs=[pl.BlockSpec(memory_space=pltpu.SMEM)] + whole,
        out_specs=[spec, spec],
        out_shape=[shape, shape],
        compiler_params=pltpu.CompilerParams(vmem_limit_bytes=VMEM_BYTES),
        name="unpack_experts",
    )(jnp.stack(places).astype(jnp.int32), *flat)


def experts_kernel(counts, steps, x_size, place_ref, *refs):
    parts = len(counts)
    rows_in, grads_in, refs = refs[:steps], refs[steps : 2 * steps], refs[2 * steps :]
    w_in_parts, refs = [refs[i * x_size : (i + 1) * x_size] for i in range(parts)], refs[parts * x_size :]
    w_back_parts, refs = [refs[i * x_size : (i + 1) * x_size] for i in range(parts)], refs[parts * x_size :]
    results, grads, (active_ref, hidden_ref, gates_ref) = refs[:2], refs[2:4], refs[4:7]
    rows_buf, grads_buf = refs[7:9]
    w_in, w_back, sems = refs[9 : 9 + parts], refs[9 + parts], refs[10 + parts]
    step = pl.program_id(0)
    half = steps // 2
    weights, late = [], [[] for _ in range(steps)]
    number = 0

    def copy_of(source, target):
        nonlocal number
        number = number + 1
        return pltpu.make_async_copy(source, target, sems.at[number - 1])

    first = 0
    for part, count in enumerate(counts):
        for x_step in range(x_size):
            place = place_ref[1 + x_step]
            source = w_in_parts[part][x_step]
            size = source.shape[1]
            for z in range(source.shape[0]):
                start = pl.multiple_of((z * x_size + place) * size, size)
                weights.append(copy_of(source.at[z], w_in[part].at[pl.ds(start, size)]))
            source = w_back_parts[part][x_step]
            size = source.shape[1]
            for e in range(count):
                start = pl.multiple_of(((first + e) * x_size + place) * size, size)
                weights.append(copy_of(source.at[e], w_back.at[pl.ds(start, size)]))
        first = first + count
    for i in range(steps):
        late[i] = [copy_of(rows_in[i], rows_buf.at[i]), copy_of(grads_in[i], grads_buf.at[i])]

    @pl.when(step == 0)
    def _():
        for copy in late[0] + weights + [copy for some in late[1:] for copy in some]:
            copy.start()
        for copy in weights:
            copy.wait()

    for i in range(steps):

        @pl.when(step == i)
        def _(i=i):
            for copy in late[i]:
                copy.wait()

    local_count = sum(counts)
    width = w_back.shape[0] // local_count
    rows = rows_buf[step, :, :MODEL_WIDTH]
    grad_rows = grads_buf[step]
    first = place_ref[0] * local_count
    source = lax.broadcasted_iota(jnp.int32, (LANES, LANES), 0)
    wanted = lax.broadcasted_iota(jnp.int32, (LANES, LANES), 1) + first
    choose = ((source == wanted) | (source == wanted + E)).astype(F32).astype(BF16)
    gates = dot(rows_buf[step, :, MODEL_WIDTH:], choose)
    lane = lax.broadcasted_iota(jnp.int32, gates.shape, 1)
    grad_gates = jnp.zeros(gates.shape, F32)
    expert = 0
    for part, count in enumerate(counts):
        for i in range(count):
            here = slice(expert * width, (expert + 1) * width)
            hidden = dot(rows, w_in[part][:, 2 * width * i : 2 * width * (i + 1)])
            grad_plain = dot(grad_rows, w_back[here, :], ((1,), (1,)))
            gate_part, up_part = hidden[:, :width], hidden[:, width:]
            sigmoid_gate = 1.0 / (1.0 + jnp.exp(-gate_part))
            silu = gate_part * sigmoid_gate
            active = silu * up_part
            weight = gates[:, expert : expert + 1]
            total = jnp.sum(active * grad_plain, axis=1, keepdims=True)
            grad_gates = jnp.where(lane == expert, total, grad_gates)
            active_ref[:, here] = (weight * active).astype(BF16)
            grad_active = weight * grad_plain
            start = 2 * width * expert
            hidden_ref[:, start : start + width] = (
                grad_active * up_part * (sigmoid_gate + silu * (1.0 - sigmoid_gate))
            ).astype(BF16)
            hidden_ref[:, start + width : start + 2 * width] = (grad_active * silu).astype(BF16)
            expert = expert + 1
    gates_ref[...] = grad_gates
    result = dot(active_ref[...], w_back[...]).astype(BF16)
    grad_in = jnp.zeros(rows.shape, F32)
    start = 0
    for part, count in enumerate(counts):
        size = 2 * width * count
        grad_in += dot(hidden_ref[:, start : start + size], w_in[part][...], ((1,), (1,)))
        start = start + size
    grad_in = grad_in.astype(BF16)

    for side, now in enumerate((step < half, step >= half)):

        @pl.when(now)
        def _(side=side):
            results[side][0] = result
            grads[side][0] = grad_in


def run_experts(rows, grads, w_in_parts, w_back_parts, counts, group):
    count, wide = rows[0].shape
    steps = len(rows)
    half = steps // 2
    local_count = sum(counts)
    x_size = len(w_in_parts[0])
    z_size, own_rows, columns = w_in_parts[0][0].shape
    width = columns // (2 * counts[0])
    copies = 2 * steps + x_size * (len(counts) * z_size + local_count)
    places, _ = places_of(("x",))
    anywhere = pl.BlockSpec(memory_space=pl.ANY)
    own = pl.BlockSpec((1, count, MODEL_WIDTH), lambda i: (jnp.minimum(i, half - 1), 0, 0))
    other = pl.BlockSpec((1, count, MODEL_WIDTH), lambda i: (jnp.maximum(i - half, 0), 0, 0))

    def by_row(columns):
        return pl.BlockSpec((count, columns), lambda i: (i, 0))

    side = jax.ShapeDtypeStruct((half, count, MODEL_WIDTH), BF16)
    flops = 2 * steps * count * MODEL_WIDTH * 6 * local_count * width
    return pl.pallas_call(
        functools.partial(experts_kernel, counts, steps, x_size),
        grid=(steps,),
        in_specs=[pl.BlockSpec(memory_space=pltpu.SMEM)]
        + [anywhere] * (2 * steps + 2 * len(counts) * x_size),
        out_specs=[own, other, own, other]
        + [by_row(local_count * width), by_row(2 * local_count * width), by_row(LANES)],
        out_shape=[side] * 4
        + [
            jax.ShapeDtypeStruct((steps * count, local_count * width), BF16),
            jax.ShapeDtypeStruct((steps * count, 2 * local_count * width), BF16),
            jax.ShapeDtypeStruct((steps * count, LANES), F32),
        ],
        scratch_shapes=[
            pltpu.VMEM((steps, count, wide), BF16),
            pltpu.VMEM((steps, count, MODEL_WIDTH), BF16),
        ]
        + [pltpu.VMEM((MODEL_WIDTH, part[0].shape[-1]), BF16) for part in w_in_parts]
        + [
            pltpu.VMEM((local_count * width, MODEL_WIDTH), BF16),
            pltpu.SemaphoreType.DMA((copies,)),
        ],
        compiler_params=pltpu.CompilerParams(vmem_limit_bytes=VMEM_BYTES),
        cost_estimate=pl.CostEstimate(
            flops=flops, bytes_accessed=30 * 1024 * 1024, transcendentals=0
        ),
        name="experts",
    )(
        jnp.stack([group] + places).astype(jnp.int32),
        *rows,
        *grads,
        *[part for parts in w_in_parts for part in parts],
        *[part for parts in w_back_parts for part in parts],
    )


def expert_grads_kernel(count_left, count_right, back, place_ref, *refs):
    whole = refs[:count_left]
    columns = refs[count_left : count_left + count_right]
    outs, (buf, total, sems) = refs[count_left + count_right : -3], refs[-3:]
    rows_each = whole[0].shape[0]

    @pl.when(pl.program_id(0) == 0)
    def _():
        copies = [
            pltpu.make_async_copy(
                part.at[:, pl.ds(0, MODEL_WIDTH)],
                buf.at[pl.ds(number * rows_each, rows_each)],
                sems.at[number],
            )
            for number, part in enumerate(whole)
        ]
        for copy in copies:
            copy.start()
        for copy in copies:
            copy.wait()

    size = columns[0].shape[0]
    for i, part in enumerate(columns):
        rows = buf[i * size : (i + 1) * size, :]
        if back:
            term = dot(part[...], rows, ((0,), (0,)))
        else:
            term = dot(rows, part[...], ((0,), (0,)))
        if i == 0:
            total[...] = term
        else:
            total[...] += term
    blocks, own = outs[0].shape[0], outs[0].shape[1]
    for step, out in enumerate(outs):
        for i in range(blocks):
            block = i if back else place_ref[len(outs) + (blocks - i) % blocks]
            start = pl.multiple_of((block * len(outs) + place_ref[step]) * own, own)
            out[i] = total[pl.ds(start, own), :].astype(BF16)


def expert_grads(whole, columns, first, last, width, back):
    x_size = lax.axis_size("x")
    places, _ = places_of(("x",) if back else ("x", "z"))
    tokens = len(whole) * whole[0].shape[0]
    experts = last - first
    anywhere = pl.BlockSpec(memory_space=pl.ANY)
    column = pl.BlockSpec((columns[0].shape[0], width), lambda e: (0, first + e))
    if back:
        own = width // x_size
        block = (1, own, MODEL_WIDTH)
        shape = (experts, own, MODEL_WIDTH)
        out = pl.BlockSpec(block, lambda e: (e, 0, 0))
        total = (width, MODEL_WIDTH)
    else:
        z_size = lax.axis_size("z")
        own = MODEL_WIDTH // (z_size * x_size)
        shape = (z_size, own, experts * width)
        out = pl.BlockSpec((z_size, own, width), lambda e: (0, 0, e))
        total = (MODEL_WIDTH, width)
    return pl.pallas_call(
        functools.partial(expert_grads_kernel, len(whole), len(columns), back),
        grid=(experts,),
        in_specs=[pl.BlockSpec(memory_space=pltpu.SMEM)]
        + [anywhere] * len(whole)
        + [column] * len(columns),
        out_specs=[out] * x_size,
        out_shape=[jax.ShapeDtypeStruct(shape, BF16)] * x_size,
        scratch_shapes=[
            pltpu.VMEM((tokens, MODEL_WIDTH), BF16),
            pltpu.VMEM(total, F32),
            pltpu.SemaphoreType.DMA((len(whole),)),
        ],
        compiler_params=pltpu.CompilerParams(vmem_limit_bytes=VMEM_BYTES),
        cost_estimate=pl.CostEstimate(
            flops=2 * tokens * MODEL_WIDTH * width * experts,
            bytes_accessed=2 * tokens * (MODEL_WIDTH + width * experts),
            transcendentals=0,
        ),
        name="expert_grads",
    )(jnp.stack(places).astype(jnp.int32), *whole, *columns)


def positions(lengths, count_of_tokens):
    seq_ends = jnp.cumsum(lengths, axis=-1)
    starts = seq_ends - lengths
    token_index = jnp.arange(count_of_tokens, dtype=jnp.int32)
    segment = jnp.sum((token_index[:, None] >= seq_ends[..., None, :]).astype(jnp.int32), axis=-1)
    choose = segment[..., None] == jnp.arange(lengths.shape[-1], dtype=jnp.int32)
    offset = jnp.sum(jnp.where(choose, starts[..., None, :], 0), axis=-1)
    return (segment, token_index - offset)


def rotary_embedding(values_in, token_position, direction):
    half_size = values_in.shape[-1] // 2
    frequency = jnp.exp(jnp.arange(half_size, dtype=F32) * (-math.log(10000.0) / half_size))
    angles = token_position.astype(F32)[..., None] * frequency
    cosine = jnp.cos(angles)[..., None, :]
    sine_part = jnp.sin(angles)[..., None, :]
    first_half = values_in[..., :half_size]
    second_half = values_in[..., half_size:]
    return jnp.concatenate(
        [
            first_half * cosine - direction * second_half * sine_part,
            second_half * cosine + direction * first_half * sine_part,
        ],
        axis=-1,
    )


def norm_back(grad_normed, values_in, inverse_root, gain):
    scaled = grad_normed * gain
    grad_gain = jnp.sum(grad_normed * values_in * inverse_root, axis=0)
    cubed = inverse_root * inverse_root * inverse_root
    grad_values = inverse_root * scaled - values_in * cubed * jnp.mean(
        scaled * values_in, axis=-1, keepdims=True
    )
    return (grad_values, grad_gain)


def body(
    inputs,
    cotangent,
    lengths,
    routes,
    norm_gain_one,
    w_query,
    key_projection_weight,
    value_projection_weight,
    w_out,
    norm_gain_two,
    w_router,
    w_gate,
    w_up,
    w_down,
):
    micro, block, _ = inputs.shape
    count = micro * block
    local_count = w_gate.shape[0]
    y_size, z_size, x_size = lax.axis_size("y"), lax.axis_size("z"), lax.axis_size("x")
    core = lax.axis_index("c")
    group = lax.axis_index("y") * 2 + core
    score_scale = 1.0 / math.sqrt(HEAD_SIZE)
    own_rows = w_query.shape[0]
    q_width, kv_width = MODEL_WIDTH // 2, KEY_VALUE_HEADS * HEAD_SIZE // 2
    kv_heads = KEY_VALUE_HEADS // 2

    def columns_of(weight, which):
        split = weight.reshape(own_rows, y_size, 2, -1)
        return lax.dynamic_index_in_dim(split, which, 2, keepdims=False).reshape(own_rows, -1)

    small = jnp.concatenate([w_router, norm_gain_one[:, None], norm_gain_two[:, None]], axis=1)
    small = jnp.pad(small, ((0, 0), (0, LANES - small.shape[1])))

    def both_cores(arrays):
        mine = jnp.concatenate([columns_of(a, core) for a in arrays], axis=1)
        theirs = jnp.concatenate([columns_of(a, 1 - core) for a in arrays], axis=1)
        return mine, theirs

    mine, theirs = both_cores([w_query, key_projection_weight, value_projection_weight])
    got = ring_step(jnp.concatenate([theirs, small], axis=1), "c")
    mine = jnp.concatenate([mine, small], axis=1)
    both = jnp.where(core == 0, jnp.stack([mine, got]), jnp.stack([got, mine]))
    both = jnp.concatenate(
        [
            both[..., : q_width + kv_width],
            both[..., q_width + 2 * kv_width :],
            both[..., q_width + kv_width : q_width + 2 * kv_width],
            jnp.stack([w_out[:, :q_width], w_out[:, q_width:]]),
        ],
        axis=-1,
    )
    counts = [local_count // 2, local_count - local_count // 2]
    ranges = [(0, counts[0]), (counts[0], local_count)]
    packed = [pack_experts(w_gate, w_up, first, last, z_size) for first, last in ranges]
    grad_final_low = cotangent.reshape(count, MODEL_WIDTH)
    grads_z = [grad_final_low]
    down = [w_down[first:last] for first, last in ranges]
    both, grads_ahead, grads_first = sync(
        both, ring_step(grad_final_low, "z"), ring_gather(grad_final_low, "y")
    )
    grads_z.append(grads_ahead)
    grads_y = [grads_first]
    pair = z_size // 2
    first_width = q_width + kv_width + LANES
    first_blocks, second_blocks = {}, {}

    def first_hops(blocks):
        rows = jnp.stack(blocks)
        return ring_gather(rows[..., :first_width], "x"), ring_gather(rows[..., first_width:], "y")

    def second_hops(by_x, by_y, z_first):
        for x_step, one in enumerate(by_x):
            for y_step, two in enumerate(ring_gather(one, "y")):
                first_blocks[y_step, z_first, x_step] = two
        for y_step, one in enumerate(by_y):
            for x_step, two in enumerate(ring_gather(one, "x")):
                second_blocks[y_step, z_first, x_step] = two

    z_blocks = [both]
    for _ in range(pair - 1):
        z_blocks.append(ring_step(z_blocks[-1], "z"))
    others = [ring_step(inputs, "c"), ring_step(lengths, "c")]
    z_blocks, others, packed, grads_second, first_down = sync(
        z_blocks, others, packed, ring_gather(grads_z[1], "y"), ring_gather(down[0], "x")
    )
    other_inputs, other_lengths = others
    grads_y.append(grads_second)
    hops, ahead, grads_ahead, grads_other = sync(
        first_hops(z_blocks),
        ring_step(z_blocks[-1], "z"),
        ring_step(grads_z[1], "z"),
        [[ring_step(part, "c") for part in some] for some in grads_y],
    )
    grads_z.append(grads_ahead)
    second_hops(*hops, 0)
    z_blocks = [ahead]
    for _ in range(pair - 1):
        z_blocks.append(ring_step(z_blocks[-1], "z"))
    first_blocks, second_blocks, z_blocks, packed = sync(
        first_blocks, second_blocks, z_blocks, packed
    )
    swapped = lax.all_to_all(packed[0], "z", 0, 0, tiled=True)
    (hops,) = sync(first_hops(z_blocks))
    second_hops(*hops, pair)
    w_first, w_second = place_weights([first_blocks, second_blocks])
    w_qk = w_first[:, : q_width + kv_width]
    small = w_first[:, q_width + kv_width :]
    w_v = w_second[:, :kv_width]
    w_out = w_second[:, kv_width:].reshape(y_size, 2, -1, q_width).transpose(0, 2, 1, 3)
    w_out = w_out.reshape(q_width, MODEL_WIDTH)
    w_router = small[:, :E]
    gain_first = small[:, E].astype(F32)
    gain_second = small[:, E + 1].astype(F32)

    all_inputs = jnp.stack([inputs, other_inputs])
    all_lengths = jnp.concatenate([lengths[:, 0], other_lengths[:, 0]])
    act_rows = all_inputs.reshape(2 * count, MODEL_WIDTH).astype(F32)
    grad_final = grad_final_low.astype(F32)
    r_one = lax.rsqrt(jnp.mean(act_rows * act_rows, axis=-1) + epsilon)[:, None]
    normalized_input = (act_rows * r_one * gain_first).astype(BF16)
    segment, token_position = positions(all_lengths, block)
    blocks = 2 * micro
    qk_pre = dot(normalized_input, w_qk)
    values = dot(normalized_input, w_v).astype(BF16)
    qk_pre, values, swapped, packed, grads_z, down = sync(
        qk_pre, values, swapped, packed, grads_z, down
    )
    first_parts = ring_gather(swapped, "x")
    swapped = lax.all_to_all(packed[1], "z", 0, 0, tiled=True)
    grads_third = ring_gather(grads_z[2], "y")
    query_pre = qk_pre[:, :q_width]
    query_pre = query_pre.reshape(blocks, block, kv_heads * QUERY_PER_GROUP, HEAD_SIZE)
    key_pre = qk_pre[:, q_width:].reshape(blocks, block, kv_heads, HEAD_SIZE)
    values = values.reshape(blocks, block, kv_heads, HEAD_SIZE)
    query = rotary_embedding(query_pre, token_position, 1.0).astype(BF16)
    query = query.reshape(blocks, block, kv_heads, QUERY_PER_GROUP, HEAD_SIZE)
    keys = rotary_embedding(key_pre, token_position, 1.0).astype(BF16)
    token_index = jnp.arange(block, dtype=jnp.int32)
    allowed = (segment[:, :, None] == segment[:, None, :]) & (
        token_index[:, None] >= token_index[None, :]
    )
    scores = jnp.einsum("bqkgd,bskd->bkgqs", query, keys, preferred_element_type=F32)
    scores = jnp.where(allowed[:, None, None], scores * score_scale, -1000000000.0)
    probs = jax.nn.softmax(scores, axis=-1)
    probs_low = probs.astype(BF16)
    mixed = jnp.einsum("bkgqs,bskd->bqkgd", probs_low, values, preferred_element_type=F32)
    mixed = mixed.reshape(2 * count, q_width).astype(BF16)
    mixed, first_parts, swapped, grads_third = sync(mixed, first_parts, swapped, grads_third)
    grads_y.append(grads_third)
    second_parts = ring_gather(swapped, "x")
    grads_ahead = ring_step(grads_z[2], "z")
    projected = dot(mixed, w_out)
    own_act = act_rows[:count]
    resid = own_act + ring_sum([projected[:count], projected[count:]], "c", F32)

    r_two = lax.rsqrt(jnp.mean(resid * resid, axis=-1) + epsilon)[:, None]
    normed_two = (resid * r_two * gain_second).astype(BF16)
    chance = jax.nn.softmax(dot(normed_two, w_router), axis=-1)
    choice = routes.reshape(count, TOPK)
    chosen = jnp.any(choice[..., None] == jnp.arange(E, dtype=jnp.int32), axis=1).astype(F32)
    picked = chance * chosen
    picked_total = jnp.sum(picked, axis=-1, keepdims=True)
    gates = picked / picked_total

    high = lax.reduce_precision(gates, 8, 7)
    low = gates - high
    spare = jnp.zeros((count, LANES - 2 * E), BF16)
    sent = jnp.concatenate([normed_two, high.astype(BF16), low.astype(BF16), spare], axis=1)
    sent, grads_ahead, down = sync(sent, grads_ahead, down)
    grads_z.append(grads_ahead)
    rows, ahead, second_parts, second_down, others, grads_third = sync(
        ring_gather(sent, "y"),
        ring_step(sent, "z"),
        second_parts,
        ring_gather(down[1], "x"),
        ring_step(sent, "c"),
        [ring_step(part, "c") for part in grads_y[2]],
    )
    grads_other.append(grads_third)
    w_in_parts, w_back_parts = [first_parts, second_parts], [first_down, second_down]
    rows, others = sync(rows, [others] + [ring_step(part, "c") for part in rows[1:]])
    width = w_in_parts[0][0].shape[-1] // (2 * counts[0])

    def plus(first, second, kind=BF16):
        return (first.astype(F32) + second.astype(F32)).astype(kind)

    def plus_all(first, second):
        return [plus(first[i], second[i]) for i in range(y_size)]

    def hops_y(parts):
        return ring_step(parts[1], "y") if y_size == 2 else ring_sum(parts, "y", BF16)

    def end_y(parts, arrived):
        return plus(arrived, parts[0]) if y_size == 2 else arrived

    sent_chunks, grad_chunks, weighted, grad_hidden, grads_gates = [], [], [], [], []
    results_c, grads_c, results_sum, grads_sum = [], [], [], []
    for z_step in range(z_size):
        sent_chunks += rows + others
        grad_chunks += grads_y[z_step] + grads_other[z_step]
        parts = run_experts(
            rows + others,
            grads_y[z_step] + grads_other[z_step],
            w_in_parts,
            w_back_parts,
            counts,
            group,
        )
        moved = {}
        if z_step + 1 < z_size:
            moved["rows"] = ring_gather(ahead, "y")
            moved["others"] = ring_step(ahead, "c")
        if z_step + 2 < z_size:
            moved["ahead"] = ring_step(ahead, "z")
        if z_step == 0:
            moved["grads"] = ring_gather(grads_z[3], "y")
        if z_step == 1:
            moved["grads_other"] = [ring_step(part, "c") for part in grads_y[3]]
        if z_step >= 1:
            moved["grad"] = hops_y(grads_c[-1])
            moved["result"] = ring_step(last_results[1], "c")
        if z_step == 3:
            moved["step"] = ring_step(grads_sum[1], "z")
            moved["result_y"] = hops_y(results_c[0])
        parts, moved = sync(parts, moved)
        weighted.append(parts[4])
        grad_hidden.append(parts[5])
        grads_gates.append(parts[6][:, :local_count])
        if z_step == 0:
            grads_y.append(moved["grads"])
        if z_step == 1:
            grads_other.append(moved["grads_other"])
        arrived = ring_step(parts[3], "c")
        if z_step + 1 < z_size:
            ahead, rows = moved.get("ahead"), moved["rows"]
            others = [ring_step(part, "c") for part in rows[1:]]
        arrived, others, rows = sync(arrived, others, rows)
        others = [moved.get("others")] + others
        if z_step >= 1:
            grads_sum.append(end_y(grads_c[-1], moved["grad"]))
            results_c.append(plus_all(moved["result"], last_results[0]))
        grads_c.append(plus_all(arrived, parts[2]))
        last_results = parts[:2]

    total = plus(moved["step"], grads_sum[2])
    results_sum.append(end_y(results_c[0], moved["result_y"]))
    spread = jnp.stack(grads_gates)
    spread = lax.dynamic_update_slice(
        jnp.zeros(spread.shape[:2] + (E,), F32), spread, (0, 0, group * local_count)
    )
    spread = spread.reshape(z_size, 2, y_size, count, E)
    spread = ring_sum([spread[:, 0], spread[:, 1]], "c", F32)

    def in_grads(which):
        first, last = ranges[which]
        return expert_grads(sent_chunks, grad_hidden, first, last, 2 * width, False)

    def halves(part):
        middle = part.shape[0] // 2
        return part[:middle], part[middle:]

    grads_c, total, results_c, last_results, spread, grad_hidden = sync(
        grads_c, total, results_c, last_results, spread, grad_hidden
    )
    first_grads, last_grad, step, result_two, result_three, spread = sync(
        in_grads(0),
        hops_y(grads_c[3]),
        ring_step(total, "z"),
        hops_y(results_c[1]),
        ring_step(last_results[1], "c"),
        ring_sum([spread[:, i] for i in range(y_size)], "y", F32),
    )
    total = plus(step, end_y(grads_c[3], last_grad))
    results_sum.append(end_y(results_c[1], result_two))
    results_c.append(plus_all(result_three, last_results[0]))
    one, two = halves(first_grads[1])
    grad_hidden, total, results_sum, results_c, one, two = sync(
        grad_hidden, total, results_sum, results_c, one, two
    )
    second_grads, step, result_step, result_two, grad_gates, one = sync(
        in_grads(1),
        ring_step(total, "z"),
        ring_step(results_sum[1], "z"),
        hops_y(results_c[2]),
        ring_sum([spread[i] for i in range(z_size)], "z", F32),
        ring_step(one, "x"),
    )
    grad_experts = plus(step, grads_sum[0], F32)
    results_sum.append(end_y(results_c[2], result_two))
    result_total = plus(result_step, results_sum[2])
    result_total, grad_experts, two = sync(result_total, grad_experts, two)
    result_three = hops_y(results_c[3])
    two = ring_step(two, "x")

    def finish_x(parts, arrived, kind):
        rest = list(parts[2:]) + [parts[0]]
        total = plus(arrived, rest[0], kind)
        for part in rest[1:]:
            total = plus(ring_step(total, "x"), part, kind)
        return total

    def shift_pieces(total):
        pieces = [total[0]]
        for step in range(1, z_size):
            to = [(i, (i + step) % z_size) for i in range(z_size)]
            pieces.append(lax.ppermute(total[step], "z", to))
        return pieces

    grad_picked = chosen * (grad_gates - jnp.sum(grad_gates * gates, axis=-1, keepdims=True))
    grad_chance = grad_picked / picked_total
    grad_logits = (
        chance * (grad_chance - jnp.sum(chance * grad_chance, axis=-1, keepdims=True))
    ).astype(BF16)
    grad_w_router = dot(normed_two, grad_logits, ((0,), (0,)))
    grad_normed_two = grad_experts + dot(grad_logits, w_router, ((1,), (1,)))
    grad_resid, grad_gain_two = norm_back(grad_normed_two, resid, r_two, gain_second)
    grad_resid = grad_final + grad_resid

    grad_att = grad_resid.astype(BF16)
    grad_att = jnp.concatenate([grad_att, ring_step(grad_att, "c")])
    grad_w_out = dot(mixed, grad_att, ((0,), (0,))).astype(BF16)
    grad_mixed = dot(grad_att, w_out, ((1,), (1,))).astype(BF16).reshape(query.shape)
    grad_mixed, grad_w_out, two, result_step, result_three = sync(
        grad_mixed, grad_w_out, two, ring_step(result_total, "z"), result_three
    )
    first_x = jnp.concatenate([one, two])
    result_total = plus(result_step, end_y(results_c[3], result_three))
    out_parts = pick_weights(grad_w_out, "x", "y", False)
    one, two = halves(second_grads[1])
    first_sum, out_parts, grad_mixed, one, two, result_total = sync(
        finish_x(first_grads, first_x, BF16), out_parts, grad_mixed, one, two, result_total
    )
    first_pieces = shift_pieces(first_sum)
    one = ring_step(one, "x")
    result_step = ring_step(result_total, "z")
    out_sum = ring_sum(out_parts, "y", BF16)
    grad_probs = jnp.einsum("bqkgd,bskd->bkgqs", grad_mixed, values, preferred_element_type=F32)
    grad_value_pre = jnp.einsum(
        "bkgqs,bqkgd->bskd", probs_low, grad_mixed, preferred_element_type=F32
    )
    grad_value_pre = grad_value_pre.reshape(2 * count, kv_width).astype(BF16)
    grad_scores = (
        probs * (grad_probs - jnp.sum(probs * grad_probs, axis=-1, keepdims=True))
    ).astype(BF16)
    grad_query = jnp.einsum("bkgqs,bskd->bqkgd", grad_scores, keys, preferred_element_type=F32)
    grad_keys = jnp.einsum("bkgqs,bqkgd->bskd", grad_scores, query, preferred_element_type=F32)
    grad_query_pre = rotary_embedding(
        (grad_query * score_scale).reshape(query_pre.shape), token_position, -1.0
    )
    grad_query_pre = grad_query_pre.reshape(2 * count, q_width).astype(BF16)
    grad_key_pre = rotary_embedding(grad_keys * score_scale, token_position, -1.0)
    grad_key_pre = grad_key_pre.reshape(2 * count, kv_width).astype(BF16)
    grad_qk_pre = jnp.concatenate([grad_query_pre, grad_key_pre], axis=1)
    grad_qk_pre, grad_value_pre, out_sum, result_step, one, two = sync(
        grad_qk_pre, grad_value_pre, out_sum, result_step, one, two
    )
    outputs = resid + plus(result_step, results_sum[0], F32)
    two = ring_step(two, "x")
    out_sum = sum_along(out_sum, "x")
    grad_w_qk = dot(normalized_input, grad_qk_pre, ((0,), (0,))).astype(BF16)
    grad_w_v = dot(normalized_input, grad_value_pre, ((0,), (0,))).astype(BF16)
    grad_normed = dot(grad_qk_pre, w_qk, ((1,), (1,)))
    grad_normed = grad_normed + dot(grad_value_pre, w_v, ((1,), (1,)))
    grad_normed = ring_sum([grad_normed[:count], grad_normed[count:]], "c", F32)
    grad_rows, grad_gain_one = norm_back(grad_normed, own_act, r_one[:count], gain_first)
    grad_rows = grad_resid + grad_rows

    grad_small = jnp.concatenate(
        [grad_w_router, grad_gain_one[:, None], grad_gain_two[:, None]], axis=1
    )
    grad_small = jnp.pad(grad_small, ((0, 0), (0, LANES - grad_small.shape[1])))
    grad_vs = jnp.concatenate([grad_w_v, grad_small.astype(BF16)], axis=1)
    q_parts = pick_weights(grad_w_qk[:, :q_width], "x", "y", True)
    rest_parts = pick_weights(
        jnp.concatenate([grad_w_qk[:, q_width:], grad_vs], axis=1), "y", "x", True
    )
    q_parts, rest_parts, grad_rows, grad_chunks, first_pieces, out_sum, two = sync(
        q_parts, rest_parts, grad_rows, grad_chunks, first_pieces, out_sum, two
    )
    second_sum = finish_x(second_grads, jnp.concatenate([one, two]), BF16)
    second_sum, q_parts, rest_parts, grad_chunks = sync(
        second_sum, q_parts, rest_parts, grad_chunks
    )
    second_pieces = shift_pieces(second_sum)
    out_sum = sum_along(out_sum, "z", F32)
    grad_w_back, q_sum, rest_sum = sync(
        expert_grads(grad_chunks, weighted, 0, local_count, width, True),
        ring_sum(q_parts, "y", BF16),
        ring_sum(rest_parts, "x", BF16),
    )
    back_x = ring_step(grad_w_back[1], "x")
    q_sum, rest_sum, grad_w_out = sync(
        sum_along(q_sum, "x"), sum_along(rest_sum, "y"), out_sum
    )
    grad_first, grad_second, first_pieces, second_pieces = sync(
        sum_along(q_sum, "z", F32), sum_along(rest_sum, "z", F32), first_pieces, second_pieces
    )
    grad_w_gate, grad_w_up = unpack_experts([first_pieces, second_pieces], counts)
    grad_w_down = finish_x(grad_w_back, back_x, F32)
    grad_both = jnp.concatenate([grad_first, grad_second], axis=-1)
    mine = lax.dynamic_index_in_dim(grad_both, core, 0, keepdims=False)
    theirs = lax.dynamic_index_in_dim(grad_both, 1 - core, 0, keepdims=False)
    got = ring_step(theirs, "c")

    def whole_columns(start, columns):
        parts = [part[:, start : start + columns].reshape(own_rows, y_size, -1) for part in (mine, got)]
        ordered = jnp.where(core == 0, jnp.stack(parts, 2), jnp.stack(parts[::-1], 2))
        return ordered.reshape(own_rows, 2 * columns)

    grad_small = (mine + got)[:, q_width + 2 * kv_width :]
    return (
        outputs.astype(BF16).reshape(inputs.shape),
        grad_rows.reshape(inputs.shape),
        grad_small[:, E],
        whole_columns(0, q_width),
        whole_columns(q_width, kv_width),
        whole_columns(q_width + kv_width, kv_width),
        grad_w_out,
        grad_small[:, E + 1],
        grad_small[:, :E],
        grad_w_gate,
        grad_w_up,
        grad_w_down,
    )


def solution(mesh):
    experts, shards = mesh.shape["expert"], mesh.shape["shard"]
    split = Mesh(
        mesh.devices.reshape(experts // 2, 2, SLICES, shards // SLICES), ("y", "c", "z", "x")
    )
    groups, within = ("y", "c"), ("z", "x")
    tokens = P(None, ALL, None)
    rows = P(ALL, None)
    expert = P(groups, within, None)
    return jax.shard_map(
        body,
        mesh=split,
        in_specs=(tokens,) * 4
        + (P(ALL), rows, rows, rows, rows, P(ALL), rows, expert, expert, expert),
        out_specs=(tokens, tokens, P(ALL), rows, rows, rows, rows, P(ALL), rows)
        + (expert, expert, expert),
        check_vma=False,
    )
```

time: 1270 us -> 879 us (0.69)
  Pallas kernels: 0 us -> 267 us
  matrix products: 272 us -> 27.2 us
  waiting for transfers between devices: 486 us -> 252 us
  local copies, waits for them, and re-layouts: 262 us -> 95.6 us
  starting transfers between devices: 92.3 us -> 130 us
  other arithmetic: 131 us -> 94.6 us
  between operations: 16.5 us -> 3.44 us
    pallas_call x0 -> x14, Pallas kernels: none -> 267 us  [the longest x4 157 us: run_experts(): pl.pallas_call(functools.partial(experts_kernel, counts, steps, x_size),...]
    dot_general x27 -> x12, matrix products: 263 us -> 22.2 us  [dot(): lax.dot_general(left, right, (dims, ((), ())), preferred_element_type=F32)]
    ppermute x59 -> x103, waiting for transfers between devices: 380 us -> 247 us  [ring_step(): return lax.ppermute(array, axis, [(i, (i + 1) % size) for i in range(size)])]
    reduce_scatter x2 -> x0, waiting for transfers between devices: 83.3 us -> none  [the longest x1 83.3 us: body(): lax.psum_scatter(grad_mine, ALL, scatter_dimension=0, tiled=True)]
    slice x28 -> x23, local copies, waits for them, and re-layouts: 59.9 us -> 16.4 us  [the longest x2 4.41 us: halves(): return (part[:middle], part[middle:])]
    dot_general x3 -> x1, local copies, waits for them, and re-layouts: 36.7 us -> 0.1 us  [dot(): lax.dot_general(left, right, (dims, ((), ())), preferred_element_type=F32)]
    dynamic_update_slice x9 -> x1, local copies, waits for them, and re-layouts: 29.2 us -> 0.36 us  [body(): lax.dynamic_update_slice(jnp.zeros(spread.shape[:2] + (E,), F32), spread,...]
    ppermute x59 -> x103, starting transfers between devices: 81.7 us -> 110 us  [ring_step(): return lax.ppermute(array, axis, [(i, (i + 1) % size) for i in range(size)])]
  transfers between devices with their start and end apart: 65 -> 111, of which waited for: 23 -> 36; matrix products, arithmetic and copies ran while one was open for 51% -> 19% of each run, Pallas kernels for 0% -> 30%
where the time goes in v2:
time: 879 us; the launch traced here: 870 us
  Pallas kernels  267 us (30%)
  waiting for transfers between devices  252 us (29%)
  starting transfers between devices  130 us (15%)
  local copies, waits for them, and re-layouts  95.6 us (11%)
  other arithmetic  94.6 us (11%)
  matrix products  27.2 us (3%)
    ppermute x103, waiting for transfers between devices, ring_step(): return lax.ppermute(array, axis, [(i, (i + 1) % size) for i in range(size)])  247 us
    pallas_call x4, Pallas kernels, run_experts(): pl.pallas_call(functools.partial(experts_kernel, counts, steps, x_size),...  157 us
    ppermute x103, starting transfers between devices, ring_step(): return lax.ppermute(array, axis, [(i, (i + 1) % size) for i in range(size)])  110 us
    pallas_call x3, Pallas kernels, expert_grads(): pl.pallas_call(functools.partial(expert_grads_kernel, len(whole), len(col...  77.1 us
    convert_element_type x17, other arithmetic, plus(): return (first.astype(F32) + second.astype(F32)).astype(kind)  39.8 us
    unnamed x343, local copies, waits for them, and re-layouts  36.5 us
    dot_general x12, matrix products, dot(): lax.dot_general(left, right, (dims, ((), ())), preferred_element_type=F32)  22.2 us
  transfers between devices with their start and end apart: 111, of which 36 were waited for; matrix products, arithmetic and copies ran while one was open for 19% of the time, Pallas kernels for 30%

profile of v2, /device:TPU:1, one launch (start us, length us, event | category | flops | bytes accessed | tf_op | source)
XLA Modules:
  0.0 869.6 jit_solution(5605169769582398323)
XLA Ops:
  16.6 5.9 collective-permute-done.1.refs_4_
  27.5 10.9 %collective-permute-done.7.refs_13_ = bf16[5,64,1536]{2,1,0:T(8,128)(2,1)} collective-permute-done((bf16[5,64,1536]{2,1,0:T(8,128)(2,1)}, bf16[5,64,1536]{2,1,0:T(8,128)(2,1)}, u32[]{:S(2)}, u32[]{:S(2)}) %collective-permute-start.7) | collective-permute-done | bytes 983072 | tf_op jit(solution)/shard_map/ppermute | solution.py:39
  39.7 4.6 pack_experts.2
  44.3 4.6 pack_experts.3
  48.8 6.5 collective-permute-done.3
  57.9 9.7 %collective-permute-done.9.refs_10_ = bf16[2,2,48,1024]{3,2,1,0:T(8,128)(2,1)S(1)} collective-permute-done((bf16[2,2,48,1024]{3,2,1,0:T(8,128)(2,1)S(1)}, bf16[2,2,48,1024]{3,2,1,0:T(8,128)(2,1)S(1)}, u32[]{:S(2)}, u32[]{:S(2)}) %collective-permute-start.9) | collective-permute-done | bytes 393248 | tf_op jit(solution)/shard_map/ppermute | solution.py:39
  74.1 5.9 collective-permute-done.18.refs_9_
  80.7 7.6 collective-permute-done.19.refs_11_
  91.3 4.4 all-to-all-start
  99.2 5.0 collective-permute-done.22.refs_14_
  108.1 3.4 maximum_convert_fusion
  113.5 5.5 collective-permute-done.26.refs_15_
  129.2 6.5 place_weights.1
  145.8 4.9 all-to-all-start.1
  184.9 6.4 collective-permute-done.28.refs_5_.refs_9_
  191.3 4.3 all-to-all-done.1.refs_10_
  214.0 11.1 %collective-permute-done.30.refs_4_.refs_12_ = bf16[256,1536]{1,0:T(8,128)(2,1)} collective-permute-done((bf16[256,1536]{1,0:T(8,128)(2,1)}, bf16[256,1536]{1,0:T(8,128)(2,1)}, u32[]{:S(2)}, u32[]{:S(2)}) %collective-permute-start.30) | collective-permute-done | bytes 786464 | tf_op jit(solution)/shard_map/ppermute | solution.py:39
  228.4 21.3 %collective-permute-done.33.refs_11_ = bf16[4,192,1280]{2,1,0:T(8,128)(2,1)} collective-permute-done((bf16[4,192,1280]{2,1,0:T(8,128)(2,1)}, bf16[4,192,1280]{2,1,0:T(8,128)(2,1)}, u32[]{:S(2)}, u32[]{:S(2)}) %collective-permute-start.33) | collective-permute-done | bytes 1966112 | tf_op jit(solution)/shard_map/ppermute | solution.py:39
  249.7 20.9 %collective-permute-done.34.refs_15_ = bf16[5,64,1536]{2,1,0:T(8,128)(2,1)S(1)} collective-permute-done((bf16[5,64,1536]{2,1,0:T(8,128)(2,1)S(1)}, bf16[5,64,1536]{2,1,0:T(8,128)(2,1)S(1)}, u32[]{:S(2)}, u32[]{:S(2)}) %collective-permute-start.34) | collective-permute-done | bytes 983072 | tf_op jit(solution)/shard_map/ppermute | solution.py:39
  278.0 39.0 %experts.4 = (bf16[2,256,1536]{2,1,0:T(8,128)(2,1)}, bf16[2,256,1536]{2,1,0:T(8,128)(2,1)}, bf16[2,256,1536]{2,1,0:T(8,128)(2,1)}, bf16[2,256,1536]{2,1,0:T(8,12...) custom-call(s32[3]{0:T(128)} %pad_add_fusion.1.place_ref, ...), custom_call_target="tpu_custom_call" | custom-call | flops 24159191040 | bytes 31457280 | tf_op jit(solution)/shard_map/experts/pallas_call | solution.py:331
  328.7 39.1 %experts.5 = (bf16[2,256,1536]{2,1,0:T(8,128)(2,1)}, bf16[2,256,1536]{2,1,0:T(8,128)(2,1)}, bf16[2,256,1536]{2,1,0:T(8,128)(2,1)}, bf16[2,256,1536]{2,1,0:T(8,12...) custom-call(s32[3]{0:T(128)} %pad_add_fusion.1.place_ref, ...), custom_call_target="tpu_custom_call" | custom-call | flops 24159191040 | bytes 31457280 | tf_op jit(solution)/shard_map/experts/pallas_call | solution.py:331
  379.6 39.4 %experts.6 = (bf16[2,256,1536]{2,1,0:T(8,128)(2,1)}, bf16[2,256,1536]{2,1,0:T(8,128)(2,1)}, bf16[2,256,1536]{2,1,0:T(8,128)(2,1)}, bf16[2,256,1536]{2,1,0:T(8,12...) custom-call(s32[3]{0:T(128)} %pad_add_fusion.1.place_ref, ...), custom_call_target="tpu_custom_call" | custom-call | flops 24159191040 | bytes 31457280 | tf_op jit(solution)/shard_map/experts/pallas_call | solution.py:331
  419.0 9.4 %collective-permute-done.54 = bf16[256,1536]{1,0:T(8,128)(2,1)} collective-permute-done((bf16[256,1536]{1,0:T(8,128)(2,1)}, bf16[256,1536]{1,0:T(8,128)(2,1)}, u32[]{:S(2)}, u32[]{:S(2)}) %collective-permute-start.54) | collective-permute-done | bytes 786464 | tf_op jit(solution)/shard_map/ppermute | solution.py:39
  441.1 39.4 %experts.7 = (bf16[2,256,1536]{2,1,0:T(8,128)(2,1)}, bf16[2,256,1536]{2,1,0:T(8,128)(2,1)}, bf16[2,256,1536]{2,1,0:T(8,128)(2,1)}, bf16[2,256,1536]{2,1,0:T(8,12...) custom-call(s32[3]{0:T(128)} %pad_add_fusion.1.place_ref, ...), custom_call_target="tpu_custom_call" | custom-call | flops 24159191040 | bytes 31457280 | tf_op jit(solution)/shard_map/experts/pallas_call | solution.py:331
  502.5 25.6 %expert_grads.3 = (bf16[4,192,1280]{2,1,0:T(8,128)(2,1)}, bf16[4,192,1280]{2,1,0:T(8,128)(2,1)}) custom-call(s32[6]{0:T(128)} %stack.210.place_ref, bf16[256,1664]{1,0:T(8,128)(2,1)} %copy-done.99, bf16[256,1664]{1,0:T(8,128)(2,1)} %copy-done.150, bf16[256,1664]{1,0:T(8,128)(2,1)} %copy-done.152, bf16[256,1664]{1,0:T(8,128)(2,1)} %copy-done.153, ...), custom_call_target="tpu_custom_call" | custom-call | flops 16106127360 | bytes 23068672 | tf_op jit(solution)/shard_map/expert_grads/pallas_call | solution.py:426
  528.1 17.4 %collective-permute-done.70 = f32[4,256,40]{2,1,0:T(8,128)} collective-permute-done((f32[4,256,40]{2,1,0:T(8,128)S(1)}, f32[4,256,40]{2,1,0:T(8,128)}, u32[]{:S(2)}, u32[]{:S(2)}) %collective-permute-start.70) | collective-permute-done | bytes 163872 | tf_op jit(solution)/shard_map/ppermute | solution.py:39
  564.3 25.5 %expert_grads.4 = (bf16[4,192,1280]{2,1,0:T(8,128)(2,1)}, bf16[4,192,1280]{2,1,0:T(8,128)(2,1)}) custom-call(s32[6]{0:T(128)} %stack.210.place_ref, bf16[256,1664]{1,0:T(8,128)(2,1)} %copy-done.99, bf16[256,1664]{1,0:T(8,128)(2,1)} %copy-done.150, bf16[256,1664]{1,0:T(8,128)(2,1)} %copy-done.152, bf16[256,1664]{1,0:T(8,128)(2,1)} %copy-done.153, ...), custom_call_target="tpu_custom_call" | custom-call | flops 16106127360 | bytes 23068672 | tf_op jit(solution)/shard_map/expert_grads/pallas_call | solution.py:426
  589.8 8.9 %collective-permute-done.76 = f32[256,40]{1,0:T(8,128)S(1)} collective-permute-done((f32[256,40]{1,0:T(8,128)S(1)}, f32[256,40]{1,0:T(8,128)S(1)}, u32[]{:S(2)}, u32[]{:S(2)}) %collective-permute-start.76) | collective-permute-done | bytes 40992 | tf_op jit(solution)/shard_map/ppermute | solution.py:39
  629.5 6.7 collective-permute-done.80
  637.6 4.3 pick_weights.3
  659.7 17.6 %collective-permute-done.82 = bf16[2,4,48,1536]{3,2,1,0:T(8,128)(2,1)S(1)} collective-permute-done((bf16[2,4,48,1536]{3,2,1,0:T(8,128)(2,1)S(1)}, bf16[2,4,48,1536]{3,2,1,0:T(8,128)(2,1)S(1)}, u32[]{:S(2)}, u32[]{:S(2)}) %collective-permute-start.82) | collective-permute-done | bytes 1179680 | tf_op jit(solution)/shard_map/ppermute | solution.py:39
  694.3 5.9 collective-permute-done.89
  707.1 3.3 pick_weights.5
  710.5 3.8 fusion.17
  714.3 8.8 %collective-permute-done.90 = bf16[2,192,1280]{2,1,0:T(8,128)(2,1)} collective-permute-done((bf16[2,192,1280]{2,1,0:T(8,128)(2,1)}, bf16[2,192,1280]{2,1,0:T(8,128)(2,1)}, u32[]{:S(2)}, u32[]{:S(2)}) %collective-permute-start.90) | collective-permute-done | bytes 983072 | tf_op jit(solution)/shard_map/ppermute | solution.py:39
  733.0 26.0 %expert_grads.5 = (bf16[10,64,1536]{2,1,0:T(8,128)(2,1)}, bf16[10,64,1536]{2,1,0:T(8,128)(2,1)}) custom-call(s32[2]{0:T(128)} %pad_add_fusion.2.place_ref, bf16[256,1536]{1,0:T(8,128)(2,1)} %bitcast.7.refs_4_.refs_0_, bf16[256,1536]{1,0:T(8,128)(2,1)} %collective-permute-done.2.refs_5_.refs_1_, bf16[256,1536]{1,0:T(8,128)(2,1)} %collective-permute-done.12.refs_6_.refs_2_, ...), custom_call_target="tpu_custom_call" | custom-call | flops 16106127360 | bytes 23068672 | tf_op jit(solution)/shard_map/expert_grads/pallas_call | solution.py:426
  759.0 3.3 collective-permute-start.106
  770.1 5.0 collective-permute-done.97
  778.3 5.8 collective-permute-done.93
  787.4 4.0 collective-permute-done.101
  791.5 5.7 collective-permute-done.98
  797.2 5.5 collective-permute-done.102
  802.8 5.7 collective-permute-done.99
  808.5 7.0 collective-permute-done.103
  815.6 6.7 collective-permute-done.100
  823.3 28.6 %collective-permute-start.107 = (f32[48,1408]{1,0:T(8,128)S(1)}, f32[48,1408]{1,0:T(8,128)S(1)}, u32[]{:S(2)}, u32[]{:S(2)}) collective-permute-start(f32[48,1408]{1,0:T(8,128)S(1)} %dynamic-slice_bitcast_fusion), channel_id=1, source_target_pairs={{0,8},{8,0},{1,9},{9,1},{2,10},{10,2},{3,11},{11,3},{4,12},{12,4},... | collective-permute-start | bytes 811016 | tf_op jit(solution)/shard_map/ppermute | solution.py:39
  853.1 7.3 unpack_experts.1
  865.2 4.2 convert_add_fusion
  (742 shorter events, 307.8 us)
Async XLA Ops:
  22.4 32.9 %collective-permute-start.6 = (bf16[256,1536]{1,0:T(8,128)(2,1)}, bf16[256,1536]{1,0:T(8,128)(2,1)}, u32[]{:S(2)}, u32[]{:S(2)}) collective-permute-start(bf16[256,1536]{1,0:T(8,128)(2,1)} %collective-permute-done.1.refs_4_), channel_id=1, source_target_pairs={{0,16},{16,0},{1,17},{17,1},{2,18},{18,2},{3,19},{19,3},{4,20},{20... | collective-permute-start | bytes 2359304 | tf_op jit(solution)/shard_map/ppermute | solution.py:39
  25.2 31.0 %collective-permute-start.11 = (bf16[256,1536]{1,0:T(8,128)(2,1)}, bf16[256,1536]{1,0:T(8,128)(2,1)}, u32[]{:S(2)}, u32[]{:S(2)}) collective-permute-start(bf16[256,1536]{1,0:T(8,128)(2,1)} %collective-permute-done.1.refs_4_), channel_id=1, source_target_pairs={{0,2},{2,4},{4,6},{6,0},{1,3},{3,5},{5,7},{7,1},{8,10},{10,12},{12... | collective-permute-start | bytes 2359304 | tf_op jit(solution)/shard_map/ppermute | solution.py:39
  26.0 30.2 %collective-permute-start.12 = (bf16[256,1536]{1,0:T(8,128)(2,1)}, bf16[256,1536]{1,0:T(8,128)(2,1)}, u32[]{:S(2)}, u32[]{:S(2)}) collective-permute-start(bf16[256,1536]{1,0:T(8,128)(2,1)} %bitcast.7.refs_4_.refs_0_), channel_id=1, source_target_pairs={{0,8},{8,0},{1,9},{9,1},{2,10},{10,2},{3,11},{11,3},{4,12},{12,4},... | collective-permute-start | bytes 2359304 | tf_op jit(solution)/shard_map/ppermute | solution.py:39
  26.3 29.0 %collective-permute-start.3 = (bf16[2,48,2176]{2,1,0:T(8,128)(2,1)S(1)}, bf16[2,48,2176]{2,1,0:T(8,128)(2,1)S(1)}, u32[]{:S(2)}, u32[]{:S(2)}) collective-permute-start(bf16[2,48,2176]{2,1,0:T(8,128)(2,1)S(1)} %maximum_maximum_fusion), channel_id=1, source_target_pairs={{0,2},{2,4},{4,6},{6,0},{1,3},{3,5},{5,7},{7,1},{8,10},{10,12},{12... | collective-permute-start | bytes 1253384 | tf_op jit(solution)/shard_map/ppermute | solution.py:39
  91.3 54.4 %all-to-all-start = ((bf16[4,192,1280]{2,1,0:T(8,128)(2,1)}), bf16[4,192,1280]{2,1,0:T(8,128)(2,1)}, u32[]{:S(2)}, u32[]{:S(2)}) async-start(bf16[4,192,1280]{2,1,0:T(8,128)(2,1)} %pack_experts.2), calls=%async_computation | async-start | bytes 3932160 | tf_op jit(solution)/shard_map/all_to_all | solution.py:588
  145.8 49.8 %all-to-all-start.1 = ((bf16[4,192,1280]{2,1,0:T(8,128)(2,1)}), bf16[4,192,1280]{2,1,0:T(8,128)(2,1)}, u32[]{:S(2)}, u32[]{:S(2)}) async-start(bf16[4,192,1280]{2,1,0:T(8,128)(2,1)} %pack_experts.3), calls=%async_computation.1 | async-start | bytes 3932160 | tf_op jit(solution)/shard_map/all_to_all | solution.py:615
  151.9 39.4 %collective-permute-start.27 = (bf16[4,192,1280]{2,1,0:T(8,128)(2,1)}, bf16[4,192,1280]{2,1,0:T(8,128)(2,1)}, u32[]{:S(2)}, u32[]{:S(2)}) collective-permute-start(bf16[4,192,1280]{2,1,0:T(8,128)(2,1)} %all-to-all-done.refs_8_), channel_id=1, source_target_pairs={{0,1},{1,0},{2,3},{3,2},{4,5},{5,4},{6,7},{7,6},{8,9},{9,8},{10,11... | collective-permute-start | bytes 5898248 | tf_op jit(solution)/shard_map/ppermute | solution.py:39
  205.7 43.9 %collective-permute-start.33 = (bf16[4,192,1280]{2,1,0:T(8,128)(2,1)}, bf16[4,192,1280]{2,1,0:T(8,128)(2,1)}, u32[]{:S(2)}, u32[]{:S(2)}) collective-permute-start(bf16[4,192,1280]{2,1,0:T(8,128)(2,1)} %all-to-all-done.1.refs_10_), channel_id=1, source_target_pairs={{0,1},{1,0},{2,3},{3,2},{4,5},{5,4},{6,7},{7,6},{8,9},{9,8},{10,11... | collective-permute-start | bytes 5898248 | tf_op jit(solution)/shard_map/ppermute | solution.py:39
  225.1 45.5 %collective-permute-start.34 = (bf16[5,64,1536]{2,1,0:T(8,128)(2,1)S(1)}, bf16[5,64,1536]{2,1,0:T(8,128)(2,1)S(1)}, u32[]{:S(2)}, u32[]{:S(2)}) collective-permute-start(bf16[5,64,1536]{2,1,0:T(8,128)(2,1)S(1)} %copy-done.97), channel_id=1, source_target_pairs={{0,1},{1,0},{2,3},{3,2},{4,5},{5,4},{6,7},{7,6},{8,9},{9,8},{10,11... | collective-permute-start | bytes 2949128 | tf_op jit(solution)/shard_map/ppermute | solution.py:39
  273.8 43.1 %collective-permute-start.40 = (bf16[256,1536]{1,0:T(8,128)(2,1)}, bf16[256,1536]{1,0:T(8,128)(2,1)}, u32[]{:S(2)}, u32[]{:S(2)}) collective-permute-start(bf16[256,1536]{1,0:T(8,128)(2,1)} %collective-permute-done.30.refs_4_.refs_12_), channel_id=1, source_target_pairs={{0,16},{16,0},{1,17},{17,1},{2,18},{18,2},{3,19},{19,3},{4,20},{20... | collective-permute-start | bytes 2359304 | tf_op jit(solution)/shard_map/ppermute | solution.py:39
  274.0 43.0 %collective-permute-start.39 = (bf16[256,1664]{1,0:T(8,128)(2,1)}, bf16[256,1664]{1,0:T(8,128)(2,1)}, u32[]{:S(2)}, u32[]{:S(2)}) collective-permute-start(bf16[256,1664]{1,0:T(8,128)(2,1)} %copy-done.151), channel_id=1, source_target_pairs={{0,2},{2,4},{4,6},{6,0},{1,3},{3,5},{5,7},{7,1},{8,10},{10,12},{12... | collective-permute-start | bytes 2555912 | tf_op jit(solution)/shard_map/ppermute | solution.py:39
  275.2 41.8 %collective-permute-start.41 = (bf16[256,1664]{1,0:T(8,128)(2,1)}, bf16[256,1664]{1,0:T(8,128)(2,1)}, u32[]{:S(2)}, u32[]{:S(2)}) collective-permute-start(bf16[256,1664]{1,0:T(8,128)(2,1)} %copy-done.151), channel_id=1, source_target_pairs={{0,8},{8,0},{1,9},{9,1},{2,10},{10,2},{3,11},{11,3},{4,12},{12,4},... | collective-permute-start | bytes 2555912 | tf_op jit(solution)/shard_map/ppermute | solution.py:39
  275.7 41.2 %collective-permute-start.42 = (bf16[256,1664]{1,0:T(8,128)(2,1)}, bf16[256,1664]{1,0:T(8,128)(2,1)}, u32[]{:S(2)}, u32[]{:S(2)}) collective-permute-start(bf16[256,1664]{1,0:T(8,128)(2,1)} %copy-done.151), channel_id=1, source_target_pairs={{0,16},{16,0},{1,17},{17,1},{2,18},{18,2},{3,19},{19,3},{4,20},{20... | collective-permute-start | bytes 2555912 | tf_op jit(solution)/shard_map/ppermute | solution.py:39
  318.1 49.8 %collective-permute-start.45 = (bf16[256,1664]{1,0:T(8,128)(2,1)}, bf16[256,1664]{1,0:T(8,128)(2,1)}, u32[]{:S(2)}, u32[]{:S(2)}) collective-permute-start(bf16[256,1664]{1,0:T(8,128)(2,1)} %collective-permute-done.39.refs_0_.refs_8_), channel_id=1, source_target_pairs={{0,2},{2,4},{4,6},{6,0},{1,3},{3,5},{5,7},{7,1},{8,10},{10,12},{12... | collective-permute-start | bytes 2555912 | tf_op jit(solution)/shard_map/ppermute | solution.py:39
  321.9 46.0 %collective-permute-start.49 = (bf16[256,1664]{1,0:T(8,128)(2,1)}, bf16[256,1664]{1,0:T(8,128)(2,1)}, u32[]{:S(2)}, u32[]{:S(2)}) collective-permute-start(bf16[256,1664]{1,0:T(8,128)(2,1)} %collective-permute-done.39.refs_0_.refs_8_), channel_id=1, source_target_pairs={{0,8},{8,0},{1,9},{9,1},{2,10},{10,2},{3,11},{11,3},{4,12},{12,4},... | collective-permute-start | bytes 2555912 | tf_op jit(solution)/shard_map/ppermute | solution.py:39
  322.8 45.1 %collective-permute-start.51 = (bf16[256,1664]{1,0:T(8,128)(2,1)}, bf16[256,1664]{1,0:T(8,128)(2,1)}, u32[]{:S(2)}, u32[]{:S(2)}) collective-permute-start(bf16[256,1664]{1,0:T(8,128)(2,1)} %collective-permute-done.39.refs_0_.refs_8_), channel_id=1, source_target_pairs={{0,16},{16,0},{1,17},{17,1},{2,18},{18,2},{3,19},{19,3},{4,20},{20... | collective-permute-start | bytes 2555912 | tf_op jit(solution)/shard_map/ppermute | solution.py:39
  326.0 41.9 %collective-permute-start.50 = (bf16[2,256,1536]{2,1,0:T(8,128)(2,1)}, bf16[2,256,1536]{2,1,0:T(8,128)(2,1)S(1)}, u32[]{:S(2)}, u32[]{:S(2)}) collective-permute-start(bf16[2,256,1536]{2,1,0:T(8,128)(2,1)} %get-tuple-element.411), channel_id=1, source_target_pairs={{0,8},{8,0},{1,9},{9,1},{2,10},{10,2},{3,11},{11,3},{4,12},{12,4},... | collective-permute-start | bytes 4718600 | tf_op jit(solution)/shard_map/ppermute | solution.py:39
  327.4 40.4 %collective-permute-start.46 = (bf16[256,1536]{1,0:T(8,128)(2,1)}, bf16[256,1536]{1,0:T(8,128)(2,1)}, u32[]{:S(2)}, u32[]{:S(2)}) collective-permute-start(bf16[256,1536]{1,0:T(8,128)(2,1)} %get-tuple-element.704), channel_id=1, source_target_pairs={{0,16},{16,0},{1,17},{17,1},{2,18},{18,2},{3,19},{19,3},{4,20},{20... | collective-permute-start | bytes 2359304 | tf_op jit(solution)/shard_map/ppermute | solution.py:39
  373.6 45.3 %collective-permute-start.55 = (bf16[256,1664]{1,0:T(8,128)(2,1)}, bf16[256,1664]{1,0:T(8,128)(2,1)}, u32[]{:S(2)}, u32[]{:S(2)}) collective-permute-start(bf16[256,1664]{1,0:T(8,128)(2,1)} %collective-permute-done.45.refs_0_.refs_12_), channel_id=1, source_target_pairs={{0,8},{8,0},{1,9},{9,1},{2,10},{10,2},{3,11},{11,3},{4,12},{12,4},... | collective-permute-start | bytes 2555912 | tf_op jit(solution)/shard_map/ppermute | solution.py:39
  374.0 45.0 %collective-permute-start.57 = (bf16[256,1664]{1,0:T(8,128)(2,1)}, bf16[256,1664]{1,0:T(8,128)(2,1)}, u32[]{:S(2)}, u32[]{:S(2)}) collective-permute-start(bf16[256,1664]{1,0:T(8,128)(2,1)} %collective-permute-done.45.refs_0_.refs_12_), channel_id=1, source_target_pairs={{0,16},{16,0},{1,17},{17,1},{2,18},{18,2},{3,19},{19,3},{4,20},{20... | collective-permute-start | bytes 2555912 | tf_op jit(solution)/shard_map/ppermute | solution.py:39
  374.2 44.8 %collective-permute-start.56 = (bf16[2,256,1536]{2,1,0:T(8,128)(2,1)}, bf16[2,256,1536]{2,1,0:T(8,128)(2,1)}, u32[]{:S(2)}, u32[]{:S(2)}) collective-permute-start(bf16[2,256,1536]{2,1,0:T(8,128)(2,1)} %get-tuple-element.431), channel_id=1, source_target_pairs={{0,8},{8,0},{1,9},{9,1},{2,10},{10,2},{3,11},{11,3},{4,12},{12,4},... | collective-permute-start | bytes 4718600 | tf_op jit(solution)/shard_map/ppermute | solution.py:39
  375.8 104.8 %collective-permute-start.62 = (bf16[256,1536]{1,0:T(8,128)(2,1)}, bf16[256,1536]{1,0:T(8,128)(2,1)}, u32[]{:S(2)}, u32[]{:S(2)}) collective-permute-start(bf16[256,1536]{1,0:T(8,128)(2,1)} %fusion.36), channel_id=1, source_target_pairs={{0,16},{16,0},{1,17},{17,1},{2,18},{18,2},{3,19},{19,3},{4,20},{20... | collective-permute-start | bytes 2359304 | tf_op jit(solution)/shard_map/ppermute | solution.py:39
  379.4 49.1 %collective-permute-start.54 = (bf16[256,1536]{1,0:T(8,128)(2,1)}, bf16[256,1536]{1,0:T(8,128)(2,1)}, u32[]{:S(2)}, u32[]{:S(2)}) collective-permute-start(bf16[256,1536]{1,0:T(8,128)(2,1)} %fusion.31), channel_id=1, source_target_pairs={{0,16},{16,0},{1,17},{17,1},{2,18},{18,2},{3,19},{19,3},{4,20},{20... | collective-permute-start | bytes 2359304 | tf_op jit(solution)/shard_map/ppermute | solution.py:39
  434.1 46.4 %collective-permute-start.61 = (bf16[2,256,1536]{2,1,0:T(8,128)(2,1)}, bf16[2,256,1536]{2,1,0:T(8,128)(2,1)}, u32[]{:S(2)}, u32[]{:S(2)}) collective-permute-start(bf16[2,256,1536]{2,1,0:T(8,128)(2,1)} %get-tuple-element.450), channel_id=1, source_target_pairs={{0,8},{8,0},{1,9},{9,1},{2,10},{10,2},{3,11},{11,3},{4,12},{12,4},... | collective-permute-start | bytes 4718600 | tf_op jit(solution)/shard_map/ppermute | solution.py:39
  434.6 46.0 %collective-permute-start.63 = (bf16[256,1536]{1,0:T(8,128)(2,1)}, bf16[256,1536]{1,0:T(8,128)(2,1)}, u32[]{:S(2)}, u32[]{:S(2)}) collective-permute-start(bf16[256,1536]{1,0:T(8,128)(2,1)} %add_convert_fusion.26), channel_id=1, source_target_pairs={{0,2},{2,4},{4,6},{6,0},{1,3},{3,5},{5,7},{7,1},{8,10},{10,12},{12... | collective-permute-start | bytes 2359304 | tf_op jit(solution)/shard_map/ppermute | solution.py:39
  440.9 39.7 %collective-permute-start.60 = (bf16[256,1536]{1,0:T(8,128)(2,1)S(1)}, bf16[256,1536]{1,0:T(8,128)(2,1)}, u32[]{:S(2)}, u32[]{:S(2)}) collective-permute-start(bf16[256,1536]{1,0:T(8,128)(2,1)S(1)} %fusion.35), channel_id=1, source_target_pairs={{0,16},{16,0},{1,17},{17,1},{2,18},{18,2},{3,19},{19,3},{4,20},{20... | collective-permute-start | bytes 2359304 | tf_op jit(solution)/shard_map/ppermute | solution.py:39
  498.3 48.3 %collective-permute-start.66 = (bf16[256,1536]{1,0:T(8,128)(2,1)}, bf16[256,1536]{1,0:T(8,128)(2,1)}, u32[]{:S(2)}, u32[]{:S(2)}) collective-permute-start(bf16[256,1536]{1,0:T(8,128)(2,1)} %get-tuple-element.479), channel_id=1, source_target_pairs={{0,16},{16,0},{1,17},{17,1},{2,18},{18,2},{3,19},{19,3},{4,20},{20... | collective-permute-start | bytes 2359304 | tf_op jit(solution)/shard_map/ppermute | solution.py:39
  499.6 47.0 %collective-permute-start.67 = (bf16[256,1536]{1,0:T(8,128)(2,1)}, bf16[256,1536]{1,0:T(8,128)(2,1)}, u32[]{:S(2)}, u32[]{:S(2)}) collective-permute-start(bf16[256,1536]{1,0:T(8,128)(2,1)} %add_convert_fusion.22), channel_id=1, source_target_pairs={{0,2},{2,4},{4,6},{6,0},{1,3},{3,5},{5,7},{7,1},{8,10},{10,12},{12... | collective-permute-start | bytes 2359304 | tf_op jit(solution)/shard_map/ppermute | solution.py:39
  499.7 46.9 %collective-permute-start.68 = (bf16[256,1536]{1,0:T(8,128)(2,1)S(1)}, bf16[256,1536]{1,0:T(8,128)(2,1)}, u32[]{:S(2)}, u32[]{:S(2)}) collective-permute-start(bf16[256,1536]{1,0:T(8,128)(2,1)S(1)} %copy-done.101), channel_id=1, source_target_pairs={{0,16},{16,0},{1,17},{17,1},{2,18},{18,2},{3,19},{19,3},{4,20},{20... | collective-permute-start | bytes 2359304 | tf_op jit(solution)/shard_map/ppermute | solution.py:39
  499.9 46.7 %collective-permute-start.69 = (bf16[2,256,1536]{2,1,0:T(8,128)(2,1)}, bf16[2,256,1536]{2,1,0:T(8,128)(2,1)}, u32[]{:S(2)}, u32[]{:S(2)}) collective-permute-start(bf16[2,256,1536]{2,1,0:T(8,128)(2,1)} %get-tuple-element.482), channel_id=1, source_target_pairs={{0,8},{8,0},{1,9},{9,1},{2,10},{10,2},{3,11},{11,3},{4,12},{12,4},... | collective-permute-start | bytes 4718600 | tf_op jit(solution)/shard_map/ppermute | solution.py:39
  501.2 44.3 %collective-permute-start.70 = (f32[4,256,40]{2,1,0:T(8,128)S(1)}, f32[4,256,40]{2,1,0:T(8,128)}, u32[]{:S(2)}, u32[]{:S(2)}) collective-permute-start(f32[4,256,40]{2,1,0:T(8,128)S(1)} %slice_bitcast_fusion.2), channel_id=1, source_target_pairs={{0,16},{16,0},{1,17},{17,1},{2,18},{18,2},{3,19},{19,3},{4,20},{20... | collective-permute-start | bytes 491528 | tf_op jit(solution)/shard_map/ppermute | solution.py:39
  559.2 40.9 %collective-permute-start.71 = (bf16[256,1536]{1,0:T(8,128)(2,1)}, bf16[256,1536]{1,0:T(8,128)(2,1)}, u32[]{:S(2)}, u32[]{:S(2)}) collective-permute-start(bf16[256,1536]{1,0:T(8,128)(2,1)} %add_convert_fusion.15), channel_id=1, source_target_pairs={{0,2},{2,4},{4,6},{6,0},{1,3},{3,5},{5,7},{7,1},{8,10},{10,12},{12... | collective-permute-start | bytes 2359304 | tf_op jit(solution)/shard_map/ppermute | solution.py:39
  560.4 39.7 %collective-permute-start.72 = (bf16[256,1536]{1,0:T(8,128)(2,1)}, bf16[256,1536]{1,0:T(8,128)(2,1)}, u32[]{:S(2)}, u32[]{:S(2)}) collective-permute-start(bf16[256,1536]{1,0:T(8,128)(2,1)} %add_convert_fusion.13), channel_id=1, source_target_pairs={{0,2},{2,4},{4,6},{6,0},{1,3},{3,5},{5,7},{7,1},{8,10},{10,12},{12... | collective-permute-start | bytes 2359304 | tf_op jit(solution)/shard_map/ppermute | solution.py:39
  561.5 38.5 %collective-permute-start.73 = (bf16[256,1536]{1,0:T(8,128)(2,1)S(1)}, bf16[256,1536]{1,0:T(8,128)(2,1)}, u32[]{:S(2)}, u32[]{:S(2)}) collective-permute-start(bf16[256,1536]{1,0:T(8,128)(2,1)S(1)} %copy-done.100), channel_id=1, source_target_pairs={{0,16},{16,0},{1,17},{17,1},{2,18},{18,2},{3,19},{19,3},{4,20},{20... | collective-permute-start | bytes 2359304 | tf_op jit(solution)/shard_map/ppermute | solution.py:39
  562.8 37.2 %collective-permute-start.77 = (bf16[2,192,1280]{2,1,0:T(8,128)(2,1)}, bf16[2,192,1280]{2,1,0:T(8,128)(2,1)S(1)}, u32[]{:S(2)}, u32[]{:S(2)}) collective-permute-start(bf16[2,192,1280]{2,1,0:T(8,128)(2,1)} %get-tuple-element.505), channel_id=1, source_target_pairs={{0,1},{1,0},{2,3},{3,2},{4,5},{5,4},{6,7},{7,6},{8,9},{9,8},{10,11... | collective-permute-start | bytes 2949128 | tf_op jit(solution)/shard_map/ppermute | solution.py:39
  564.1 34.7 %collective-permute-start.76 = (f32[256,40]{1,0:T(8,128)S(1)}, f32[256,40]{1,0:T(8,128)S(1)}, u32[]{:S(2)}, u32[]{:S(2)}) collective-permute-start(f32[256,40]{1,0:T(8,128)S(1)} %bitcast_add_fusion.3), channel_id=1, source_target_pairs={{0,2},{2,4},{4,6},{6,0},{1,3},{3,5},{5,7},{7,1},{8,10},{10,12},{12... | collective-permute-start | bytes 122888 | tf_op jit(solution)/shard_map/ppermute | solution.py:39
  598.7 30.8 %collective-permute-start.81 = (bf16[256,1536]{1,0:T(8,128)(2,1)}, bf16[256,1536]{1,0:T(8,128)(2,1)}, u32[]{:S(2)}, u32[]{:S(2)}) collective-permute-start(bf16[256,1536]{1,0:T(8,128)(2,1)} %get-tuple-element.517), channel_id=1, source_target_pairs={{0,16},{16,0},{1,17},{17,1},{2,18},{18,2},{3,19},{19,3},{4,20},{20... | collective-permute-start | bytes 2359304 | tf_op jit(solution)/shard_map/ppermute | solution.py:39
  651.1 27.5 %collective-permute-start.83 = (bf16[256,1536]{1,0:T(8,128)(2,1)S(1)}, bf16[256,1536]{1,0:T(8,128)(2,1)S(1)}, u32[]{:S(2)}, u32[]{:S(2)}) collective-permute-start(bf16[256,1536]{1,0:T(8,128)(2,1)S(1)} %add_convert_fusion.6), channel_id=1, source_target_pairs={{0,2},{2,4},{4,6},{6,0},{1,3},{3,5},{5,7},{7,1},{8,10},{10,12},{12... | collective-permute-start | bytes 2359304 | tf_op jit(solution)/shard_map/ppermute | solution.py:39
  656.6 57.7 %collective-permute-start.86 = (bf16[192,1280]{1,0:T(8,128)(2,1)}, bf16[192,1280]{1,0:T(8,128)(2,1)}, u32[]{:S(2)}, u32[]{:S(2)}) collective-permute-start(bf16[192,1280]{1,0:T(8,128)(2,1)} %get-tuple-element.712), channel_id=1, source_target_pairs={{0,2},{2,4},{4,6},{6,0},{1,3},{3,5},{5,7},{7,1},{8,10},{10,12},{12... | collective-permute-start | bytes 1474568 | tf_op jit(solution)/shard_map/ppermute | solution.py:792
  656.7 57.6 %collective-permute-start.87 = (bf16[192,1280]{1,0:T(8,128)(2,1)}, bf16[192,1280]{1,0:T(8,128)(2,1)}, u32[]{:S(2)}, u32[]{:S(2)}) collective-permute-start(bf16[192,1280]{1,0:T(8,128)(2,1)} %get-tuple-element.711), channel_id=1, source_target_pairs={{0,4},{2,6},{4,0},{6,2},{1,5},{3,7},{5,1},{7,3},{8,12},{10,14},{12... | collective-permute-start | bytes 1474568 | tf_op jit(solution)/shard_map/ppermute | solution.py:792
  677.3 37.0 %collective-permute-start.88 = (bf16[192,1280]{1,0:T(8,128)(2,1)}, bf16[192,1280]{1,0:T(8,128)(2,1)}, u32[]{:S(2)}, u32[]{:S(2)}) collective-permute-start(bf16[192,1280]{1,0:T(8,128)(2,1)} %get-tuple-element.710), channel_id=1, source_target_pairs={{0,6},{2,0},{4,2},{6,4},{1,7},{3,1},{5,3},{7,5},{8,14},{10,8},{12,... | collective-permute-start | bytes 1474568 | tf_op jit(solution)/shard_map/ppermute | solution.py:792
  724.9 42.0 %collective-permute-start.91 = (bf16[2,4,2,48,768]{4,3,2,1,0:T(8,128)(2,1)S(1)}, bf16[2,4,2,48,768]{4,3,2,1,0:T(8,128)(2,1)}, u32[]{:S(2)}, u32[]{:S(2)}) collective-permute-start(bf16[2,4,2,48,768]{4,3,2,1,0:T(8,128)(2,1)S(1)} %get-tuple-element.591), channel_id=1, source_target_pairs={{0,16},{16,0},{1,17},{17,1},{2,18},{18,2},{3,19},{19,3},{4,20},{20... | collective-permute-start | bytes 3538952 | tf_op jit(solution)/shard_map/ppermute | solution.py:39
  725.2 38.1 %collective-permute-start.92 = (bf16[2,4,2,48,640]{4,3,2,1,0:T(8,128)(2,1)}, bf16[2,4,2,48,640]{4,3,2,1,0:T(8,128)(2,1)}, u32[]{:S(2)}, u32[]{:S(2)}) collective-permute-start(bf16[2,4,2,48,640]{4,3,2,1,0:T(8,128)(2,1)} %get-tuple-element.593), channel_id=1, source_target_pairs={{0,1},{1,0},{2,3},{3,2},{4,5},{5,4},{6,7},{7,6},{8,9},{9,8},{10,11... | collective-permute-start | bytes 2949128 | tf_op jit(solution)/shard_map/ppermute | solution.py:39
  728.4 93.9 %collective-permute-start.104 = (bf16[192,1280]{1,0:T(8,128)(2,1)}, bf16[192,1280]{1,0:T(8,128)(2,1)S(1)}, u32[]{:S(2)}, u32[]{:S(2)}) collective-permute-start(bf16[192,1280]{1,0:T(8,128)(2,1)} %get-tuple-element.708), channel_id=1, source_target_pairs={{0,2},{2,4},{4,6},{6,0},{1,3},{3,5},{5,7},{7,1},{8,10},{10,12},{12... | collective-permute-start | bytes 1474568 | tf_op jit(solution)/shard_map/ppermute | solution.py:792
  728.4 93.9 %collective-permute-start.105 = (bf16[192,1280]{1,0:T(8,128)(2,1)}, bf16[192,1280]{1,0:T(8,128)(2,1)}, u32[]{:S(2)}, u32[]{:S(2)}) collective-permute-start(bf16[192,1280]{1,0:T(8,128)(2,1)} %get-tuple-element.707), channel_id=1, source_target_pairs={{0,4},{2,6},{4,0},{6,2},{1,5},{3,7},{5,1},{7,3},{8,12},{10,14},{12... | collective-permute-start | bytes 1474568 | tf_op jit(solution)/shard_map/ppermute | solution.py:792
  759.0 63.4 %collective-permute-start.106 = (bf16[192,1280]{1,0:T(8,128)(2,1)}, bf16[192,1280]{1,0:T(8,128)(2,1)S(1)}, u32[]{:S(2)}, u32[]{:S(2)}) collective-permute-start(bf16[192,1280]{1,0:T(8,128)(2,1)} %get-tuple-element.706), channel_id=1, source_target_pairs={{0,6},{2,0},{4,2},{6,4},{1,7},{3,1},{5,3},{7,5},{8,14},{10,8},{12,... | collective-permute-start | bytes 1474568 | tf_op jit(solution)/shard_map/ppermute | solution.py:792
  777.0 88.3 %collective-permute-start.108 = (bf16[10,64,1536]{2,1,0:T(8,128)(2,1)}, bf16[10,64,1536]{2,1,0:T(8,128)(2,1)}, u32[]{:S(2)}, u32[]{:S(2)}) collective-permute-start(bf16[10,64,1536]{2,1,0:T(8,128)(2,1)} %get-tuple-element.618), channel_id=1, source_target_pairs={{0,1},{1,0},{2,3},{3,2},{4,5},{5,4},{6,7},{7,6},{8,9},{9,8},{10,11... | collective-permute-start | bytes 5898248 | tf_op jit(solution)/shard_map/ppermute | solution.py:39
  823.3 37.1 %collective-permute-start.107 = (f32[48,1408]{1,0:T(8,128)S(1)}, f32[48,1408]{1,0:T(8,128)S(1)}, u32[]{:S(2)}, u32[]{:S(2)}) collective-permute-start(f32[48,1408]{1,0:T(8,128)S(1)} %dynamic-slice_bitcast_fusion), channel_id=1, source_target_pairs={{0,8},{8,0},{1,9},{9,1},{2,10},{10,2},{3,11},{11,3},{4,12},{12,4},... | collective-permute-start | bytes 811016 | tf_op jit(solution)/shard_map/ppermute | solution.py:39
  (226 other events, 2247.8 us)

commit v3 on v2

--- a/solution.py
+++ b/solution.py
@@ -7,6 +7,7 @@
 from jax import lax
 from jax.experimental import pallas as pl
 from jax.experimental.pallas import tpu as pltpu
+from jax.experimental.layout import Layout, with_layout_constraint
 from jax.sharding import Mesh, PartitionSpec as P
 
 MODEL_WIDTH = 1536
@@ -52,6 +53,15 @@
         total = ring_step(total, axis).astype(F32) + part.astype(F32)
         total = total.astype(kind if part is parts[0] else part.dtype)
     return total
+
+
+def direct_sum(parts, axis, kind):
+    size = lax.axis_size(axis)
+    total = parts[0].astype(F32)
+    for step in range(1, size):
+        to = [(i, (i - step) % size) for i in range(size)]
+        total = total + lax.ppermute(parts[step], axis, to).astype(F32)
+    return total.astype(kind)
 
 
 def index_at(axis, step):
@@ -94,7 +104,7 @@
         out_shape=shapes,
         scratch_shapes=[pltpu.VMEM(s.shape, s.dtype) for s in shapes]
         + [pltpu.SemaphoreType.DMA((len(moves) + len(shapes),))],
-        compiler_params=pltpu.CompilerParams(vmem_limit_bytes=VMEM_BYTES // 3),
+        compiler_params=pltpu.CompilerParams(vmem_limit_bytes=VMEM_BYTES),
         cost_estimate=pl.CostEstimate(flops=0, bytes_accessed=2 * total, transcendentals=0),
         name=name,
     )(jnp.stack(places).astype(jnp.int32), *sources)
@@ -125,24 +135,29 @@
     return [part.reshape(-1, part.shape[-1]) for part in whole]
 
 
-def pick_weights(grad, first, second, with_core):
+def pick_weights(grads, first, second, with_core):
     sizes = {axis: lax.axis_size(axis) for axis in ("y", "z", "x")}
     core = (2,) if with_core else ()
-    shape = (sizes["y"],) + core + (sizes["z"], sizes["x"], -1, grad.shape[-1])
-    grad = grad.reshape(shape)
     places, where = places_of(("y", "z", "x"))
-    moves = []
-    for y_step, z_step, x_step in itertools.product(
-        range(sizes["y"]), range(sizes["z"]), range(sizes["x"])
-    ):
-        spot = [where["y", y_step], where["z", z_step], where["x", x_step]]
-        if with_core:
-            spot.insert(1, slice(None))
-        steps = {"y": y_step, "x": x_step}
-        moves.append((0, tuple(spot), steps[second], (steps[first], z_step)))
-    tail = core + grad.shape[-2:]
-    shape = jax.ShapeDtypeStruct((sizes[first], sizes["z"]) + tail, grad.dtype)
-    return move(moves, places, [grad], [shape] * sizes[second], "pick_weights")
+    moves, sources, start = [], [], 0
+    for number, (grad, column, columns) in enumerate(grads):
+        shape = (sizes["y"],) + core + (sizes["z"], sizes["x"], -1, grad.shape[-1])
+        sources.append(grad.reshape(shape))
+        rows = slice(None)
+        for y_step, z_step, x_step in itertools.product(
+            range(sizes["y"]), range(sizes["z"]), range(sizes["x"])
+        ):
+            spot = [where["y", y_step], where["z", z_step], where["x", x_step]]
+            if with_core:
+                spot.insert(1, rows)
+            spot += [rows, pl.ds(column, columns)]
+            steps = {"y": y_step, "x": x_step}
+            to = (steps[first], z_step) + (rows,) * (1 + len(core)) + (pl.ds(start, columns),)
+            moves.append((number, tuple(spot), steps[second], to))
+        start = start + columns
+    tail = core + (sources[0].shape[-2], start)
+    shape = jax.ShapeDtypeStruct((sizes[first], sizes["z"]) + tail, sources[0].dtype)
+    return move(moves, places, sources, [shape] * sizes[second], "pick_weights")
 
 
 def sum_along(parts, axis, kind=BF16):
@@ -170,56 +185,45 @@
     )(w_gate, w_up)
 
 
-def unpack_kernel(counts, slices, place_ref, *refs):
-    parts, (gate_ref, up_ref) = refs[:-2], refs[-2:]
-    expert = pl.program_id(0)
+def unpack_kernel(part_ref, *refs):
+    gate_ref, up_ref = refs[-2:]
+    slices = part_ref.shape[0]
     width = gate_ref.shape[-1] // slices
-    first = 0
-    for which, count in enumerate(counts):
-
-        @pl.when((expert >= first) & (expert < first + count))
-        def _(which=which, first=first):
-            start = pl.multiple_of((expert - first) * 2 * width, 2 * width)
-            for step in range(slices):
-                both = parts[which * slices + step][:, pl.ds(start, 2 * width)].astype(F32)
-                spot = pl.multiple_of(place_ref[step] * width, width)
-                gate_ref[0, :, pl.ds(spot, width)] = both[:, :width]
-                up_ref[0, :, pl.ds(spot, width)] = both[:, width:]
-
-        first = first + count
-
-
-def unpack_experts(parts, counts):
-    places, _ = places_of(("z",))
-    slices, local_count = len(parts[0]), sum(counts)
-    rows, columns = parts[0][0].shape
-    hidden = columns // (2 * counts[0]) * slices
-    flat = [part for half in parts for part in half]
-    spec = pl.BlockSpec((1, rows, hidden), lambda e: (e, 0, 0))
-    whole = [pl.BlockSpec(part.shape, lambda e: (0, 0)) for part in flat]
-    shape = jax.ShapeDtypeStruct((local_count, rows, hidden), F32)
+    for z in range(slices):
+        both = part_ref[z].astype(F32)
+        gate_ref[0, :, z * width : (z + 1) * width] = both[:, :width]
+        up_ref[0, :, z * width : (z + 1) * width] = both[:, width:]
+
+
+def unpack_experts(part, first, last, local_count, earlier):
+    slices, rows, columns = part.shape
+    width = columns // (last - first)
+    spec = pl.BlockSpec((1, rows, width // 2 * slices), lambda e: (first + e, 0, 0))
+    shape = jax.ShapeDtypeStruct((local_count, rows, width // 2 * slices), F32)
+    anywhere = pl.BlockSpec(memory_space=pl.ANY)
     return pl.pallas_call(
-        functools.partial(unpack_kernel, counts, slices),
-        grid=(local_count,),
-        in_specs=[pl.BlockSpec(memory_space=pltpu.SMEM)] + whole,
+        unpack_kernel,
+        grid=(last - first,),
+        in_specs=[pl.BlockSpec((slices, rows, width), lambda e: (0, 0, e))]
+        + [anywhere] * len(earlier),
         out_specs=[spec, spec],
         out_shape=[shape, shape],
-        compiler_params=pltpu.CompilerParams(vmem_limit_bytes=VMEM_BYTES),
+        input_output_aliases={1 + i: i for i in range(len(earlier))},
         name="unpack_experts",
-    )(jnp.stack(places).astype(jnp.int32), *flat)
+    )(part, *earlier)
 
 
 def experts_kernel(counts, steps, x_size, place_ref, *refs):
     parts = len(counts)
     rows_in, grads_in, refs = refs[:steps], refs[steps : 2 * steps], refs[2 * steps :]
     w_in_parts, refs = [refs[i * x_size : (i + 1) * x_size] for i in range(parts)], refs[parts * x_size :]
-    w_back_parts, refs = [refs[i * x_size : (i + 1) * x_size] for i in range(parts)], refs[parts * x_size :]
+    w_back_parts, refs = refs[:x_size], refs[x_size:]
     results, grads, (active_ref, hidden_ref, gates_ref) = refs[:2], refs[2:4], refs[4:7]
     rows_buf, grads_buf = refs[7:9]
     w_in, w_back, sems = refs[9 : 9 + parts], refs[9 + parts], refs[10 + parts]
     step = pl.program_id(0)
     half = steps // 2
-    weights, late = [], [[] for _ in range(steps)]
+    weights, late = [[] for _ in counts], [[] for _ in range(steps)]
     number = 0
 
     def copy_of(source, target):
@@ -235,22 +239,21 @@
             size = source.shape[1]
             for z in range(source.shape[0]):
                 start = pl.multiple_of((z * x_size + place) * size, size)
-                weights.append(copy_of(source.at[z], w_in[part].at[pl.ds(start, size)]))
-            source = w_back_parts[part][x_step]
+                weights[part].append(copy_of(source.at[z], w_in[part].at[pl.ds(start, size)]))
+            source = w_back_parts[x_step]
             size = source.shape[1]
-            for e in range(count):
-                start = pl.multiple_of(((first + e) * x_size + place) * size, size)
-                weights.append(copy_of(source.at[e], w_back.at[pl.ds(start, size)]))
+            for e in range(first, first + count):
+                start = pl.multiple_of((e * x_size + place) * size, size)
+                weights[part].append(copy_of(source.at[e], w_back.at[pl.ds(start, size)]))
         first = first + count
     for i in range(steps):
         late[i] = [copy_of(rows_in[i], rows_buf.at[i]), copy_of(grads_in[i], grads_buf.at[i])]
 
     @pl.when(step == 0)
     def _():
-        for copy in late[0] + weights + [copy for some in late[1:] for copy in some]:
-            copy.start()
-        for copy in weights:
-            copy.wait()
+        for some in late[:1] + weights + late[1:]:
+            for copy in some:
+                copy.start()
 
     for i in range(steps):
 
@@ -272,6 +275,12 @@
     grad_gates = jnp.zeros(gates.shape, F32)
     expert = 0
     for part, count in enumerate(counts):
+
+        @pl.when(step == 0)
+        def _(part=part):
+            for copy in weights[part]:
+                copy.wait()
+
         for i in range(count):
             here = slice(expert * width, (expert + 1) * width)
             hidden = dot(rows, w_in[part][:, 2 * width * i : 2 * width * (i + 1)])
@@ -282,7 +291,7 @@
             active = silu * up_part
             weight = gates[:, expert : expert + 1]
             total = jnp.sum(active * grad_plain, axis=1, keepdims=True)
-            grad_gates = jnp.where(lane == expert, total, grad_gates)
+            grad_gates = jnp.where(lane == first + expert, total, grad_gates)
             active_ref[:, here] = (weight * active).astype(BF16)
             grad_active = weight * grad_plain
             start = 2 * width * expert
@@ -291,7 +300,7 @@
             ).astype(BF16)
             hidden_ref[:, start + width : start + 2 * width] = (grad_active * silu).astype(BF16)
             expert = expert + 1
-    gates_ref[...] = grad_gates
+    gates_ref[0] = grad_gates.T[:E]
     result = dot(active_ref[...], w_back[...]).astype(BF16)
     grad_in = jnp.zeros(rows.shape, F32)
     start = 0
@@ -332,14 +341,15 @@
         functools.partial(experts_kernel, counts, steps, x_size),
         grid=(steps,),
         in_specs=[pl.BlockSpec(memory_space=pltpu.SMEM)]
-        + [anywhere] * (2 * steps + 2 * len(counts) * x_size),
+        + [anywhere] * (2 * steps + (len(counts) + 1) * x_size),
         out_specs=[own, other, own, other]
-        + [by_row(local_count * width), by_row(2 * local_count * width), by_row(LANES)],
+        + [by_row(local_count * width), by_row(2 * local_count * width)]
+        + [pl.BlockSpec((1, E, count), lambda i: (i, 0, 0))],
         out_shape=[side] * 4
         + [
             jax.ShapeDtypeStruct((steps * count, local_count * width), BF16),
             jax.ShapeDtypeStruct((steps * count, 2 * local_count * width), BF16),
-            jax.ShapeDtypeStruct((steps * count, LANES), F32),
+            jax.ShapeDtypeStruct((steps, E, count), F32),
         ],
         scratch_shapes=[
             pltpu.VMEM((steps, count, wide), BF16),
@@ -360,7 +370,7 @@
         *rows,
         *grads,
         *[part for parts in w_in_parts for part in parts],
-        *[part for parts in w_back_parts for part in parts],
+        *w_back_parts,
     )
 
 
@@ -397,20 +407,23 @@
         else:
             total[...] += term
     blocks, own = outs[0].shape[0], outs[0].shape[1]
-    for step, out in enumerate(outs):
+    devices = len(outs) if back else len(outs) // 2
+    for number, out in enumerate(outs):
+        step, half = (number, 0) if back else (number // 2, number % 2)
         for i in range(blocks):
-            block = i if back else place_ref[len(outs) + (blocks - i) % blocks]
-            start = pl.multiple_of((block * len(outs) + place_ref[step]) * own, own)
+            block = half * blocks + i
+            start = pl.multiple_of((block * devices + place_ref[step]) * own, own)
             out[i] = total[pl.ds(start, own), :].astype(BF16)
 
 
 def expert_grads(whole, columns, first, last, width, back):
     x_size = lax.axis_size("x")
-    places, _ = places_of(("x",) if back else ("x", "z"))
+    places, _ = places_of(("x",))
     tokens = len(whole) * whole[0].shape[0]
     experts = last - first
     anywhere = pl.BlockSpec(memory_space=pl.ANY)
     column = pl.BlockSpec((columns[0].shape[0], width), lambda e: (0, first + e))
+    outs = x_size if back else 2 * x_size
     if back:
         own = width // x_size
         block = (1, own, MODEL_WIDTH)
@@ -420,8 +433,8 @@
     else:
         z_size = lax.axis_size("z")
         own = MODEL_WIDTH // (z_size * x_size)
-        shape = (z_size, own, experts * width)
-        out = pl.BlockSpec((z_size, own, width), lambda e: (0, 0, e))
+        shape = (z_size // 2, own, experts * width)
+        out = pl.BlockSpec((z_size // 2, own, width), lambda e: (0, 0, e))
         total = (MODEL_WIDTH, width)
     return pl.pallas_call(
         functools.partial(expert_grads_kernel, len(whole), len(columns), back),
@@ -429,8 +442,8 @@
         in_specs=[pl.BlockSpec(memory_space=pltpu.SMEM)]
         + [anywhere] * len(whole)
         + [column] * len(columns),
-        out_specs=[out] * x_size,
-        out_shape=[jax.ShapeDtypeStruct(shape, BF16)] * x_size,
+        out_specs=[out] * outs,
+        out_shape=[jax.ShapeDtypeStruct(shape, BF16)] * outs,
         scratch_shapes=[
             pltpu.VMEM((tokens, MODEL_WIDTH), BF16),
             pltpu.VMEM(total, F32),
@@ -523,7 +536,9 @@
         return mine, theirs
 
     mine, theirs = both_cores([w_query, key_projection_weight, value_projection_weight])
-    got = ring_step(jnp.concatenate([theirs, small], axis=1), "c")
+    got, other_lengths = sync(
+        ring_step(jnp.concatenate([theirs, small], axis=1), "c"), ring_step(lengths, "c")
+    )
     mine = jnp.concatenate([mine, small], axis=1)
     both = jnp.where(core == 0, jnp.stack([mine, got]), jnp.stack([got, mine]))
     both = jnp.concatenate(
@@ -537,15 +552,11 @@
     )
     counts = [local_count // 2, local_count - local_count // 2]
     ranges = [(0, counts[0]), (counts[0], local_count)]
-    packed = [pack_experts(w_gate, w_up, first, last, z_size) for first, last in ranges]
     grad_final_low = cotangent.reshape(count, MODEL_WIDTH)
     grads_z = [grad_final_low]
-    down = [w_down[first:last] for first, last in ranges]
-    both, grads_ahead, grads_first = sync(
-        both, ring_step(grad_final_low, "z"), ring_gather(grad_final_low, "y")
-    )
-    grads_z.append(grads_ahead)
-    grads_y = [grads_first]
+    grads_ahead = ring_step(grad_final_low, "z")
+    grads_y = [ring_gather(grad_final_low, "y")]
+    down_parts = ring_gather(w_down, "x")
     pair = z_size // 2
     first_width = q_width + kv_width + LANES
     first_blocks, second_blocks = {}, {}
@@ -565,29 +576,28 @@
     z_blocks = [both]
     for _ in range(pair - 1):
         z_blocks.append(ring_step(z_blocks[-1], "z"))
-    others = [ring_step(inputs, "c"), ring_step(lengths, "c")]
-    z_blocks, others, packed, grads_second, first_down = sync(
-        z_blocks, others, packed, ring_gather(grads_z[1], "y"), ring_gather(down[0], "x")
-    )
-    other_inputs, other_lengths = others
-    grads_y.append(grads_second)
-    hops, ahead, grads_ahead, grads_other = sync(
-        first_hops(z_blocks),
-        ring_step(z_blocks[-1], "z"),
-        ring_step(grads_z[1], "z"),
-        [[ring_step(part, "c") for part in some] for some in grads_y],
-    )
+    others = ring_step(inputs, "c")
+    packed = [pack_experts(w_gate, w_up, first, last, z_size) for first, last in ranges]
+    z_blocks, others, grads_ahead, grads_y, packed = sync(
+        z_blocks, others, grads_ahead, grads_y, packed
+    )
+    other_inputs = others
     grads_z.append(grads_ahead)
+    ahead = []
+    for _ in range(pair):
+        ahead.append(ring_step((z_blocks + ahead)[-1], "z"))
+    hops, ahead, down_parts, packed = sync(first_hops(z_blocks), ahead, down_parts, packed)
+    swapped = lax.all_to_all(packed[0], "z", 0, 0, tiled=True)
     second_hops(*hops, 0)
-    z_blocks = [ahead]
-    for _ in range(pair - 1):
-        z_blocks.append(ring_step(z_blocks[-1], "z"))
-    first_blocks, second_blocks, z_blocks, packed = sync(
-        first_blocks, second_blocks, z_blocks, packed
-    )
-    swapped = lax.all_to_all(packed[0], "z", 0, 0, tiled=True)
-    (hops,) = sync(first_hops(z_blocks))
+    first_blocks, second_blocks, ahead = sync(first_blocks, second_blocks, ahead)
+    hops, grads_z = sync(first_hops(ahead), grads_z)
     second_hops(*hops, pair)
+    first_blocks, second_blocks, swapped, packed, grads_z = sync(
+        first_blocks, second_blocks, swapped, packed, grads_z
+    )
+    grads_y.append(ring_gather(grads_z[1], "y"))
+    first_parts = ring_gather(swapped, "x")
+    swapped = lax.all_to_all(packed[1], "z", 0, 0, tiled=True)
     w_first, w_second = place_weights([first_blocks, second_blocks])
     w_qk = w_first[:, : q_width + kv_width]
     small = w_first[:, q_width + kv_width :]
@@ -608,12 +618,7 @@
     blocks = 2 * micro
     qk_pre = dot(normalized_input, w_qk)
     values = dot(normalized_input, w_v).astype(BF16)
-    qk_pre, values, swapped, packed, grads_z, down = sync(
-        qk_pre, values, swapped, packed, grads_z, down
-    )
-    first_parts = ring_gather(swapped, "x")
-    swapped = lax.all_to_all(packed[1], "z", 0, 0, tiled=True)
-    grads_third = ring_gather(grads_z[2], "y")
+    qk_pre, values, grads_y = sync(qk_pre, values, grads_y)
     query_pre = qk_pre[:, :q_width]
     query_pre = query_pre.reshape(blocks, block, kv_heads * QUERY_PER_GROUP, HEAD_SIZE)
     key_pre = qk_pre[:, q_width:].reshape(blocks, block, kv_heads, HEAD_SIZE)
@@ -625,16 +630,17 @@
     allowed = (segment[:, :, None] == segment[:, None, :]) & (
         token_index[:, None] >= token_index[None, :]
     )
+    query, keys, first_parts, swapped, grads_z = sync(query, keys, first_parts, swapped, grads_z)
+    second_parts = ring_gather(swapped, "x")
+    grads_ahead = ring_step(grads_z[1], "z")
     scores = jnp.einsum("bqkgd,bskd->bkgqs", query, keys, preferred_element_type=F32)
     scores = jnp.where(allowed[:, None, None], scores * score_scale, -1000000000.0)
     probs = jax.nn.softmax(scores, axis=-1)
     probs_low = probs.astype(BF16)
     mixed = jnp.einsum("bkgqs,bskd->bqkgd", probs_low, values, preferred_element_type=F32)
     mixed = mixed.reshape(2 * count, q_width).astype(BF16)
-    mixed, first_parts, swapped, grads_third = sync(mixed, first_parts, swapped, grads_third)
-    grads_y.append(grads_third)
-    second_parts = ring_gather(swapped, "x")
-    grads_ahead = ring_step(grads_z[2], "z")
+    grads_other = [[ring_step(part, "c") for part in some] for some in grads_y]
+    mixed, grads_other = sync(mixed, grads_other)
     projected = dot(mixed, w_out)
     own_act = act_rows[:count]
     resid = own_act + ring_sum([projected[:count], projected[count:]], "c", F32)
@@ -652,18 +658,17 @@
     low = gates - high
     spare = jnp.zeros((count, LANES - 2 * E), BF16)
     sent = jnp.concatenate([normed_two, high.astype(BF16), low.astype(BF16), spare], axis=1)
-    sent, grads_ahead, down = sync(sent, grads_ahead, down)
+    sent, grads_ahead = sync(sent, grads_ahead)
     grads_z.append(grads_ahead)
-    rows, ahead, second_parts, second_down, others, grads_third = sync(
+    rows, ahead, second_parts, others, grads_third = sync(
         ring_gather(sent, "y"),
         ring_step(sent, "z"),
         second_parts,
-        ring_gather(down[1], "x"),
         ring_step(sent, "c"),
-        [ring_step(part, "c") for part in grads_y[2]],
-    )
-    grads_other.append(grads_third)
-    w_in_parts, w_back_parts = [first_parts, second_parts], [first_down, second_down]
+        ring_step(grads_z[2], "c"),
+    )
+    grads_other.append([grads_third])
+    w_in_parts, w_back_parts = [first_parts, second_parts], down_parts
     rows, others = sync(rows, [others] + [ring_step(part, "c") for part in rows[1:]])
     width = w_in_parts[0][0].shape[-1] // (2 * counts[0])
 
@@ -680,7 +685,7 @@
         return plus(arrived, parts[0]) if y_size == 2 else arrived
 
     sent_chunks, grad_chunks, weighted, grad_hidden, grads_gates = [], [], [], [], []
-    results_c, grads_c, results_sum, grads_sum = [], [], [], []
+    results_c, grads_c, results_sum, grads_sum = [], [], {}, {}
     for z_step in range(z_size):
         sent_chunks += rows + others
         grad_chunks += grads_y[z_step] + grads_other[z_step]
@@ -695,46 +700,52 @@
         moved = {}
         if z_step + 1 < z_size:
             moved["rows"] = ring_gather(ahead, "y")
-            moved["others"] = ring_step(ahead, "c")
         if z_step + 2 < z_size:
             moved["ahead"] = ring_step(ahead, "z")
+        if z_step <= 1:
+            moved["grads"] = ring_gather(grads_z[2 + z_step], "y")
         if z_step == 0:
-            moved["grads"] = ring_gather(grads_z[3], "y")
+            moved["grads_z"] = ring_step(grads_z[2], "z")
         if z_step == 1:
+            moved["grads_other"] = [ring_step(part, "c") for part in grads_y[2][1:]]
+        if z_step == 2:
             moved["grads_other"] = [ring_step(part, "c") for part in grads_y[3]]
+        if z_step >= 2:
+            moved["grad"] = hops_y(grads_c[z_step - 1])
         if z_step >= 1:
-            moved["grad"] = hops_y(grads_c[-1])
             moved["result"] = ring_step(last_results[1], "c")
         if z_step == 3:
             moved["step"] = ring_step(grads_sum[1], "z")
-            moved["result_y"] = hops_y(results_c[0])
+            moved["grad_zero"] = hops_y(grads_c[0])
+            moved["result_one"] = hops_y(results_c[1])
         parts, moved = sync(parts, moved)
         weighted.append(parts[4])
         grad_hidden.append(parts[5])
-        grads_gates.append(parts[6][:, :local_count])
+        grads_gates.append(parts[6])
+        if z_step <= 1:
+            grads_y.append(moved["grads"])
         if z_step == 0:
-            grads_y.append(moved["grads"])
+            grads_z.append(moved["grads_z"])
         if z_step == 1:
+            grads_other[2] += moved["grads_other"]
+        if z_step == 2:
             grads_other.append(moved["grads_other"])
         arrived = ring_step(parts[3], "c")
         if z_step + 1 < z_size:
             ahead, rows = moved.get("ahead"), moved["rows"]
-            others = [ring_step(part, "c") for part in rows[1:]]
+            others = [ring_step(part, "c") for part in rows]
         arrived, others, rows = sync(arrived, others, rows)
-        others = [moved.get("others")] + others
         if z_step >= 1:
-            grads_sum.append(end_y(grads_c[-1], moved["grad"]))
             results_c.append(plus_all(moved["result"], last_results[0]))
+        if z_step >= 2:
+            grads_sum[z_step - 1] = end_y(grads_c[z_step - 1], moved["grad"])
         grads_c.append(plus_all(arrived, parts[2]))
         last_results = parts[:2]
 
     total = plus(moved["step"], grads_sum[2])
-    results_sum.append(end_y(results_c[0], moved["result_y"]))
-    spread = jnp.stack(grads_gates)
-    spread = lax.dynamic_update_slice(
-        jnp.zeros(spread.shape[:2] + (E,), F32), spread, (0, 0, group * local_count)
-    )
-    spread = spread.reshape(z_size, 2, y_size, count, E)
+    grads_sum[0] = end_y(grads_c[0], moved["grad_zero"])
+    results_sum[1] = end_y(results_c[1], moved["result_one"])
+    spread = jnp.stack(grads_gates).reshape(z_size, 2, y_size, E, count)
     spread = ring_sum([spread[:, 0], spread[:, 1]], "c", F32)
 
     def in_grads(which):
@@ -745,38 +756,38 @@
         middle = part.shape[0] // 2
         return part[:middle], part[middle:]
 
-    grads_c, total, results_c, last_results, spread, grad_hidden = sync(
-        grads_c, total, results_c, last_results, spread, grad_hidden
-    )
-    first_grads, last_grad, step, result_two, result_three, spread = sync(
+    grads_c, total, results_c, results_sum, last_results, spread, grad_hidden = sync(
+        grads_c, total, results_c, results_sum, last_results, spread, grad_hidden
+    )
+    first_grads, last_grad, step, result_three, spread = sync(
         in_grads(0),
         hops_y(grads_c[3]),
         ring_step(total, "z"),
-        hops_y(results_c[1]),
         ring_step(last_results[1], "c"),
         ring_sum([spread[:, i] for i in range(y_size)], "y", F32),
     )
     total = plus(step, end_y(grads_c[3], last_grad))
-    results_sum.append(end_y(results_c[1], result_two))
-    results_c.append(plus_all(result_three, last_results[0]))
-    one, two = halves(first_grads[1])
-    grad_hidden, total, results_sum, results_c, one, two = sync(
-        grad_hidden, total, results_sum, results_c, one, two
-    )
-    second_grads, step, result_step, result_two, grad_gates, one = sync(
+    grad_hidden, total, results_sum, results_c, first_grads, result_three = sync(
+        grad_hidden, total, results_sum, results_c, first_grads, result_three
+    )
+    second_grads, step, result_two, grad_gates, one = sync(
         in_grads(1),
         ring_step(total, "z"),
-        ring_step(results_sum[1], "z"),
         hops_y(results_c[2]),
         ring_sum([spread[i] for i in range(z_size)], "z", F32),
-        ring_step(one, "x"),
-    )
+        ring_step(first_grads[2], "x"),
+    )
+    grad_gates = with_layout_constraint(grad_gates, Layout((0, 1))).T
     grad_experts = plus(step, grads_sum[0], F32)
-    results_sum.append(end_y(results_c[2], result_two))
-    result_total = plus(result_step, results_sum[2])
-    result_total, grad_experts, two = sync(result_total, grad_experts, two)
+    grad_experts, first_grads, second_grads, results_c, results_sum, result_two, result_three = sync(
+        grad_experts, first_grads, second_grads, results_c, results_sum, result_two, result_three
+    )
+    two = ring_step(first_grads[3], "x")
+    second_one = ring_step(second_grads[2], "x")
+    result_step = ring_step(results_sum[1], "z")
+    results_sum[2] = end_y(results_c[2], result_two)
+    results_c.append(plus_all(result_three, last_results[0]))
     result_three = hops_y(results_c[3])
-    two = ring_step(two, "x")
 
     def finish_x(parts, arrived, kind):
         rest = list(parts[2:]) + [parts[0]]
@@ -785,12 +796,8 @@
             total = plus(ring_step(total, "x"), part, kind)
         return total
 
-    def shift_pieces(total):
-        pieces = [total[0]]
-        for step in range(1, z_size):
-            to = [(i, (i + step) % z_size) for i in range(z_size)]
-            pieces.append(lax.ppermute(total[step], "z", to))
-        return pieces
+    def finish_in(parts, one, two):
+        return jnp.concatenate([finish_x(parts[0::2], one, BF16), finish_x(parts[1::2], two, BF16)])
 
     grad_picked = chosen * (grad_gates - jnp.sum(grad_gates * gates, axis=-1, keepdims=True))
     grad_chance = grad_picked / picked_total
@@ -806,20 +813,21 @@
     grad_att = jnp.concatenate([grad_att, ring_step(grad_att, "c")])
     grad_w_out = dot(mixed, grad_att, ((0,), (0,))).astype(BF16)
     grad_mixed = dot(grad_att, w_out, ((1,), (1,))).astype(BF16).reshape(query.shape)
-    grad_mixed, grad_w_out, two, result_step, result_three = sync(
-        grad_mixed, grad_w_out, two, ring_step(result_total, "z"), result_three
-    )
-    first_x = jnp.concatenate([one, two])
-    result_total = plus(result_step, end_y(results_c[3], result_three))
-    out_parts = pick_weights(grad_w_out, "x", "y", False)
-    one, two = halves(second_grads[1])
-    first_sum, out_parts, grad_mixed, one, two, result_total = sync(
-        finish_x(first_grads, first_x, BF16), out_parts, grad_mixed, one, two, result_total
-    )
-    first_pieces = shift_pieces(first_sum)
-    one = ring_step(one, "x")
+    grad_mixed, grad_w_out, two, result_step, result_three, second_grads, results_c = sync(
+        grad_mixed, grad_w_out, two, result_step, result_three, second_grads, results_c
+    )
+    first_sum = finish_in(first_grads, one, two)
+    result_total = plus(result_step, results_sum[2])
+    results_sum[3] = end_y(results_c[3], result_three)
+    out_parts = pick_weights([(grad_w_out, 0, MODEL_WIDTH)], "x", "y", False)
+    first_sum, out_parts, grad_mixed, result_total, second_grads = sync(
+        first_sum, out_parts, grad_mixed, result_total, second_grads
+    )
+    first_pieces = lax.all_to_all(first_sum, "z", 0, 0, tiled=True)
+    second_two = ring_step(second_grads[3], "x")
+    out_sum = ring_sum(out_parts, "y", BF16)
     result_step = ring_step(result_total, "z")
-    out_sum = ring_sum(out_parts, "y", BF16)
+    result_zero = hops_y(results_c[0])
     grad_probs = jnp.einsum("bqkgd,bskd->bkgqs", grad_mixed, values, preferred_element_type=F32)
     grad_value_pre = jnp.einsum(
         "bkgqs,bqkgd->bskd", probs_low, grad_mixed, preferred_element_type=F32
@@ -837,17 +845,25 @@
     grad_key_pre = rotary_embedding(grad_keys * score_scale, token_position, -1.0)
     grad_key_pre = grad_key_pre.reshape(2 * count, kv_width).astype(BF16)
     grad_qk_pre = jnp.concatenate([grad_query_pre, grad_key_pre], axis=1)
-    grad_qk_pre, grad_value_pre, out_sum, result_step, one, two = sync(
-        grad_qk_pre, grad_value_pre, out_sum, result_step, one, two
-    )
-    outputs = resid + plus(result_step, results_sum[0], F32)
-    two = ring_step(two, "x")
+    grad_qk_pre, grad_value_pre, second_one, out_sum = sync(
+        grad_qk_pre, grad_value_pre, second_one, out_sum
+    )
     out_sum = sum_along(out_sum, "x")
     grad_w_qk = dot(normalized_input, grad_qk_pre, ((0,), (0,))).astype(BF16)
     grad_w_v = dot(normalized_input, grad_value_pre, ((0,), (0,))).astype(BF16)
     grad_normed = dot(grad_qk_pre, w_qk, ((1,), (1,)))
     grad_normed = grad_normed + dot(grad_value_pre, w_v, ((1,), (1,)))
-    grad_normed = ring_sum([grad_normed[:count], grad_normed[count:]], "c", F32)
+    grad_normed, other_normed, second_two, grad_w_qk, grad_w_v, result_step = sync(
+        grad_normed[:count],
+        ring_step(grad_normed[count:], "c"),
+        second_two,
+        grad_w_qk,
+        grad_w_v,
+        result_step,
+    )
+    result_step = ring_step(plus(result_step, results_sum[3]), "z")
+    second_sum = finish_in(second_grads, second_one, second_two)
+    grad_normed = grad_normed + other_normed
     grad_rows, grad_gain_one = norm_back(grad_normed, own_act, r_one[:count], gain_first)
     grad_rows = grad_resid + grad_rows
 
@@ -855,33 +871,41 @@
         [grad_w_router, grad_gain_one[:, None], grad_gain_two[:, None]], axis=1
     )
     grad_small = jnp.pad(grad_small, ((0, 0), (0, LANES - grad_small.shape[1])))
-    grad_vs = jnp.concatenate([grad_w_v, grad_small.astype(BF16)], axis=1)
-    q_parts = pick_weights(grad_w_qk[:, :q_width], "x", "y", True)
-    rest_parts = pick_weights(
-        jnp.concatenate([grad_w_qk[:, q_width:], grad_vs], axis=1), "y", "x", True
-    )
-    q_parts, rest_parts, grad_rows, grad_chunks, first_pieces, out_sum, two = sync(
-        q_parts, rest_parts, grad_rows, grad_chunks, first_pieces, out_sum, two
-    )
-    second_sum = finish_x(second_grads, jnp.concatenate([one, two]), BF16)
-    second_sum, q_parts, rest_parts, grad_chunks = sync(
-        second_sum, q_parts, rest_parts, grad_chunks
-    )
-    second_pieces = shift_pieces(second_sum)
-    out_sum = sum_along(out_sum, "z", F32)
+    q_parts = pick_weights([(grad_w_qk, 0, q_width)], "x", "y", True)
+    rest = [
+        (grad_w_qk, q_width, kv_width),
+        (grad_w_v, 0, kv_width),
+        (grad_small.astype(BF16), 0, LANES),
+    ]
+    rest_parts = pick_weights(rest, "y", "x", True)
+    q_parts, rest_parts, grad_rows, grad_chunks, out_sum, result_zero, first_pieces, second_sum = sync(
+        q_parts, rest_parts, grad_rows, grad_chunks, out_sum, result_zero, first_pieces, second_sum
+    )
+    second_pieces = lax.all_to_all(second_sum, "z", 0, 0, tiled=True)
     grad_w_back, q_sum, rest_sum = sync(
         expert_grads(grad_chunks, weighted, 0, local_count, width, True),
         ring_sum(q_parts, "y", BF16),
         ring_sum(rest_parts, "x", BF16),
     )
     back_x = ring_step(grad_w_back[1], "x")
-    q_sum, rest_sum, grad_w_out = sync(
-        sum_along(q_sum, "x"), sum_along(rest_sum, "y"), out_sum
-    )
-    grad_first, grad_second, first_pieces, second_pieces = sync(
-        sum_along(q_sum, "z", F32), sum_along(rest_sum, "z", F32), first_pieces, second_pieces
-    )
-    grad_w_gate, grad_w_up = unpack_experts([first_pieces, second_pieces], counts)
+    q_sum, rest_sum, out_sum, first_pieces, second_pieces, result_step = sync(
+        sum_along(q_sum, "x"),
+        sum_along(rest_sum, "y"),
+        out_sum,
+        first_pieces,
+        second_pieces,
+        result_step,
+    )
+    grad_gate_up = unpack_experts(first_pieces, *ranges[0], local_count, [])
+    outputs = resid + plus(result_step, end_y(results_c[0], result_zero), F32)
+    grad_first, grad_second, grad_w_out, grad_gate_up, outputs = sync(
+        *[sum_along(part, "z", F32) for part in (q_sum, rest_sum, out_sum)],
+        grad_gate_up,
+        outputs,
+    )
+    grad_w_gate, grad_w_up = unpack_experts(
+        second_pieces, *ranges[1], local_count, list(grad_gate_up)
+    )
     grad_w_down = finish_x(grad_w_back, back_x, F32)
     grad_both = jnp.concatenate([grad_first, grad_second], axis=-1)
     mine = lax.dynamic_index_in_dim(grad_both, core, 0, keepdims=False)

time: 879 us -> 758 us (0.86)
  waiting for transfers between devices: 252 us -> 177 us
  local copies, waits for them, and re-layouts: 95.6 us -> 75.1 us
  starting transfers between devices: 130 us -> 110 us
    ppermute x103 -> x102, waiting for transfers between devices: 247 us -> 168 us  [ring_step(): return lax.ppermute(array, axis, [(i, (i + 1) % size) for i in range(size)])]
    ppermute x103 -> x102, starting transfers between devices: 110 us -> 92.7 us  [ring_step(): return lax.ppermute(array, axis, [(i, (i + 1) % size) for i in range(size)])]
    ppermute x6 -> x0, starting transfers between devices: 10.3 us -> none  [shift_pieces(): pieces.append(lax.ppermute(total[step], 'z', to))]
    all_to_all x0 -> x2, waiting for transfers between devices: none -> 9.3 us  [the longest x1 9.29 us: body(): second_pieces = lax.all_to_all(second_sum, 'z', 0, 0, tiled=True)]
    unnamed x343 -> x257, local copies, waits for them, and re-layouts: 36.5 us -> 28 us
    convert_element_type x17 -> x18, other arithmetic: 39.8 us -> 36.3 us  [plus(): return (first.astype(F32) + second.astype(F32)).astype(kind)]
  transfers between devices with their start and end apart: 111 -> 106, of which waited for: 36 -> 32; matrix products, arithmetic and copies ran while one was open for 19% -> 21% of each run, Pallas kernels for 30% -> 36%
where the time goes in v3:
time: 758 us; the launch traced here: 751 us
  Pallas kernels  269 us (35%)
  waiting for transfers between devices  177 us (23%)
  starting transfers between devices  110 us (15%)
  other arithmetic  88.2 us (12%)
  local copies, waits for them, and re-layouts  75.1 us (10%)
  matrix products  28.2 us (4%)
    ppermute x102, waiting for transfers between devices, ring_step(): return lax.ppermute(array, axis, [(i, (i + 1) % size) for i in range(size)])  168 us
    pallas_call x4, Pallas kernels, run_experts(): pl.pallas_call(functools.partial(experts_kernel, counts, steps, x_size),...  156 us
    ppermute x102, starting transfers between devices, ring_step(): return lax.ppermute(array, axis, [(i, (i + 1) % size) for i in range(size)])  92.7 us
    pallas_call x3, Pallas kernels, expert_grads(): pl.pallas_call(functools.partial(expert_grads_kernel, len(whole), len(col...  77.3 us
    convert_element_type x18, other arithmetic, plus(): return (first.astype(F32) + second.astype(F32)).astype(kind)  36.3 us
    unnamed x257, local copies, waits for them, and re-layouts  28 us
    dot_general x12, matrix products, dot(): lax.dot_general(left, right, (dims, ((), ())), preferred_element_type=F32)  24.3 us
    pallas_call x4, Pallas kernels, move(): pl.pallas_call(functools.partial(move_kernel, moves, len(sources), len(sh...  17.1 us
  transfers between devices with their start and end apart: 106, of which 32 were waited for; matrix products, arithmetic and copies ran while one was open for 21% of the time, Pallas kernels for 36%

profile of v3, /device:TPU:1, one launch (start us, length us, event | category | flops | bytes accessed | tf_op | source)
XLA Modules:
  0.0 750.8 jit_solution(3333048043600703009)
XLA Ops:
  15.8 4.5 pack_experts.2
  20.3 4.5 pack_experts.3
  24.8 6.5 collective-permute-done.2
  32.5 10.6 %collective-permute-done.8 = bf16[2,48,2176]{2,1,0:T(8,128)(2,1)S(1)} collective-permute-done((bf16[2,48,2176]{2,1,0:T(8,128)(2,1)S(1)}, bf16[2,48,2176]{2,1,0:T(8,128)(2,1)S(1)}, u32[]{:S(2)}, u32[]{:S(2)}) %collective-permute-start.8) | collective-permute-done | bytes 417824 | tf_op jit(solution)/shard_map/ppermute | solution.py:40
  44.9 7.8 %collective-permute-done.7.refs_12_ = bf16[2,2,48,1024]{3,2,1,0:T(8,128)(2,1)S(1)} collective-permute-done((bf16[2,2,48,1024]{3,2,1,0:T(8,128)(2,1)S(1)}, bf16[2,2,48,1024]{3,2,1,0:T(8,128)(2,1)S(1)}, u32[]{:S(2)}, u32[]{:S(2)}) %collective-permute-start.7) | collective-permute-done | bytes 393248 | tf_op jit(solution)/shard_map/ppermute | solution.py:40
  52.7 13.2 %collective-permute-done.6.refs_1_ = bf16[2,2,48,1152]{3,2,1,0:T(8,128)(2,1)S(1)} collective-permute-done((bf16[2,2,48,1152]{3,2,1,0:T(8,128)(2,1)S(1)}, bf16[2,2,48,1152]{3,2,1,0:T(8,128)(2,1)S(1)}, u32[]{:S(2)}, u32[]{:S(2)}) %collective-permute-start.6) | collective-permute-done | bytes 442400 | tf_op jit(solution)/shard_map/ppermute | solution.py:40
  66.7 4.5 all-to-all-start
  75.6 7.2 collective-permute-done.13.refs_9_
  82.8 8.4 %collective-permute-done.14.refs_13_ = bf16[2,2,48,1024]{3,2,1,0:T(8,128)(2,1)} collective-permute-done((bf16[2,2,48,1024]{3,2,1,0:T(8,128)(2,1)}, bf16[2,2,48,1024]{3,2,1,0:T(8,128)(2,1)}, u32[]{:S(2)}, u32[]{:S(2)}) %collective-permute-start.14) | collective-permute-done | bytes 393248 | tf_op jit(solution)/shard_map/ppermute | solution.py:40
  97.5 4.4 collective-permute-done.16.refs_14_
  106.4 4.2 collective-permute-done.19.refs_11_
  110.6 8.0 %collective-permute-done.20.refs_15_ = bf16[2,2,48,1024]{3,2,1,0:T(8,128)(2,1)S(1)} collective-permute-done((bf16[2,2,48,1024]{3,2,1,0:T(8,128)(2,1)S(1)}, bf16[2,2,48,1024]{3,2,1,0:T(8,128)(2,1)S(1)}, u32[]{:S(2)}, u32[]{:S(2)}) %collective-permute-start.20) | collective-permute-done | bytes 393248 | tf_op jit(solution)/shard_map/ppermute | solution.py:40
  120.2 4.6 all-to-all-start.1
  124.8 5.9 place_weights.1
  149.9 3.0 copy.157
  167.7 5.6 collective-permute-start.23
  183.7 3.5 collective-permute-start.27
  198.5 11.3 %collective-permute-done.28.refs_4_.refs_8_ = bf16[256,1536]{1,0:T(8,128)(2,1)} collective-permute-done((bf16[256,1536]{1,0:T(8,128)(2,1)}, bf16[256,1536]{1,0:T(8,128)(2,1)}, u32[]{:S(2)}, u32[]{:S(2)}) %collective-permute-start.28) | collective-permute-done | bytes 786464 | tf_op jit(solution)/shard_map/ppermute | solution.py:40
  212.8 21.6 %collective-permute-done.31.refs_11_ = bf16[4,192,1280]{2,1,0:T(8,128)(2,1)} collective-permute-done((bf16[4,192,1280]{2,1,0:T(8,128)(2,1)}, bf16[4,192,1280]{2,1,0:T(8,128)(2,1)}, u32[]{:S(2)}, u32[]{:S(2)}) %collective-permute-start.31) | collective-permute-done | bytes 1966112 | tf_op jit(solution)/shard_map/ppermute | solution.py:40
  242.7 38.7 %experts.4 = (bf16[2,256,1536]{2,1,0:T(8,128)(2,1)}, bf16[2,256,1536]{2,1,0:T(8,128)(2,1)}, bf16[2,256,1536]{2,1,0:T(8,128)(2,1)}, bf16[2,256,1536]{2,1,0:T(8,12...) custom-call(s32[3]{0:T(128)} %pad_add_fusion.2.place_ref, ...), custom_call_target="tpu_custom_call" | custom-call | flops 24159191040 | bytes 31457280 | tf_op jit(solution)/shard_map/experts/pallas_call | solution.py:340
  289.8 39.1 %experts.5 = (bf16[2,256,1536]{2,1,0:T(8,128)(2,1)}, bf16[2,256,1536]{2,1,0:T(8,128)(2,1)}, bf16[2,256,1536]{2,1,0:T(8,128)(2,1)}, bf16[2,256,1536]{2,1,0:T(8,12...) custom-call(s32[3]{0:T(128)} %pad_add_fusion.2.place_ref, ...), custom_call_target="tpu_custom_call" | custom-call | flops 24159191040 | bytes 31457280 | tf_op jit(solution)/shard_map/experts/pallas_call | solution.py:340
  331.9 3.4 fusion.30
  339.1 38.8 %experts.6 = (bf16[2,256,1536]{2,1,0:T(8,128)(2,1)}, bf16[2,256,1536]{2,1,0:T(8,128)(2,1)}, bf16[2,256,1536]{2,1,0:T(8,128)(2,1)}, bf16[2,256,1536]{2,1,0:T(8,12...) custom-call(s32[3]{0:T(128)} %pad_add_fusion.2.place_ref, ...), custom_call_target="tpu_custom_call" | custom-call | flops 24159191040 | bytes 31457280 | tf_op jit(solution)/shard_map/experts/pallas_call | solution.py:340
  381.4 3.5 fusion.38
  392.3 38.9 %experts.7 = (bf16[2,256,1536]{2,1,0:T(8,128)(2,1)}, bf16[2,256,1536]{2,1,0:T(8,128)(2,1)}, bf16[2,256,1536]{2,1,0:T(8,128)(2,1)}, bf16[2,256,1536]{2,1,0:T(8,12...) custom-call(s32[3]{0:T(128)} %pad_add_fusion.2.place_ref, ...), custom_call_target="tpu_custom_call" | custom-call | flops 24159191040 | bytes 31457280 | tf_op jit(solution)/shard_map/experts/pallas_call | solution.py:340
  439.2 3.0 fusion.41
  446.3 25.8 %expert_grads.3 = (bf16[2,192,1280]{2,1,0:T(8,128)(2,1)}, bf16[2,192,1280]{2,1,0:T(8,128)(2,1)}, bf16[2,192,1280]{2,1,0:T(8,128)(2,1)}, bf16[2,192,1280]{2,1,0:T(8,128)(2,1)}) custom-call(s32[2]{0:T(128)} %pad_add_fusion.1.place_ref, bf16[256,1664]{1,0:T(8,128)(2,1)} %concatenate.72.refs_0_, bf16[256,1664]{1,0:T(8,128)(2,1)} %copy-done.107, ...), custom_call_target="tpu_custom_call" | custom-call | flops 16106127360 | bytes 23068672 | tf_op jit(solution)/shard_map/expert_grads/pallas_call | solution.py:439
  483.4 25.5 %expert_grads.4 = (bf16[2,192,1280]{2,1,0:T(8,128)(2,1)}, bf16[2,192,1280]{2,1,0:T(8,128)(2,1)}, bf16[2,192,1280]{2,1,0:T(8,128)(2,1)}, bf16[2,192,1280]{2,1,0:T(8,128)(2,1)}) custom-call(s32[2]{0:T(128)} %pad_add_fusion.1.place_ref, bf16[256,1664]{1,0:T(8,128)(2,1)} %concatenate.72.refs_0_, bf16[256,1664]{1,0:T(8,128)(2,1)} %copy-done.107, ...), custom_call_target="tpu_custom_call" | custom-call | flops 16106127360 | bytes 23068672 | tf_op jit(solution)/shard_map/expert_grads/pallas_call | solution.py:439
  521.4 3.0 fusion.43
  537.1 4.2 convolution_convert_fusion.1
  543.2 3.6 pick_weights.3
  563.6 4.6 all-to-all-start.2
  568.3 14.7 %collective-permute-done.80 = bf16[2,4,48,1536]{3,2,1,0:T(8,128)(2,1)} collective-permute-done((bf16[2,4,48,1536]{3,2,1,0:T(8,128)(2,1)}, bf16[2,4,48,1536]{3,2,1,0:T(8,128)(2,1)}, u32[]{:S(2)}, u32[]{:S(2)}) %collective-permute-start.80) | collective-permute-done | bytes 1179680 | tf_op jit(solution)/shard_map/ppermute | solution.py:40
  588.9 4.3 collective-permute-start.81
  596.3 3.5 convolution_convert_fusion
  601.4 7.0 collective-permute-done.84
  614.1 3.7 pick_weights.4
  619.8 4.0 pick_weights.5
  623.9 4.2 fusion.15
  630.8 3.6 all-to-all-start.3
  634.4 26.1 %expert_grads.5 = (bf16[10,64,1536]{2,1,0:T(8,128)(2,1)}, bf16[10,64,1536]{2,1,0:T(8,128)(2,1)}) custom-call(s32[2]{0:T(128)} %pad_add_fusion.1.place_ref, bf16[256,1536]{1,0:T(8,128)(2,1)} %bitcast.366, bf16[256,1536]{1,0:T(8,128)(2,1)} %collective-permute-done.5.refs_5_.refs_1_, bf16[256,1536]{1,0:T(8,128)(2,1)} %collective-permute-done.23.refs_6_.refs_2_, ...), custom_call_target="tpu_custom_call" | custom-call | flops 16106127360 | bytes 23068672 | tf_op jit(solution)/shard_map/expert_grads/pallas_call | solution.py:439
  669.3 6.2 collective-permute-done.89
  678.7 8.1 %collective-permute-done.90 = bf16[256,1536]{1,0:T(8,128)(2,1)} collective-permute-done((bf16[256,1536]{1,0:T(8,128)(2,1)S(1)}, bf16[256,1536]{1,0:T(8,128)(2,1)}, u32[]{:S(2)}, u32[]{:S(2)}) %collective-permute-start.90) | collective-permute-done | bytes 786464 | tf_op jit(solution)/shard_map/ppermute | solution.py:40
  686.8 9.3 %all-to-all-done.3.part_ref = bf16[4,192,1280]{2,1,0:T(8,128)(2,1)S(1)} async-done(((bf16[4,192,1280]{2,1,0:T(8,128)(2,1)}), bf16[4,192,1280]{2,1,0:T(8,128)(2,1)S(1)}, u32[]{:S(2)}, u32[]{:S(2)}) %all-to-all-start.3) | async-done | bytes 1966112 | tf_op jit(solution)/shard_map/all_to_all | solution.py:884
  706.7 4.9 unpack_experts.2
  730.3 3.1 collective-permute-done.99
  736.9 4.0 convert_add_fusion
  740.9 4.8 unpack_experts.3
  (632 shorter events, 264.5 us)
Async XLA Ops:
  0.7 30.6 %collective-permute-start.4 = (bf16[256,1536]{1,0:T(8,128)(2,1)}, bf16[256,1536]{1,0:T(8,128)(2,1)}, u32[]{:S(2)}, u32[]{:S(2)}) collective-permute-start(bf16[256,1536]{1,0:T(8,128)(2,1)} %bitcast.362), channel_id=1, source_target_pairs={{0,2},{2,4},{4,6},{6,0},{1,3},{3,5},{5,7},{7,1},{8,10},{10,12},{12... | collective-permute-start | bytes 2359304 | tf_op jit(solution)/shard_map/ppermute | solution.py:40
  2.9 28.5 %collective-permute-start.5 = (bf16[256,1536]{1,0:T(8,128)(2,1)}, bf16[256,1536]{1,0:T(8,128)(2,1)}, u32[]{:S(2)}, u32[]{:S(2)}) collective-permute-start(bf16[256,1536]{1,0:T(8,128)(2,1)} %bitcast.363), channel_id=1, source_target_pairs={{0,16},{16,0},{1,17},{17,1},{2,18},{18,2},{3,19},{19,3},{4,20},{20... | collective-permute-start | bytes 2359304 | tf_op jit(solution)/shard_map/ppermute | solution.py:40
  12.3 54.4 %collective-permute-start.10 = (bf16[10,64,1536]{2,1,0:T(8,128)(2,1)}, bf16[10,64,1536]{2,1,0:T(8,128)(2,1)}, u32[]{:S(2)}, u32[]{:S(2)}) collective-permute-start(bf16[10,64,1536]{2,1,0:T(8,128)(2,1)} %refs_12_.3), channel_id=1, source_target_pairs={{0,1},{1,0},{2,3},{3,2},{4,5},{5,4},{6,7},{7,6},{8,9},{9,8},{10,11... | collective-permute-start | bytes 5898248 | tf_op jit(solution)/shard_map/ppermute | solution.py:40
  31.5 34.5 %collective-permute-start.6 = (bf16[2,2,48,1152]{3,2,1,0:T(8,128)(2,1)S(1)}, bf16[2,2,48,1152]{3,2,1,0:T(8,128)(2,1)S(1)}, u32[]{:S(2)}, u32[]{:S(2)}) collective-permute-start(bf16[2,2,48,1152]{3,2,1,0:T(8,128)(2,1)S(1)} %fusion.53.refs_0_), channel_id=1, source_target_pairs={{0,1},{1,0},{2,3},{3,2},{4,5},{5,4},{6,7},{7,6},{8,9},{9,8},{10,11... | collective-permute-start | bytes 1327112 | tf_op jit(solution)/shard_map/ppermute | solution.py:40
  66.7 53.5 %all-to-all-start = ((bf16[4,192,1280]{2,1,0:T(8,128)(2,1)}), bf16[4,192,1280]{2,1,0:T(8,128)(2,1)}, u32[]{:S(2)}, u32[]{:S(2)}) async-start(bf16[4,192,1280]{2,1,0:T(8,128)(2,1)} %pack_experts.2), calls=%async_computation | async-start | bytes 3932160 | tf_op jit(solution)/shard_map/all_to_all | solution.py:590
  120.2 55.0 %all-to-all-start.1 = ((bf16[4,192,1280]{2,1,0:T(8,128)(2,1)}), bf16[4,192,1280]{2,1,0:T(8,128)(2,1)}, u32[]{:S(2)}, u32[]{:S(2)}) async-start(bf16[4,192,1280]{2,1,0:T(8,128)(2,1)} %pack_experts.3), calls=%async_computation.1 | async-start | bytes 3932160 | tf_op jit(solution)/shard_map/all_to_all | solution.py:600
  133.3 41.9 %collective-permute-start.22 = (bf16[4,192,1280]{2,1,0:T(8,128)(2,1)}, bf16[4,192,1280]{2,1,0:T(8,128)(2,1)}, u32[]{:S(2)}, u32[]{:S(2)}) collective-permute-start(bf16[4,192,1280]{2,1,0:T(8,128)(2,1)} %all-to-all-done.refs_8_), channel_id=1, source_target_pairs={{0,1},{1,0},{2,3},{3,2},{4,5},{5,4},{6,7},{7,6},{8,9},{9,8},{10,11... | collective-permute-start | bytes 5898248 | tf_op jit(solution)/shard_map/ppermute | solution.py:40
  190.6 43.8 %collective-permute-start.31 = (bf16[4,192,1280]{2,1,0:T(8,128)(2,1)}, bf16[4,192,1280]{2,1,0:T(8,128)(2,1)}, u32[]{:S(2)}, u32[]{:S(2)}) collective-permute-start(bf16[4,192,1280]{2,1,0:T(8,128)(2,1)} %all-to-all-done.1.refs_10_), channel_id=1, source_target_pairs={{0,1},{1,0},{2,3},{3,2},{4,5},{5,4},{6,7},{7,6},{8,9},{9,8},{10,11... | collective-permute-start | bytes 5898248 | tf_op jit(solution)/shard_map/ppermute | solution.py:40
  209.8 24.6 %collective-permute-start.29 = (bf16[256,1664]{1,0:T(8,128)(2,1)}, bf16[256,1664]{1,0:T(8,128)(2,1)S(1)}, u32[]{:S(2)}, u32[]{:S(2)}) collective-permute-start(bf16[256,1664]{1,0:T(8,128)(2,1)} %concatenate.72.refs_0_), channel_id=1, source_target_pairs={{0,16},{16,0},{1,17},{17,1},{2,18},{18,2},{3,19},{19,3},{4,20},{20... | collective-permute-start | bytes 2555912 | tf_op jit(solution)/shard_map/ppermute | solution.py:40
  211.1 24.3 %collective-permute-start.32 = (bf16[256,1664]{1,0:T(8,128)(2,1)}, bf16[256,1664]{1,0:T(8,128)(2,1)S(1)}, u32[]{:S(2)}, u32[]{:S(2)}) collective-permute-start(bf16[256,1664]{1,0:T(8,128)(2,1)} %concatenate.72.refs_0_), channel_id=1, source_target_pairs={{0,8},{8,0},{1,9},{9,1},{2,10},{10,2},{3,11},{11,3},{4,12},{12,4},... | collective-permute-start | bytes 2555912 | tf_op jit(solution)/shard_map/ppermute | solution.py:40
  238.9 42.6 %collective-permute-start.36 = (bf16[256,1536]{1,0:T(8,128)(2,1)}, bf16[256,1536]{1,0:T(8,128)(2,1)}, u32[]{:S(2)}, u32[]{:S(2)}) collective-permute-start(bf16[256,1536]{1,0:T(8,128)(2,1)} %collective-permute-done.28.refs_4_.refs_8_), channel_id=1, source_target_pairs={{0,16},{16,0},{1,17},{17,1},{2,18},{18,2},{3,19},{19,3},{4,20},{20... | collective-permute-start | bytes 2359304 | tf_op jit(solution)/shard_map/ppermute | solution.py:40
  240.1 41.4 %collective-permute-start.37 = (bf16[256,1536]{1,0:T(8,128)(2,1)}, bf16[256,1536]{1,0:T(8,128)(2,1)}, u32[]{:S(2)}, u32[]{:S(2)}) collective-permute-start(bf16[256,1536]{1,0:T(8,128)(2,1)} %collective-permute-done.28.refs_4_.refs_8_), channel_id=1, source_target_pairs={{0,2},{2,4},{4,6},{6,0},{1,3},{3,5},{5,7},{7,1},{8,10},{10,12},{12... | collective-permute-start | bytes 2359304 | tf_op jit(solution)/shard_map/ppermute | solution.py:40
  241.3 40.2 %collective-permute-start.35 = (bf16[256,1664]{1,0:T(8,128)(2,1)}, bf16[256,1664]{1,0:T(8,128)(2,1)}, u32[]{:S(2)}, u32[]{:S(2)}) collective-permute-start(bf16[256,1664]{1,0:T(8,128)(2,1)} %copy-done.108), channel_id=1, source_target_pairs={{0,2},{2,4},{4,6},{6,0},{1,3},{3,5},{5,7},{7,1},{8,10},{10,12},{12... | collective-permute-start | bytes 2555912 | tf_op jit(solution)/shard_map/ppermute | solution.py:40
  242.5 39.0 %collective-permute-start.38 = (bf16[256,1664]{1,0:T(8,128)(2,1)}, bf16[256,1664]{1,0:T(8,128)(2,1)}, u32[]{:S(2)}, u32[]{:S(2)}) collective-permute-start(bf16[256,1664]{1,0:T(8,128)(2,1)} %copy-done.108), channel_id=1, source_target_pairs={{0,16},{16,0},{1,17},{17,1},{2,18},{18,2},{3,19},{19,3},{4,20},{20... | collective-permute-start | bytes 2555912 | tf_op jit(solution)/shard_map/ppermute | solution.py:40
  283.2 45.6 %collective-permute-start.42 = (bf16[256,1664]{1,0:T(8,128)(2,1)}, bf16[256,1664]{1,0:T(8,128)(2,1)}, u32[]{:S(2)}, u32[]{:S(2)}) collective-permute-start(bf16[256,1664]{1,0:T(8,128)(2,1)} %collective-permute-done.35.refs_0_.refs_8_), channel_id=1, source_target_pairs={{0,2},{2,4},{4,6},{6,0},{1,3},{3,5},{5,7},{7,1},{8,10},{10,12},{12... | collective-permute-start | bytes 2555912 | tf_op jit(solution)/shard_map/ppermute | solution.py:40
  283.3 45.6 %collective-permute-start.46 = (bf16[256,1664]{1,0:T(8,128)(2,1)}, bf16[256,1664]{1,0:T(8,128)(2,1)}, u32[]{:S(2)}, u32[]{:S(2)}) collective-permute-start(bf16[256,1664]{1,0:T(8,128)(2,1)} %collective-permute-done.35.refs_0_.refs_8_), channel_id=1, source_target_pairs={{0,16},{16,0},{1,17},{17,1},{2,18},{18,2},{3,19},{19,3},{4,20},{20... | collective-permute-start | bytes 2555912 | tf_op jit(solution)/shard_map/ppermute | solution.py:40
  287.1 41.8 %collective-permute-start.43 = (bf16[256,1536]{1,0:T(8,128)(2,1)}, bf16[256,1536]{1,0:T(8,128)(2,1)}, u32[]{:S(2)}, u32[]{:S(2)}) collective-permute-start(bf16[256,1536]{1,0:T(8,128)(2,1)} %collective-permute-done.37.refs_4_.refs_12_), channel_id=1, source_target_pairs={{0,16},{16,0},{1,17},{17,1},{2,18},{18,2},{3,19},{19,3},{4,20},{20... | collective-permute-start | bytes 2359304 | tf_op jit(solution)/shard_map/ppermute | solution.py:40
  288.4 40.5 %collective-permute-start.44 = (bf16[256,1536]{1,0:T(8,128)(2,1)}, bf16[256,1536]{1,0:T(8,128)(2,1)}, u32[]{:S(2)}, u32[]{:S(2)}) collective-permute-start(bf16[256,1536]{1,0:T(8,128)(2,1)} %collective-permute-done.36.refs_5_.refs_9_), channel_id=1, source_target_pairs={{0,8},{8,0},{1,9},{9,1},{2,10},{10,2},{3,11},{11,3},{4,12},{12,4},... | collective-permute-start | bytes 2359304 | tf_op jit(solution)/shard_map/ppermute | solution.py:40
  289.3 39.6 %collective-permute-start.45 = (bf16[2,256,1536]{2,1,0:T(8,128)(2,1)}, bf16[2,256,1536]{2,1,0:T(8,128)(2,1)S(1)}, u32[]{:S(2)}, u32[]{:S(2)}) collective-permute-start(bf16[2,256,1536]{2,1,0:T(8,128)(2,1)} %get-tuple-element.453), channel_id=1, source_target_pairs={{0,8},{8,0},{1,9},{9,1},{2,10},{10,2},{3,11},{11,3},{4,12},{12,4},... | collective-permute-start | bytes 4718600 | tf_op jit(solution)/shard_map/ppermute | solution.py:40
  331.4 46.6 %collective-permute-start.51 = (bf16[256,1536]{1,0:T(8,128)(2,1)}, bf16[256,1536]{1,0:T(8,128)(2,1)}, u32[]{:S(2)}, u32[]{:S(2)}) collective-permute-start(bf16[256,1536]{1,0:T(8,128)(2,1)} %collective-permute-done.37.refs_4_.refs_12_), channel_id=1, source_target_pairs={{0,8},{8,0},{1,9},{9,1},{2,10},{10,2},{3,11},{11,3},{4,12},{12,4},... | collective-permute-start | bytes 2359304 | tf_op jit(solution)/shard_map/ppermute | solution.py:40
  331.9 47.4 %collective-permute-start.52 = (bf16[256,1536]{1,0:T(8,128)(2,1)}, bf16[256,1536]{1,0:T(8,128)(2,1)}, u32[]{:S(2)}, u32[]{:S(2)}) collective-permute-start(bf16[256,1536]{1,0:T(8,128)(2,1)} %collective-permute-done.43.refs_5_.refs_13_), channel_id=1, source_target_pairs={{0,8},{8,0},{1,9},{9,1},{2,10},{10,2},{3,11},{11,3},{4,12},{12,4},... | collective-permute-start | bytes 2359304 | tf_op jit(solution)/shard_map/ppermute | solution.py:40
  335.3 43.9 %collective-permute-start.53 = (bf16[2,256,1536]{2,1,0:T(8,128)(2,1)}, bf16[2,256,1536]{2,1,0:T(8,128)(2,1)S(1)}, u32[]{:S(2)}, u32[]{:S(2)}) collective-permute-start(bf16[2,256,1536]{2,1,0:T(8,128)(2,1)} %get-tuple-element.475), channel_id=1, source_target_pairs={{0,8},{8,0},{1,9},{9,1},{2,10},{10,2},{3,11},{11,3},{4,12},{12,4},... | collective-permute-start | bytes 4718600 | tf_op jit(solution)/shard_map/ppermute | solution.py:40
  336.3 43.0 %collective-permute-start.54 = (bf16[256,1664]{1,0:T(8,128)(2,1)}, bf16[256,1664]{1,0:T(8,128)(2,1)}, u32[]{:S(2)}, u32[]{:S(2)}) collective-permute-start(bf16[256,1664]{1,0:T(8,128)(2,1)} %collective-permute-done.42.refs_0_.refs_12_), channel_id=1, source_target_pairs={{0,16},{16,0},{1,17},{17,1},{2,18},{18,2},{3,19},{19,3},{4,20},{20... | collective-permute-start | bytes 2555912 | tf_op jit(solution)/shard_map/ppermute | solution.py:40
  338.8 40.4 %collective-permute-start.50 = (bf16[256,1536]{1,0:T(8,128)(2,1)}, bf16[256,1536]{1,0:T(8,128)(2,1)}, u32[]{:S(2)}, u32[]{:S(2)}) collective-permute-start(bf16[256,1536]{1,0:T(8,128)(2,1)} %fusion.28), channel_id=1, source_target_pairs={{0,16},{16,0},{1,17},{17,1},{2,18},{18,2},{3,19},{19,3},{4,20},{20... | collective-permute-start | bytes 2359304 | tf_op jit(solution)/shard_map/ppermute | solution.py:40
  378.0 53.2 %collective-permute-start.59 = (bf16[256,1536]{1,0:T(8,128)(2,1)}, bf16[256,1536]{1,0:T(8,128)(2,1)}, u32[]{:S(2)}, u32[]{:S(2)}) collective-permute-start(bf16[256,1536]{1,0:T(8,128)(2,1)} %get-tuple-element.750), channel_id=1, source_target_pairs={{0,16},{16,0},{1,17},{17,1},{2,18},{18,2},{3,19},{19,3},{4,20},{20... | collective-permute-start | bytes 2359304 | tf_op jit(solution)/shard_map/ppermute | solution.py:40
  385.4 45.8 %collective-permute-start.60 = (bf16[2,256,1536]{2,1,0:T(8,128)(2,1)}, bf16[2,256,1536]{2,1,0:T(8,128)(2,1)}, u32[]{:S(2)}, u32[]{:S(2)}) collective-permute-start(bf16[2,256,1536]{2,1,0:T(8,128)(2,1)} %get-tuple-element.497), channel_id=1, source_target_pairs={{0,8},{8,0},{1,9},{9,1},{2,10},{10,2},{3,11},{11,3},{4,12},{12,4},... | collective-permute-start | bytes 4718600 | tf_op jit(solution)/shard_map/ppermute | solution.py:40
  389.1 42.1 %collective-permute-start.61 = (bf16[256,1536]{1,0:T(8,128)(2,1)}, bf16[256,1536]{1,0:T(8,128)(2,1)}, u32[]{:S(2)}, u32[]{:S(2)}) collective-permute-start(bf16[256,1536]{1,0:T(8,128)(2,1)} %fusion.34), channel_id=1, source_target_pairs={{0,16},{16,0},{1,17},{17,1},{2,18},{18,2},{3,19},{19,3},{4,20},{20... | collective-permute-start | bytes 2359304 | tf_op jit(solution)/shard_map/ppermute | solution.py:40
  390.0 41.2 %collective-permute-start.62 = (bf16[256,1536]{1,0:T(8,128)(2,1)}, bf16[256,1536]{1,0:T(8,128)(2,1)}, u32[]{:S(2)}, u32[]{:S(2)}) collective-permute-start(bf16[256,1536]{1,0:T(8,128)(2,1)} %add_convert_fusion.27), channel_id=1, source_target_pairs={{0,2},{2,4},{4,6},{6,0},{1,3},{3,5},{5,7},{7,1},{8,10},{10,12},{12... | collective-permute-start | bytes 2359304 | tf_op jit(solution)/shard_map/ppermute | solution.py:40
  391.7 39.5 %collective-permute-start.58 = (bf16[256,1536]{1,0:T(8,128)(2,1)}, bf16[256,1536]{1,0:T(8,128)(2,1)}, u32[]{:S(2)}, u32[]{:S(2)}) collective-permute-start(bf16[256,1536]{1,0:T(8,128)(2,1)} %fusion.33), channel_id=1, source_target_pairs={{0,16},{16,0},{1,17},{17,1},{2,18},{18,2},{3,19},{19,3},{4,20},{20... | collective-permute-start | bytes 2359304 | tf_op jit(solution)/shard_map/ppermute | solution.py:40
  442.7 30.4 %collective-permute-start.65 = (bf16[256,1536]{1,0:T(8,128)(2,1)S(1)}, bf16[256,1536]{1,0:T(8,128)(2,1)}, u32[]{:S(2)}, u32[]{:S(2)}) collective-permute-start(bf16[256,1536]{1,0:T(8,128)(2,1)S(1)} %get-tuple-element.529), channel_id=1, source_target_pairs={{0,16},{16,0},{1,17},{17,1},{2,18},{18,2},{3,19},{19,3},{4,20},{20... | collective-permute-start | bytes 2359304 | tf_op jit(solution)/shard_map/ppermute | solution.py:40
  443.6 29.5 %collective-permute-start.66 = (bf16[256,1536]{1,0:T(8,128)(2,1)}, bf16[256,1536]{1,0:T(8,128)(2,1)}, u32[]{:S(2)}, u32[]{:S(2)}) collective-permute-start(bf16[256,1536]{1,0:T(8,128)(2,1)} %add_convert_fusion.23), channel_id=1, source_target_pairs={{0,2},{2,4},{4,6},{6,0},{1,3},{3,5},{5,7},{7,1},{8,10},{10,12},{12... | collective-permute-start | bytes 2359304 | tf_op jit(solution)/shard_map/ppermute | solution.py:40
  444.4 28.7 %collective-permute-start.67 = (bf16[2,256,1536]{2,1,0:T(8,128)(2,1)}, bf16[2,256,1536]{2,1,0:T(8,128)(2,1)}, u32[]{:S(2)}, u32[]{:S(2)}) collective-permute-start(bf16[2,256,1536]{2,1,0:T(8,128)(2,1)} %get-tuple-element.531), channel_id=1, source_target_pairs={{0,8},{8,0},{1,9},{9,1},{2,10},{10,2},{3,11},{11,3},{4,12},{12,4},... | collective-permute-start | bytes 4718600 | tf_op jit(solution)/shard_map/ppermute | solution.py:40
  445.1 27.1 %collective-permute-start.68 = (f32[4,40,256]{2,1,0:T(8,128)S(1)}, f32[4,40,256]{2,1,0:T(8,128)}, u32[]{:S(2)}, u32[]{:S(2)}) collective-permute-start(f32[4,40,256]{2,1,0:T(8,128)S(1)} %slice_bitcast_fusion.5), channel_id=1, source_target_pairs={{0,16},{16,0},{1,17},{17,1},{2,18},{18,2},{3,19},{19,3},{4,20},{20... | collective-permute-start | bytes 491528 | tf_op jit(solution)/shard_map/ppermute | solution.py:40
  480.4 28.5 %collective-permute-start.69 = (bf16[256,1536]{1,0:T(8,128)(2,1)}, bf16[256,1536]{1,0:T(8,128)(2,1)}, u32[]{:S(2)}, u32[]{:S(2)}) collective-permute-start(bf16[256,1536]{1,0:T(8,128)(2,1)} %add_convert_fusion.15), channel_id=1, source_target_pairs={{0,2},{2,4},{4,6},{6,0},{1,3},{3,5},{5,7},{7,1},{8,10},{10,12},{12... | collective-permute-start | bytes 2359304 | tf_op jit(solution)/shard_map/ppermute | solution.py:40
  481.0 27.9 %collective-permute-start.70 = (bf16[256,1536]{1,0:T(8,128)(2,1)}, bf16[256,1536]{1,0:T(8,128)(2,1)}, u32[]{:S(2)}, u32[]{:S(2)}) collective-permute-start(bf16[256,1536]{1,0:T(8,128)(2,1)} %get-tuple-element.555), channel_id=1, source_target_pairs={{0,16},{16,0},{1,17},{17,1},{2,18},{18,2},{3,19},{19,3},{4,20},{20... | collective-permute-start | bytes 2359304 | tf_op jit(solution)/shard_map/ppermute | solution.py:40
  481.3 27.6 %collective-permute-start.74 = (bf16[2,192,1280]{2,1,0:T(8,128)(2,1)}, bf16[2,192,1280]{2,1,0:T(8,128)(2,1)S(1)}, u32[]{:S(2)}, u32[]{:S(2)}) collective-permute-start(bf16[2,192,1280]{2,1,0:T(8,128)(2,1)} %get-tuple-element.557), channel_id=1, source_target_pairs={{0,1},{1,0},{2,3},{3,2},{4,5},{5,4},{6,7},{7,6},{8,9},{9,8},{10,11... | collective-permute-start | bytes 2949128 | tf_op jit(solution)/shard_map/ppermute | solution.py:40
  482.7 26.1 %collective-permute-start.73 = (f32[40,256]{1,0:T(8,128)S(1)}, f32[40,256]{1,0:T(8,128)S(1)}, u32[]{:S(2)}, u32[]{:S(2)}) collective-permute-start(f32[40,256]{1,0:T(8,128)S(1)} %bitcast_add_fusion.2), channel_id=1, source_target_pairs={{0,2},{2,4},{4,6},{6,0},{1,3},{3,5},{5,7},{7,1},{8,10},{10,12},{12... | collective-permute-start | bytes 122888 | tf_op jit(solution)/shard_map/ppermute | solution.py:40
  518.6 24.7 %collective-permute-start.76 = (bf16[2,192,1280]{2,1,0:T(8,128)(2,1)}, bf16[2,192,1280]{2,1,0:T(8,128)(2,1)}, u32[]{:S(2)}, u32[]{:S(2)}) collective-permute-start(bf16[2,192,1280]{2,1,0:T(8,128)(2,1)} %get-tuple-element.577), channel_id=1, source_target_pairs={{0,1},{1,0},{2,3},{3,2},{4,5},{5,4},{6,7},{7,6},{8,9},{9,8},{10,11... | collective-permute-start | bytes 2949128 | tf_op jit(solution)/shard_map/ppermute | solution.py:40
  525.5 59.0 %collective-permute-start.79 = (bf16[2,192,1280]{2,1,0:T(8,128)(2,1)}, bf16[2,192,1280]{2,1,0:T(8,128)(2,1)}, u32[]{:S(2)}, u32[]{:S(2)}) collective-permute-start(bf16[2,192,1280]{2,1,0:T(8,128)(2,1)} %get-tuple-element.583), channel_id=1, source_target_pairs={{0,1},{1,0},{2,3},{3,2},{4,5},{5,4},{6,7},{7,6},{8,9},{9,8},{10,11... | collective-permute-start | bytes 2949128 | tf_op jit(solution)/shard_map/ppermute | solution.py:40
  556.5 26.4 %collective-permute-start.80 = (bf16[2,4,48,1536]{3,2,1,0:T(8,128)(2,1)}, bf16[2,4,48,1536]{3,2,1,0:T(8,128)(2,1)}, u32[]{:S(2)}, u32[]{:S(2)}) collective-permute-start(bf16[2,4,48,1536]{3,2,1,0:T(8,128)(2,1)} %get-tuple-element.600), channel_id=1, source_target_pairs={{0,16},{16,0},{1,17},{17,1},{2,18},{18,2},{3,19},{19,3},{4,20},{20... | collective-permute-start | bytes 3538952 | tf_op jit(solution)/shard_map/ppermute | solution.py:40
  561.2 48.2 %collective-permute-start.82 = (bf16[2,192,1280]{2,1,0:T(8,128)(2,1)}, bf16[2,192,1280]{2,1,0:T(8,128)(2,1)}, u32[]{:S(2)}, u32[]{:S(2)}) collective-permute-start(bf16[2,192,1280]{2,1,0:T(8,128)(2,1)} %get-tuple-element.604), channel_id=1, source_target_pairs={{0,1},{1,0},{2,3},{3,2},{4,5},{5,4},{6,7},{7,6},{8,9},{9,8},{10,11... | collective-permute-start | bytes 2949128 | tf_op jit(solution)/shard_map/ppermute | solution.py:40
  562.7 46.6 %collective-permute-start.83 = (bf16[256,1536]{1,0:T(8,128)(2,1)}, bf16[256,1536]{1,0:T(8,128)(2,1)}, u32[]{:S(2)}, u32[]{:S(2)}) collective-permute-start(bf16[256,1536]{1,0:T(8,128)(2,1)} %add_convert_fusion.10), channel_id=1, source_target_pairs={{0,2},{2,4},{4,6},{6,0},{1,3},{3,5},{5,7},{7,1},{8,10},{10,12},{12... | collective-permute-start | bytes 2359304 | tf_op jit(solution)/shard_map/ppermute | solution.py:40
  563.1 65.1 %collective-permute-start.85 = (bf16[256,1536]{1,0:T(8,128)(2,1)}, bf16[256,1536]{1,0:T(8,128)(2,1)}, u32[]{:S(2)}, u32[]{:S(2)}) collective-permute-start(bf16[256,1536]{1,0:T(8,128)(2,1)} %get-tuple-element.615), channel_id=1, source_target_pairs={{0,16},{16,0},{1,17},{17,1},{2,18},{18,2},{3,19},{19,3},{4,20},{20... | collective-permute-start | bytes 2359304 | tf_op jit(solution)/shard_map/ppermute | solution.py:40
  563.6 64.6 %all-to-all-start.2 = ((bf16[4,192,1280]{2,1,0:T(8,128)(2,1)}), bf16[4,192,1280]{2,1,0:T(8,128)(2,1)}, u32[]{:S(2)}, u32[]{:S(2)}) async-start(bf16[4,192,1280]{2,1,0:T(8,128)(2,1)} %pad_maximum_fusion), calls=%async_computation.2 | async-start | bytes 3932160 | tf_op jit(solution)/shard_map/all_to_all | solution.py:826
  628.2 34.2 %collective-permute-start.86 = (bf16[2,4,2,48,768]{4,3,2,1,0:T(8,128)(2,1)}, bf16[2,4,2,48,768]{4,3,2,1,0:T(8,128)(2,1)}, u32[]{:S(2)}, u32[]{:S(2)}) collective-permute-start(bf16[2,4,2,48,768]{4,3,2,1,0:T(8,128)(2,1)} %get-tuple-element.643), channel_id=1, source_target_pairs={{0,16},{16,0},{1,17},{17,1},{2,18},{18,2},{3,19},{19,3},{4,20},{20... | collective-permute-start | bytes 3538952 | tf_op jit(solution)/shard_map/ppermute | solution.py:40
  629.3 31.1 %collective-permute-start.87 = (bf16[2,4,2,48,640]{4,3,2,1,0:T(8,128)(2,1)}, bf16[2,4,2,48,640]{4,3,2,1,0:T(8,128)(2,1)}, u32[]{:S(2)}, u32[]{:S(2)}) collective-permute-start(bf16[2,4,2,48,640]{4,3,2,1,0:T(8,128)(2,1)} %get-tuple-element.645), channel_id=1, source_target_pairs={{0,1},{1,0},{2,3},{3,2},{4,5},{5,4},{6,7},{7,6},{8,9},{9,8},{10,11... | collective-permute-start | bytes 2949128 | tf_op jit(solution)/shard_map/ppermute | solution.py:40
  630.8 65.3 %all-to-all-start.3 = ((bf16[4,192,1280]{2,1,0:T(8,128)(2,1)}), bf16[4,192,1280]{2,1,0:T(8,128)(2,1)S(1)}, u32[]{:S(2)}, u32[]{:S(2)}) async-start(bf16[4,192,1280]{2,1,0:T(8,128)(2,1)} %pad_maximum_fusion.1), calls=%async_computation.3 | async-start | bytes 3932160 | tf_op jit(solution)/shard_map/all_to_all | solution.py:884
  668.4 68.5 %collective-permute-start.101 = (bf16[10,64,1536]{2,1,0:T(8,128)(2,1)}, bf16[10,64,1536]{2,1,0:T(8,128)(2,1)}, u32[]{:S(2)}, u32[]{:S(2)}) collective-permute-start(bf16[10,64,1536]{2,1,0:T(8,128)(2,1)} %get-tuple-element.674), channel_id=1, source_target_pairs={{0,1},{1,0},{2,3},{3,2},{4,5},{5,4},{6,7},{7,6},{8,9},{9,8},{10,11... | collective-permute-start | bytes 5898248 | tf_op jit(solution)/shard_map/ppermute | solution.py:40
  (177 other events, 1418.4 us)

commit v4 on v3

--- a/solution.py
+++ b/solution.py
@@ -281,10 +281,14 @@
             for copy in weights[part]:
                 copy.wait()
 
+        all_hidden = dot(rows, w_in[part][...])
+        all_plain = dot(
+            grad_rows, w_back[expert * width : (expert + count) * width, :], ((1,), (1,))
+        )
         for i in range(count):
             here = slice(expert * width, (expert + 1) * width)
-            hidden = dot(rows, w_in[part][:, 2 * width * i : 2 * width * (i + 1)])
-            grad_plain = dot(grad_rows, w_back[here, :], ((1,), (1,)))
+            hidden = all_hidden[:, 2 * width * i : 2 * width * (i + 1)]
+            grad_plain = all_plain[:, width * i : width * (i + 1)]
             gate_part, up_part = hidden[:, :width], hidden[:, width:]
             sigmoid_gate = 1.0 / (1.0 + jnp.exp(-gate_part))
             silu = gate_part * sigmoid_gate
@@ -469,21 +473,124 @@
     return (segment, token_index - offset)
 
 
-def rotary_embedding(values_in, token_position, direction):
-    half_size = values_in.shape[-1] // 2
+def rotary_tables(token_position):
+    half_size = HEAD_SIZE // 2
     frequency = jnp.exp(jnp.arange(half_size, dtype=F32) * (-math.log(10000.0) / half_size))
-    angles = token_position.astype(F32)[..., None] * frequency
-    cosine = jnp.cos(angles)[..., None, :]
-    sine_part = jnp.sin(angles)[..., None, :]
-    first_half = values_in[..., :half_size]
-    second_half = values_in[..., half_size:]
-    return jnp.concatenate(
-        [
-            first_half * cosine - direction * second_half * sine_part,
-            second_half * cosine + direction * first_half * sine_part,
-        ],
-        axis=-1,
-    )
+    angles = token_position.astype(F32)[:, None] * frequency
+    cosine, sine_part = jnp.cos(angles), jnp.sin(angles)
+    repeat = LANES // HEAD_SIZE
+    return (
+        jnp.concatenate([cosine, cosine] * repeat, axis=1),
+        jnp.concatenate([-sine_part, sine_part] * repeat, axis=1),
+    )
+
+
+def rotate(values, cosine, sine_part, direction):
+    lane = lax.broadcasted_iota(jnp.int32, (values.shape[0], LANES), 1)
+    first = lane % HEAD_SIZE < HEAD_SIZE // 2
+    tiles = []
+    for start in range(0, values.shape[1], LANES):
+        tile = values[:, start : start + LANES]
+        after = pltpu.roll(tile, LANES - HEAD_SIZE // 2, 1)
+        before = pltpu.roll(tile, HEAD_SIZE // 2, 1)
+        swapped = jnp.where(first, after, before)
+        tiles.append(tile * cosine + direction * swapped * sine_part)
+    return jnp.concatenate(tiles, axis=1)
+
+
+def allowed_pairs(column_ref, row_ref):
+    shape = column_ref.shape
+    same = column_ref[...] == row_ref[0, :1, :]
+    earlier = lax.broadcasted_iota(jnp.int32, shape, 0) >= lax.broadcasted_iota(jnp.int32, shape, 1)
+    return jnp.concatenate([same & earlier] * QUERY_PER_GROUP, axis=0)
+
+
+def group_rows(rows, group):
+    heads = [group * QUERY_PER_GROUP + i for i in range(QUERY_PER_GROUP)]
+    return jnp.concatenate([rows[:, HEAD_SIZE * h : HEAD_SIZE * (h + 1)] for h in heads], axis=0)
+
+
+def probabilities(query, keys, allowed):
+    scores = dot(query, keys, ((1,), (1,))) * (1.0 / math.sqrt(HEAD_SIZE))
+    scores = jnp.where(allowed, scores, -1000000000.0)
+    shifted = jnp.exp(scores - jnp.max(scores, axis=-1, keepdims=True))
+    return shifted / jnp.sum(shifted, axis=-1, keepdims=True)
+
+
+def attention_kernel(
+    qk_ref, value_ref, cos_ref, sin_ref, column_ref, row_ref, query_ref, key_ref, mixed_ref
+):
+    width = query_ref.shape[1]
+    block = query_ref.shape[0]
+    rotated = rotate(qk_ref[...], cos_ref[...], sin_ref[...], 1.0).astype(BF16)
+    query_ref[...] = rotated[:, :width]
+    key_ref[...] = rotated[:, width:]
+    allowed = allowed_pairs(column_ref, row_ref)
+    for group in range(key_ref.shape[1] // HEAD_SIZE):
+        here = slice(HEAD_SIZE * group, HEAD_SIZE * (group + 1))
+        query = group_rows(query_ref[...], group)
+        probs = probabilities(query, key_ref[:, here], allowed)
+        mixed = dot(probs.astype(BF16), value_ref[:, here]).astype(BF16)
+        for i in range(QUERY_PER_GROUP):
+            start = HEAD_SIZE * (group * QUERY_PER_GROUP + i)
+            mixed_ref[:, start : start + HEAD_SIZE] = mixed[block * i : block * (i + 1)]
+
+
+def attention_back_kernel(
+    query_ref,
+    key_ref,
+    value_ref,
+    grad_ref,
+    cos_ref,
+    sin_ref,
+    column_ref,
+    row_ref,
+    grad_qk_ref,
+    grad_value_ref,
+    total,
+):
+    width = query_ref.shape[1]
+    block = query_ref.shape[0]
+    scale = 1.0 / math.sqrt(HEAD_SIZE)
+    allowed = allowed_pairs(column_ref, row_ref)
+    for group in range(key_ref.shape[1] // HEAD_SIZE):
+        here = slice(HEAD_SIZE * group, HEAD_SIZE * (group + 1))
+        query = group_rows(query_ref[...], group)
+        grad_mixed = group_rows(grad_ref[...], group)
+        probs = probabilities(query, key_ref[:, here], allowed)
+        grad_probs = dot(grad_mixed, value_ref[:, here], ((1,), (1,)))
+        grad_value_ref[:, here] = dot(probs.astype(BF16), grad_mixed, ((0,), (0,))).astype(BF16)
+        spread = jnp.sum(probs * grad_probs, axis=-1, keepdims=True)
+        grad_scores = (probs * (grad_probs - spread)).astype(BF16)
+        grad_query = dot(grad_scores, key_ref[:, here]) * scale
+        for i in range(QUERY_PER_GROUP):
+            start = HEAD_SIZE * (group * QUERY_PER_GROUP + i)
+            total[:, start : start + HEAD_SIZE] = grad_query[block * i : block * (i + 1)]
+        start = width + HEAD_SIZE * group
+        total[:, start : start + HEAD_SIZE] = dot(grad_scores, query, ((0,), (0,))) * scale
+    grad_qk_ref[...] = rotate(total[...], cos_ref[...], sin_ref[...], -1.0).astype(BF16)
+
+
+def attention_call(kernel, arrays, widths, tables, block, scratch, name):
+    rows = arrays[0].shape[0]
+
+    def by_row(columns):
+        return pl.BlockSpec((block, columns), lambda i: (i, 0))
+
+    return pl.pallas_call(
+        kernel,
+        grid=(rows // block,),
+        in_specs=[by_row(a.shape[1]) for a in list(arrays) + list(tables[:3])]
+        + [pl.BlockSpec((1,) + tables[3].shape[1:], lambda i: (i, 0, 0))],
+        out_specs=[by_row(width) for width in widths],
+        out_shape=[jax.ShapeDtypeStruct((rows, width), BF16) for width in widths],
+        scratch_shapes=scratch,
+        compiler_params=pltpu.CompilerParams(vmem_limit_bytes=VMEM_BYTES // 2),
+        cost_estimate=pl.CostEstimate(
+            flops=2 * rows * block * 4 * MODEL_WIDTH, bytes_accessed=8 << 20, transcendentals=0
+        ),
+        name=name,
+    )(*arrays, *tables)
 
 
 def norm_back(grad_normed, values_in, inverse_root, gain):
@@ -518,7 +625,6 @@
     y_size, z_size, x_size = lax.axis_size("y"), lax.axis_size("z"), lax.axis_size("x")
     core = lax.axis_index("c")
     group = lax.axis_index("y") * 2 + core
-    score_scale = 1.0 / math.sqrt(HEAD_SIZE)
     own_rows = w_query.shape[0]
     q_width, kv_width = MODEL_WIDTH // 2, KEY_VALUE_HEADS * HEAD_SIZE // 2
     kv_heads = KEY_VALUE_HEADS // 2
@@ -618,30 +724,27 @@
     blocks = 2 * micro
     qk_pre = dot(normalized_input, w_qk)
     values = dot(normalized_input, w_v).astype(BF16)
-    qk_pre, values, grads_y = sync(qk_pre, values, grads_y)
-    query_pre = qk_pre[:, :q_width]
-    query_pre = query_pre.reshape(blocks, block, kv_heads * QUERY_PER_GROUP, HEAD_SIZE)
-    key_pre = qk_pre[:, q_width:].reshape(blocks, block, kv_heads, HEAD_SIZE)
-    values = values.reshape(blocks, block, kv_heads, HEAD_SIZE)
-    query = rotary_embedding(query_pre, token_position, 1.0).astype(BF16)
-    query = query.reshape(blocks, block, kv_heads, QUERY_PER_GROUP, HEAD_SIZE)
-    keys = rotary_embedding(key_pre, token_position, 1.0).astype(BF16)
-    token_index = jnp.arange(block, dtype=jnp.int32)
-    allowed = (segment[:, :, None] == segment[:, None, :]) & (
-        token_index[:, None] >= token_index[None, :]
-    )
-    query, keys, first_parts, swapped, grads_z = sync(query, keys, first_parts, swapped, grads_z)
+    qk_pre, values, grads_y[0] = sync(qk_pre, values, grads_y[0])
+    grads_other = [[ring_step(part, "c") for part in grads_y[0]]]
+    tables = rotary_tables(token_position.reshape(-1)) + (
+        jnp.broadcast_to(segment.reshape(-1, 1), (blocks * block, block)),
+        jnp.broadcast_to(segment[:, None, :], (blocks, 8, block)),
+    )
+    query, keys, mixed = attention_call(
+        attention_kernel,
+        [qk_pre, values],
+        [q_width, kv_width, q_width],
+        tables,
+        block,
+        [],
+        "attention",
+    )
+    projected = dot(mixed, w_out)
+    projected, first_parts, swapped, grads_other, grads_y = sync(
+        projected, first_parts, swapped, grads_other, grads_y
+    )
     second_parts = ring_gather(swapped, "x")
-    grads_ahead = ring_step(grads_z[1], "z")
-    scores = jnp.einsum("bqkgd,bskd->bkgqs", query, keys, preferred_element_type=F32)
-    scores = jnp.where(allowed[:, None, None], scores * score_scale, -1000000000.0)
-    probs = jax.nn.softmax(scores, axis=-1)
-    probs_low = probs.astype(BF16)
-    mixed = jnp.einsum("bkgqs,bskd->bqkgd", probs_low, values, preferred_element_type=F32)
-    mixed = mixed.reshape(2 * count, q_width).astype(BF16)
-    grads_other = [[ring_step(part, "c") for part in some] for some in grads_y]
-    mixed, grads_other = sync(mixed, grads_other)
-    projected = dot(mixed, w_out)
+    grads_other.append([ring_step(part, "c") for part in grads_y[1]])
     own_act = act_rows[:count]
     resid = own_act + ring_sum([projected[:count], projected[count:]], "c", F32)
 
@@ -658,16 +761,10 @@
     low = gates - high
     spare = jnp.zeros((count, LANES - 2 * E), BF16)
     sent = jnp.concatenate([normed_two, high.astype(BF16), low.astype(BF16), spare], axis=1)
-    sent, grads_ahead = sync(sent, grads_ahead)
-    grads_z.append(grads_ahead)
-    rows, ahead, second_parts, others, grads_third = sync(
-        ring_gather(sent, "y"),
-        ring_step(sent, "z"),
-        second_parts,
-        ring_step(sent, "c"),
-        ring_step(grads_z[2], "c"),
-    )
-    grads_other.append([grads_third])
+    sent, grads_other = sync(sent, grads_other)
+    rows, ahead, second_parts, others = sync(
+        ring_gather(sent, "y"), ring_step(sent, "z"), second_parts, ring_step(sent, "c")
+    )
     w_in_parts, w_back_parts = [first_parts, second_parts], down_parts
     rows, others = sync(rows, [others] + [ring_step(part, "c") for part in rows[1:]])
     width = w_in_parts[0][0].shape[-1] // (2 * counts[0])
@@ -683,6 +780,12 @@
 
     def end_y(parts, arrived):
         return plus(arrived, parts[0]) if y_size == 2 else arrived
+
+    def begin(parts, axis):
+        return ring_step(parts[1], axis) if len(parts) == 2 else ring_sum(parts, axis, BF16)
+
+    def finish(parts, arrived):
+        return plus(arrived, parts[0]) if len(parts) == 2 else arrived
 
     sent_chunks, grad_chunks, weighted, grad_hidden, grads_gates = [], [], [], [], []
     results_c, grads_c, results_sum, grads_sum = [], [], {}, {}
@@ -703,13 +806,12 @@
         if z_step + 2 < z_size:
             moved["ahead"] = ring_step(ahead, "z")
         if z_step <= 1:
-            moved["grads"] = ring_gather(grads_z[2 + z_step], "y")
-        if z_step == 0:
-            moved["grads_z"] = ring_step(grads_z[2], "z")
+            moved["grads_z"] = ring_step(grads_z[1 + z_step], "z")
         if z_step == 1:
-            moved["grads_other"] = [ring_step(part, "c") for part in grads_y[2][1:]]
+            moved["grads"] = ring_gather(grads_z[2], "y")
         if z_step == 2:
-            moved["grads_other"] = [ring_step(part, "c") for part in grads_y[3]]
+            moved["grads"] = [ring_step(part, "z") for part in grads_y[2][1:]]
+            moved["grads_other"] = [ring_step(grads_z[3], "c")]
         if z_step >= 2:
             moved["grad"] = hops_y(grads_c[z_step - 1])
         if z_step >= 1:
@@ -722,19 +824,21 @@
         weighted.append(parts[4])
         grad_hidden.append(parts[5])
         grads_gates.append(parts[6])
+        grads_last = []
         if z_step <= 1:
-            grads_y.append(moved["grads"])
-        if z_step == 0:
             grads_z.append(moved["grads_z"])
-        if z_step == 1:
-            grads_other[2] += moved["grads_other"]
-        if z_step == 2:
-            grads_other.append(moved["grads_other"])
+        if z_step in (1, 2):
+            grads_y.append(([grads_z[3]] if z_step == 2 else []) + moved["grads"])
+            grads_other.append(moved.get("grads_other", []))
+            missing = grads_y[-1][len(grads_other[-1]) :]
+            grads_last = [ring_step(part, "c") for part in missing]
         arrived = ring_step(parts[3], "c")
         if z_step + 1 < z_size:
             ahead, rows = moved.get("ahead"), moved["rows"]
             others = [ring_step(part, "c") for part in rows]
-        arrived, others, rows = sync(arrived, others, rows)
+        arrived, others, rows, grads_last = sync(arrived, others, rows, grads_last)
+        if grads_last:
+            grads_other[-1] = grads_other[-1] + grads_last
         if z_step >= 1:
             results_c.append(plus_all(moved["result"], last_results[0]))
         if z_step >= 2:
@@ -770,22 +874,23 @@
     grad_hidden, total, results_sum, results_c, first_grads, result_three = sync(
         grad_hidden, total, results_sum, results_c, first_grads, result_three
     )
-    second_grads, step, result_two, grad_gates, one = sync(
+    second_grads, step, result_two, result_step, grad_gates, one = sync(
         in_grads(1),
         ring_step(total, "z"),
         hops_y(results_c[2]),
+        ring_step(results_sum[1], "z"),
         ring_sum([spread[i] for i in range(z_size)], "z", F32),
         ring_step(first_grads[2], "x"),
     )
     grad_gates = with_layout_constraint(grad_gates, Layout((0, 1))).T
     grad_experts = plus(step, grads_sum[0], F32)
-    grad_experts, first_grads, second_grads, results_c, results_sum, result_two, result_three = sync(
-        grad_experts, first_grads, second_grads, results_c, results_sum, result_two, result_three
+    result_total = plus(result_step, end_y(results_c[2], result_two))
+    grad_experts, first_grads, second_grads, results_c, result_total, result_three = sync(
+        grad_experts, first_grads, second_grads, results_c, result_total, result_three
     )
     two = ring_step(first_grads[3], "x")
     second_one = ring_step(second_grads[2], "x")
-    result_step = ring_step(results_sum[1], "z")
-    results_sum[2] = end_y(results_c[2], result_two)
+    result_step = ring_step(result_total, "z")
     results_c.append(plus_all(result_three, last_results[0]))
     result_three = hops_y(results_c[3])
 
@@ -812,43 +917,36 @@
     grad_att = grad_resid.astype(BF16)
     grad_att = jnp.concatenate([grad_att, ring_step(grad_att, "c")])
     grad_w_out = dot(mixed, grad_att, ((0,), (0,))).astype(BF16)
-    grad_mixed = dot(grad_att, w_out, ((1,), (1,))).astype(BF16).reshape(query.shape)
+    grad_mixed = dot(grad_att, w_out, ((1,), (1,))).astype(BF16)
     grad_mixed, grad_w_out, two, result_step, result_three, second_grads, results_c = sync(
         grad_mixed, grad_w_out, two, result_step, result_three, second_grads, results_c
     )
     first_sum = finish_in(first_grads, one, two)
-    result_total = plus(result_step, results_sum[2])
-    results_sum[3] = end_y(results_c[3], result_three)
+    result_total = plus(result_step, end_y(results_c[3], result_three))
     out_parts = pick_weights([(grad_w_out, 0, MODEL_WIDTH)], "x", "y", False)
     first_sum, out_parts, grad_mixed, result_total, second_grads = sync(
         first_sum, out_parts, grad_mixed, result_total, second_grads
     )
     first_pieces = lax.all_to_all(first_sum, "z", 0, 0, tiled=True)
     second_two = ring_step(second_grads[3], "x")
-    out_sum = ring_sum(out_parts, "y", BF16)
+    out_hop = begin(out_parts, "y")
     result_step = ring_step(result_total, "z")
     result_zero = hops_y(results_c[0])
-    grad_probs = jnp.einsum("bqkgd,bskd->bkgqs", grad_mixed, values, preferred_element_type=F32)
-    grad_value_pre = jnp.einsum(
-        "bkgqs,bqkgd->bskd", probs_low, grad_mixed, preferred_element_type=F32
-    )
-    grad_value_pre = grad_value_pre.reshape(2 * count, kv_width).astype(BF16)
-    grad_scores = (
-        probs * (grad_probs - jnp.sum(probs * grad_probs, axis=-1, keepdims=True))
-    ).astype(BF16)
-    grad_query = jnp.einsum("bkgqs,bskd->bqkgd", grad_scores, keys, preferred_element_type=F32)
-    grad_keys = jnp.einsum("bkgqs,bqkgd->bskd", grad_scores, query, preferred_element_type=F32)
-    grad_query_pre = rotary_embedding(
-        (grad_query * score_scale).reshape(query_pre.shape), token_position, -1.0
-    )
-    grad_query_pre = grad_query_pre.reshape(2 * count, q_width).astype(BF16)
-    grad_key_pre = rotary_embedding(grad_keys * score_scale, token_position, -1.0)
-    grad_key_pre = grad_key_pre.reshape(2 * count, kv_width).astype(BF16)
-    grad_qk_pre = jnp.concatenate([grad_query_pre, grad_key_pre], axis=1)
-    grad_qk_pre, grad_value_pre, second_one, out_sum = sync(
-        grad_qk_pre, grad_value_pre, second_one, out_sum
-    )
-    out_sum = sum_along(out_sum, "x")
+    grad_qk_pre, grad_value_pre = attention_call(
+        attention_back_kernel,
+        [query, keys, values, grad_mixed],
+        [q_width + kv_width, kv_width],
+        tables,
+        block,
+        [pltpu.VMEM((block, q_width + kv_width), F32)],
+        "attention_back",
+    )
+    grad_qk_pre, grad_value_pre, second_one, out_hop, out_parts = sync(
+        grad_qk_pre, grad_value_pre, second_one, out_hop, out_parts
+    )
+    out_parts = finish(out_parts, out_hop)
+    out_parts = [out_parts[i] for i in range(x_size)]
+    out_hop = begin(out_parts, "x")
     grad_w_qk = dot(normalized_input, grad_qk_pre, ((0,), (0,))).astype(BF16)
     grad_w_v = dot(normalized_input, grad_value_pre, ((0,), (0,))).astype(BF16)
     grad_normed = dot(grad_qk_pre, w_qk, ((1,), (1,)))
@@ -861,7 +959,6 @@
         grad_w_v,
         result_step,
     )
-    result_step = ring_step(plus(result_step, results_sum[3]), "z")
     second_sum = finish_in(second_grads, second_one, second_two)
     grad_normed = grad_normed + other_normed
     grad_rows, grad_gain_one = norm_back(grad_normed, own_act, r_one[:count], gain_first)
@@ -878,15 +975,18 @@
         (grad_small.astype(BF16), 0, LANES),
     ]
     rest_parts = pick_weights(rest, "y", "x", True)
-    q_parts, rest_parts, grad_rows, grad_chunks, out_sum, result_zero, first_pieces, second_sum = sync(
-        q_parts, rest_parts, grad_rows, grad_chunks, out_sum, result_zero, first_pieces, second_sum
+    q_parts, rest_parts, grad_rows, grad_chunks, result_zero, first_pieces, second_sum = sync(
+        q_parts, rest_parts, grad_rows, grad_chunks, result_zero, first_pieces, second_sum
     )
     second_pieces = lax.all_to_all(second_sum, "z", 0, 0, tiled=True)
-    grad_w_back, q_sum, rest_sum = sync(
+    grad_w_back, q_sum, rest_sum, out_hop, out_parts = sync(
         expert_grads(grad_chunks, weighted, 0, local_count, width, True),
         ring_sum(q_parts, "y", BF16),
         ring_sum(rest_parts, "x", BF16),
-    )
+        out_hop,
+        out_parts,
+    )
+    out_sum = finish(out_parts, out_hop)
     back_x = ring_step(grad_w_back[1], "x")
     q_sum, rest_sum, out_sum, first_pieces, second_pieces, result_step = sync(
         sum_along(q_sum, "x"),

time: 758 us -> 732 us (0.966)
  local copies, waits for them, and re-layouts: 75.1 us -> 45.3 us
    pallas_call x0 -> x2, Pallas kernels: none -> 18.5 us  [attention_call(): pl.pallas_call(kernel, grid=(rows // block,), in_specs=[by_row(a.shape[1]...]
    unnamed x257 -> x215, local copies, waits for them, and re-layouts: 28 us -> 14.9 us
    pallas_call x4, Pallas kernels: 156 us -> 144 us  [run_experts(): pl.pallas_call(functools.partial(experts_kernel, counts, steps, x_size),...]
    all_to_all x1, waiting for transfers between devices: 9.29 us -> 1.71 us  [body(): second_pieces = lax.all_to_all(second_sum, 'z', 0, 0, tiled=True)]
    convert_element_type x18 -> x20, other arithmetic: 36.3 us -> 42.8 us  [plus(): return (first.astype(F32) + second.astype(F32)).astype(kind)]
  transfers between devices with their start and end apart: 106 -> 106, of which waited for: 32 -> 35; matrix products, arithmetic and copies ran while one was open for 21% -> 17% of each run, Pallas kernels for 36% -> 38%
where the time goes in v4:
time: 732 us; the launch traced here: 726 us
  Pallas kernels  276 us (38%)
  waiting for transfers between devices  176 us (24%)
  starting transfers between devices  112 us (15%)
  other arithmetic  90.7 us (12%)
  local copies, waits for them, and re-layouts  45.3 us (6%)
  matrix products  23.4 us (3%)
    ppermute x102, waiting for transfers between devices, ring_step(): return lax.ppermute(array, axis, [(i, (i + 1) % size) for i in range(size)])  172 us
    pallas_call x4, Pallas kernels, run_experts(): pl.pallas_call(functools.partial(experts_kernel, counts, steps, x_size),...  144 us
    ppermute x102, starting transfers between devices, ring_step(): return lax.ppermute(array, axis, [(i, (i + 1) % size) for i in range(size)])  94 us
    pallas_call x3, Pallas kernels, expert_grads(): pl.pallas_call(functools.partial(expert_grads_kernel, len(whole), len(col...  76.9 us
    convert_element_type x20, other arithmetic, plus(): return (first.astype(F32) + second.astype(F32)).astype(kind)  42.8 us
    dot_general x12, matrix products, dot(): lax.dot_general(left, right, (dims, ((), ())), preferred_element_type=F32)  23.4 us
    pallas_call x2, Pallas kernels, attention_call(): pl.pallas_call(kernel, grid=(rows // block,), in_specs=[by_row(a.shape[1]...  18.5 us
    pallas_call x4, Pallas kernels, move(): pl.pallas_call(functools.partial(move_kernel, moves, len(sources), len(sh...  17.1 us
  transfers between devices with their start and end apart: 106, of which 35 were waited for; matrix products, arithmetic and copies ran while one was open for 17% of the time, Pallas kernels for 38%

profile of v4, /device:TPU:1, one launch (start us, length us, event | category | flops | bytes accessed | tf_op | source)
XLA Modules:
  0.0 725.5 jit_solution(15422387064842853329)
XLA Ops:
  15.8 4.5 pack_experts.2
  20.3 4.6 pack_experts.3
  24.9 6.4 collective-permute-done.2
  32.5 10.6 %collective-permute-done.8 = bf16[2,48,2176]{2,1,0:T(8,128)(2,1)S(1)} collective-permute-done((bf16[2,48,2176]{2,1,0:T(8,128)(2,1)S(1)}, bf16[2,48,2176]{2,1,0:T(8,128)(2,1)S(1)}, u32[]{:S(2)}, u32[]{:S(2)}) %collective-permute-start.8) | collective-permute-done | bytes 417824 | tf_op jit(solution)/shard_map/ppermute | solution.py:40
  44.9 7.8 %collective-permute-done.7.refs_12_ = bf16[2,2,48,1024]{3,2,1,0:T(8,128)(2,1)S(1)} collective-permute-done((bf16[2,2,48,1024]{3,2,1,0:T(8,128)(2,1)S(1)}, bf16[2,2,48,1024]{3,2,1,0:T(8,128)(2,1)S(1)}, u32[]{:S(2)}, u32[]{:S(2)}) %collective-permute-start.7) | collective-permute-done | bytes 393248 | tf_op jit(solution)/shard_map/ppermute | solution.py:40
  52.7 13.2 %collective-permute-done.6.refs_1_ = bf16[2,2,48,1152]{3,2,1,0:T(8,128)(2,1)S(1)} collective-permute-done((bf16[2,2,48,1152]{3,2,1,0:T(8,128)(2,1)S(1)}, bf16[2,2,48,1152]{3,2,1,0:T(8,128)(2,1)S(1)}, u32[]{:S(2)}, u32[]{:S(2)}) %collective-permute-start.6) | collective-permute-done | bytes 442400 | tf_op jit(solution)/shard_map/ppermute | solution.py:40
  66.7 4.6 all-to-all-start
  76.0 6.9 collective-permute-done.13.refs_9_
  82.9 8.4 %collective-permute-done.14.refs_13_ = bf16[2,2,48,1024]{3,2,1,0:T(8,128)(2,1)} collective-permute-done((bf16[2,2,48,1024]{3,2,1,0:T(8,128)(2,1)}, bf16[2,2,48,1024]{3,2,1,0:T(8,128)(2,1)}, u32[]{:S(2)}, u32[]{:S(2)}) %collective-permute-start.14) | collective-permute-done | bytes 393248 | tf_op jit(solution)/shard_map/ppermute | solution.py:40
  95.3 6.9 collective-permute-done.16.refs_14_
  106.6 4.2 collective-permute-done.19.refs_11_
  110.7 8.0 %collective-permute-done.20.refs_15_ = bf16[2,2,48,1024]{3,2,1,0:T(8,128)(2,1)S(1)} collective-permute-done((bf16[2,2,48,1024]{3,2,1,0:T(8,128)(2,1)S(1)}, bf16[2,2,48,1024]{3,2,1,0:T(8,128)(2,1)S(1)}, u32[]{:S(2)}, u32[]{:S(2)}) %collective-permute-start.20) | collective-permute-done | bytes 393248 | tf_op jit(solution)/shard_map/ppermute | solution.py:40
  120.4 4.7 all-to-all-start.1
  125.1 5.9 place_weights.1
  141.2 4.8 collective-permute-start.22
  151.3 6.2 attention.1
  157.5 3.1 fusion.73
  160.6 4.5 collective-permute-done.24.refs_5_
  165.2 9.1 %collective-permute-done.21.refs_9_ = bf16[4,192,1280]{2,1,0:T(8,128)(2,1)} collective-permute-done((bf16[4,192,1280]{2,1,0:T(8,128)(2,1)}, bf16[4,192,1280]{2,1,0:T(8,128)(2,1)}, u32[]{:S(2)}, u32[]{:S(2)}) %collective-permute-start.21) | collective-permute-done | bytes 1966112 | tf_op jit(solution)/shard_map/ppermute | solution.py:40
  175.9 5.8 collective-permute-start.25
  201.3 28.0 %collective-permute-done.30.refs_11_ = bf16[4,192,1280]{2,1,0:T(8,128)(2,1)} collective-permute-done((bf16[4,192,1280]{2,1,0:T(8,128)(2,1)}, bf16[4,192,1280]{2,1,0:T(8,128)(2,1)}, u32[]{:S(2)}, u32[]{:S(2)}) %collective-permute-start.30) | collective-permute-done | bytes 1966112 | tf_op jit(solution)/shard_map/ppermute | solution.py:40
  234.1 36.2 %experts.4 = (bf16[2,256,1536]{2,1,0:T(8,128)(2,1)}, bf16[2,256,1536]{2,1,0:T(8,128)(2,1)}, bf16[2,256,1536]{2,1,0:T(8,128)(2,1)}, bf16[2,256,1536]{2,1,0:T(8,12...) custom-call(s32[3]{0:T(128)} %pad_add_fusion.2.place_ref, ...), custom_call_target="tpu_custom_call" | custom-call | flops 24159191040 | bytes 31457280 | tf_op jit(solution)/shard_map/experts/pallas_call | solution.py:344
  279.4 36.1 %experts.5 = (bf16[2,256,1536]{2,1,0:T(8,128)(2,1)}, bf16[2,256,1536]{2,1,0:T(8,128)(2,1)}, bf16[2,256,1536]{2,1,0:T(8,128)(2,1)}, bf16[2,256,1536]{2,1,0:T(8,12...) custom-call(s32[3]{0:T(128)} %pad_add_fusion.2.place_ref, ...), custom_call_target="tpu_custom_call" | custom-call | flops 24159191040 | bytes 31457280 | tf_op jit(solution)/shard_map/experts/pallas_call | solution.py:344
  317.2 3.3 fusion.15
  327.3 36.1 %experts.6 = (bf16[2,256,1536]{2,1,0:T(8,128)(2,1)}, bf16[2,256,1536]{2,1,0:T(8,128)(2,1)}, bf16[2,256,1536]{2,1,0:T(8,128)(2,1)}, bf16[2,256,1536]{2,1,0:T(8,12...) custom-call(s32[3]{0:T(128)} %pad_add_fusion.2.place_ref, ...), custom_call_target="tpu_custom_call" | custom-call | flops 24159191040 | bytes 31457280 | tf_op jit(solution)/shard_map/experts/pallas_call | solution.py:344
  364.9 3.6 fusion.23
  378.1 36.0 %experts.7 = (bf16[2,256,1536]{2,1,0:T(8,128)(2,1)}, bf16[2,256,1536]{2,1,0:T(8,128)(2,1)}, bf16[2,256,1536]{2,1,0:T(8,128)(2,1)}, bf16[2,256,1536]{2,1,0:T(8,12...) custom-call(s32[3]{0:T(128)} %pad_add_fusion.2.place_ref, ...), custom_call_target="tpu_custom_call" | custom-call | flops 24159191040 | bytes 31457280 | tf_op jit(solution)/shard_map/experts/pallas_call | solution.py:344
  432.1 25.4 %expert_grads.3 = (bf16[2,192,1280]{2,1,0:T(8,128)(2,1)}, bf16[2,192,1280]{2,1,0:T(8,128)(2,1)}, bf16[2,192,1280]{2,1,0:T(8,128)(2,1)}, bf16[2,192,1280]{2,1,0:T(8,128)(2,1)}) custom-call(s32[2]{0:T(128)} %pad_add_fusion.1.place_ref, bf16[256,1664]{1,0:T(8,128)(2,1)} %concatenate.52.refs_0_, bf16[256,1664]{1,0:T(8,128)(2,1)} %collective-permute-done.28.refs_1_, ...), custom_call_target="tpu_custom_call" | custom-call | flops 16106127360 | bytes 23068672 | tf_op jit(solution)/shard_map/expert_grads/pallas_call | solution.py:443
  459.5 3.7 collective-permute-done.72
  471.6 25.4 %expert_grads.4 = (bf16[2,192,1280]{2,1,0:T(8,128)(2,1)}, bf16[2,192,1280]{2,1,0:T(8,128)(2,1)}, bf16[2,192,1280]{2,1,0:T(8,128)(2,1)}, bf16[2,192,1280]{2,1,0:T(8,128)(2,1)}) custom-call(s32[2]{0:T(128)} %pad_add_fusion.1.place_ref, bf16[256,1664]{1,0:T(8,128)(2,1)} %concatenate.52.refs_0_, bf16[256,1664]{1,0:T(8,128)(2,1)} %collective-permute-done.28.refs_1_, ...), custom_call_target="tpu_custom_call" | custom-call | flops 16106127360 | bytes 23068672 | tf_op jit(solution)/shard_map/expert_grads/pallas_call | solution.py:443
  497.0 6.4 collective-permute-done.74
  529.1 11.8 %collective-permute-done.78 = bf16[256,1536]{1,0:T(8,128)(2,1)S(1)} collective-permute-done((bf16[256,1536]{1,0:T(8,128)(2,1)S(1)}, bf16[256,1536]{1,0:T(8,128)(2,1)S(1)}, u32[]{:S(2)}, u32[]{:S(2)}) %collective-permute-start.78) | collective-permute-done | bytes 786464 | tf_op jit(solution)/shard_map/ppermute | solution.py:40
  542.9 3.6 pick_weights.3
  555.7 4.5 all-to-all-start.2
  560.3 12.3 %attention_back.1 = (bf16[512,1024]{1,0:T(8,128)(2,1)S(1)}, bf16[512,256]{1,0:T(8,128)(2,1)S(1)}) custom-call(bf16[512,768]{1,0:T(8,128)(2,1)S(1)} %get-tuple-element.403.query_ref, bf16[512,256]{1,0:T(8,128)(2,1)S(1)} %get-tuple-element.404.key_ref, bf16[512,256]{1,0:T(8,128)(2,1)S(1)} %copy-done.7, ...), custom_call_target="tpu_custom_call" | custom-call | flops 805306368 | bytes 8388608 | tf_op jit(solution)/shard_map/attention_back/pallas_call | solution.py:580
  574.1 4.2 collective-permute-done.81
  582.7 3.7 collective-permute-start.82
  589.7 3.5 convolution_convert_fusion
  602.1 3.6 pick_weights.4
  607.7 4.0 pick_weights.5
  611.7 3.6 fusion.9
  620.2 3.8 all-to-all-start.3
  624.0 26.1 %expert_grads.5 = (bf16[10,64,1536]{2,1,0:T(8,128)(2,1)}, bf16[10,64,1536]{2,1,0:T(8,128)(2,1)}) custom-call(s32[2]{0:T(128)} %pad_add_fusion.1.place_ref, bf16[256,1536]{1,0:T(8,128)(2,1)} %bitcast.261, bf16[256,1536]{1,0:T(8,128)(2,1)} %collective-permute-done.5.refs_5_.refs_1_, bf16[256,1536]{1,0:T(8,128)(2,1)} %copy-done.97, ...), custom_call_target="tpu_custom_call" | custom-call | flops 16106127360 | bytes 23068672 | tf_op jit(solution)/shard_map/expert_grads/pallas_call | solution.py:443
  656.3 8.3 %collective-permute-done.90 = bf16[4,2,48,640]{3,2,1,0:T(8,128)(2,1)S(1)} collective-permute-done((bf16[4,2,48,640]{3,2,1,0:T(8,128)(2,1)S(1)}, bf16[4,2,48,640]{3,2,1,0:T(8,128)(2,1)S(1)}, u32[]{:S(2)}, u32[]{:S(2)}) %collective-permute-start.90) | collective-permute-done | bytes 491552 | tf_op jit(solution)/shard_map/ppermute | solution.py:40
  678.5 4.9 unpack_experts.2
  705.5 6.2 collective-permute-start.100
  711.7 4.0 convert_add_fusion
  715.7 4.8 unpack_experts.3
  (558 shorter events, 239.5 us)
Async XLA Ops:
  0.7 30.6 %collective-permute-start.4 = (bf16[256,1536]{1,0:T(8,128)(2,1)}, bf16[256,1536]{1,0:T(8,128)(2,1)}, u32[]{:S(2)}, u32[]{:S(2)}) collective-permute-start(bf16[256,1536]{1,0:T(8,128)(2,1)} %bitcast.258), channel_id=1, source_target_pairs={{0,2},{2,4},{4,6},{6,0},{1,3},{3,5},{5,7},{7,1},{8,10},{10,12},{12... | collective-permute-start | bytes 2359304 | tf_op jit(solution)/shard_map/ppermute | solution.py:40
  2.9 28.5 %collective-permute-start.5 = (bf16[256,1536]{1,0:T(8,128)(2,1)}, bf16[256,1536]{1,0:T(8,128)(2,1)}, u32[]{:S(2)}, u32[]{:S(2)}) collective-permute-start(bf16[256,1536]{1,0:T(8,128)(2,1)} %bitcast.259), channel_id=1, source_target_pairs={{0,16},{16,0},{1,17},{17,1},{2,18},{18,2},{3,19},{19,3},{4,20},{20... | collective-permute-start | bytes 2359304 | tf_op jit(solution)/shard_map/ppermute | solution.py:40
  12.3 54.4 %collective-permute-start.10 = (bf16[10,64,1536]{2,1,0:T(8,128)(2,1)}, bf16[10,64,1536]{2,1,0:T(8,128)(2,1)}, u32[]{:S(2)}, u32[]{:S(2)}) collective-permute-start(bf16[10,64,1536]{2,1,0:T(8,128)(2,1)} %refs_12_.3), channel_id=1, source_target_pairs={{0,1},{1,0},{2,3},{3,2},{4,5},{5,4},{6,7},{7,6},{8,9},{9,8},{10,11... | collective-permute-start | bytes 5898248 | tf_op jit(solution)/shard_map/ppermute | solution.py:40
  31.5 34.5 %collective-permute-start.6 = (bf16[2,2,48,1152]{3,2,1,0:T(8,128)(2,1)S(1)}, bf16[2,2,48,1152]{3,2,1,0:T(8,128)(2,1)S(1)}, u32[]{:S(2)}, u32[]{:S(2)}) collective-permute-start(bf16[2,2,48,1152]{3,2,1,0:T(8,128)(2,1)S(1)} %fusion.33.refs_0_), channel_id=1, source_target_pairs={{0,1},{1,0},{2,3},{3,2},{4,5},{5,4},{6,7},{7,6},{8,9},{9,8},{10,11... | collective-permute-start | bytes 1327112 | tf_op jit(solution)/shard_map/ppermute | solution.py:40
  66.7 53.7 %all-to-all-start = ((bf16[4,192,1280]{2,1,0:T(8,128)(2,1)}), bf16[4,192,1280]{2,1,0:T(8,128)(2,1)}, u32[]{:S(2)}, u32[]{:S(2)}) async-start(bf16[4,192,1280]{2,1,0:T(8,128)(2,1)} %pack_experts.2), calls=%async_computation | async-start | bytes 3932160 | tf_op jit(solution)/shard_map/all_to_all | solution.py:696
  120.4 53.8 %all-to-all-start.1 = ((bf16[4,192,1280]{2,1,0:T(8,128)(2,1)}), bf16[4,192,1280]{2,1,0:T(8,128)(2,1)}, u32[]{:S(2)}, u32[]{:S(2)}) async-start(bf16[4,192,1280]{2,1,0:T(8,128)(2,1)} %pack_experts.3), calls=%async_computation.1 | async-start | bytes 3932160 | tf_op jit(solution)/shard_map/all_to_all | solution.py:706
  134.3 39.9 %collective-permute-start.21 = (bf16[4,192,1280]{2,1,0:T(8,128)(2,1)}, bf16[4,192,1280]{2,1,0:T(8,128)(2,1)}, u32[]{:S(2)}, u32[]{:S(2)}) collective-permute-start(bf16[4,192,1280]{2,1,0:T(8,128)(2,1)} %all-to-all-done.refs_8_), channel_id=1, source_target_pairs={{0,1},{1,0},{2,3},{3,2},{4,5},{5,4},{6,7},{7,6},{8,9},{9,8},{10,11... | collective-permute-start | bytes 5898248 | tf_op jit(solution)/shard_map/ppermute | solution.py:40
  184.5 44.7 %collective-permute-start.30 = (bf16[4,192,1280]{2,1,0:T(8,128)(2,1)}, bf16[4,192,1280]{2,1,0:T(8,128)(2,1)}, u32[]{:S(2)}, u32[]{:S(2)}) collective-permute-start(bf16[4,192,1280]{2,1,0:T(8,128)(2,1)} %all-to-all-done.1.refs_10_), channel_id=1, source_target_pairs={{0,1},{1,0},{2,3},{3,2},{4,5},{5,4},{6,7},{7,6},{8,9},{9,8},{10,11... | collective-permute-start | bytes 5898248 | tf_op jit(solution)/shard_map/ppermute | solution.py:40
  198.6 30.6 %collective-permute-start.28 = (bf16[256,1664]{1,0:T(8,128)(2,1)}, bf16[256,1664]{1,0:T(8,128)(2,1)}, u32[]{:S(2)}, u32[]{:S(2)}) collective-permute-start(bf16[256,1664]{1,0:T(8,128)(2,1)} %concatenate.52.refs_0_), channel_id=1, source_target_pairs={{0,16},{16,0},{1,17},{17,1},{2,18},{18,2},{3,19},{19,3},{4,20},{20... | collective-permute-start | bytes 2555912 | tf_op jit(solution)/shard_map/ppermute | solution.py:40
  198.9 30.3 %collective-permute-start.29 = (bf16[256,1664]{1,0:T(8,128)(2,1)}, bf16[256,1664]{1,0:T(8,128)(2,1)}, u32[]{:S(2)}, u32[]{:S(2)}) collective-permute-start(bf16[256,1664]{1,0:T(8,128)(2,1)} %concatenate.52.refs_0_), channel_id=1, source_target_pairs={{0,2},{2,4},{4,6},{6,0},{1,3},{3,5},{5,7},{7,1},{8,10},{10,12},{12... | collective-permute-start | bytes 2555912 | tf_op jit(solution)/shard_map/ppermute | solution.py:40
  200.3 28.9 %collective-permute-start.31 = (bf16[256,1664]{1,0:T(8,128)(2,1)}, bf16[256,1664]{1,0:T(8,128)(2,1)}, u32[]{:S(2)}, u32[]{:S(2)}) collective-permute-start(bf16[256,1664]{1,0:T(8,128)(2,1)} %concatenate.52.refs_0_), channel_id=1, source_target_pairs={{0,8},{8,0},{1,9},{9,1},{2,10},{10,2},{3,11},{11,3},{4,12},{12,4},... | collective-permute-start | bytes 2555912 | tf_op jit(solution)/shard_map/ppermute | solution.py:40
  230.7 39.5 %collective-permute-start.34 = (bf16[256,1536]{1,0:T(8,128)(2,1)}, bf16[256,1536]{1,0:T(8,128)(2,1)}, u32[]{:S(2)}, u32[]{:S(2)}) collective-permute-start(bf16[256,1536]{1,0:T(8,128)(2,1)} %collective-permute-done.4.refs_4_), channel_id=1, source_target_pairs={{0,2},{2,4},{4,6},{6,0},{1,3},{3,5},{5,7},{7,1},{8,10},{10,12},{12... | collective-permute-start | bytes 2359304 | tf_op jit(solution)/shard_map/ppermute | solution.py:40
  232.2 38.1 %collective-permute-start.33 = (bf16[256,1664]{1,0:T(8,128)(2,1)}, bf16[256,1664]{1,0:T(8,128)(2,1)}, u32[]{:S(2)}, u32[]{:S(2)}) collective-permute-start(bf16[256,1664]{1,0:T(8,128)(2,1)} %collective-permute-done.29.refs_0_.refs_4_), channel_id=1, source_target_pairs={{0,2},{2,4},{4,6},{6,0},{1,3},{3,5},{5,7},{7,1},{8,10},{10,12},{12... | collective-permute-start | bytes 2555912 | tf_op jit(solution)/shard_map/ppermute | solution.py:40
  233.9 36.4 %collective-permute-start.35 = (bf16[256,1664]{1,0:T(8,128)(2,1)}, bf16[256,1664]{1,0:T(8,128)(2,1)}, u32[]{:S(2)}, u32[]{:S(2)}) collective-permute-start(bf16[256,1664]{1,0:T(8,128)(2,1)} %collective-permute-done.29.refs_0_.refs_4_), channel_id=1, source_target_pairs={{0,16},{16,0},{1,17},{17,1},{2,18},{18,2},{3,19},{19,3},{4,20},{20... | collective-permute-start | bytes 2555912 | tf_op jit(solution)/shard_map/ppermute | solution.py:40
  271.8 43.7 %collective-permute-start.40 = (bf16[256,1536]{1,0:T(8,128)(2,1)}, bf16[256,1536]{1,0:T(8,128)(2,1)}, u32[]{:S(2)}, u32[]{:S(2)}) collective-permute-start(bf16[256,1536]{1,0:T(8,128)(2,1)} %collective-permute-done.34.refs_4_.refs_8_), channel_id=1, source_target_pairs={{0,16},{16,0},{1,17},{17,1},{2,18},{18,2},{3,19},{19,3},{4,20},{20... | collective-permute-start | bytes 2359304 | tf_op jit(solution)/shard_map/ppermute | solution.py:40
  273.0 42.4 %collective-permute-start.41 = (bf16[256,1536]{1,0:T(8,128)(2,1)}, bf16[256,1536]{1,0:T(8,128)(2,1)}, u32[]{:S(2)}, u32[]{:S(2)}) collective-permute-start(bf16[256,1536]{1,0:T(8,128)(2,1)} %collective-permute-done.34.refs_4_.refs_8_), channel_id=1, source_target_pairs={{0,2},{2,4},{4,6},{6,0},{1,3},{3,5},{5,7},{7,1},{8,10},{10,12},{12... | collective-permute-start | bytes 2359304 | tf_op jit(solution)/shard_map/ppermute | solution.py:40
  275.8 39.6 %collective-permute-start.39 = (bf16[256,1664]{1,0:T(8,128)(2,1)}, bf16[256,1664]{1,0:T(8,128)(2,1)}, u32[]{:S(2)}, u32[]{:S(2)}) collective-permute-start(bf16[256,1664]{1,0:T(8,128)(2,1)} %collective-permute-done.33.refs_0_.refs_8_), channel_id=1, source_target_pairs={{0,2},{2,4},{4,6},{6,0},{1,3},{3,5},{5,7},{7,1},{8,10},{10,12},{12... | collective-permute-start | bytes 2555912 | tf_op jit(solution)/shard_map/ppermute | solution.py:40
  277.2 38.3 %collective-permute-start.43 = (bf16[256,1664]{1,0:T(8,128)(2,1)}, bf16[256,1664]{1,0:T(8,128)(2,1)}, u32[]{:S(2)}, u32[]{:S(2)}) collective-permute-start(bf16[256,1664]{1,0:T(8,128)(2,1)} %collective-permute-done.33.refs_0_.refs_8_), channel_id=1, source_target_pairs={{0,16},{16,0},{1,17},{17,1},{2,18},{18,2},{3,19},{19,3},{4,20},{20... | collective-permute-start | bytes 2555912 | tf_op jit(solution)/shard_map/ppermute | solution.py:40
  278.4 37.1 %collective-permute-start.42 = (bf16[2,256,1536]{2,1,0:T(8,128)(2,1)}, bf16[2,256,1536]{2,1,0:T(8,128)(2,1)}, u32[]{:S(2)}, u32[]{:S(2)}) collective-permute-start(bf16[2,256,1536]{2,1,0:T(8,128)(2,1)} %get-tuple-element.461), channel_id=1, source_target_pairs={{0,8},{8,0},{1,9},{9,1},{2,10},{10,2},{3,11},{11,3},{4,12},{12,4},... | collective-permute-start | bytes 4718600 | tf_op jit(solution)/shard_map/ppermute | solution.py:40
  322.7 40.7 %collective-permute-start.50 = (bf16[256,1536]{1,0:T(8,128)(2,1)}, bf16[256,1536]{1,0:T(8,128)(2,1)}, u32[]{:S(2)}, u32[]{:S(2)}) collective-permute-start(bf16[256,1536]{1,0:T(8,128)(2,1)} %collective-permute-done.40.refs_5_.refs_9_), channel_id=1, source_target_pairs={{0,2},{2,4},{4,6},{6,0},{1,3},{3,5},{5,7},{7,1},{8,10},{10,12},{12... | collective-permute-start | bytes 2359304 | tf_op jit(solution)/shard_map/ppermute | solution.py:40
  323.9 39.9 %collective-permute-start.51 = (bf16[256,1536]{1,0:T(8,128)(2,1)}, bf16[256,1536]{1,0:T(8,128)(2,1)}, u32[]{:S(2)}, u32[]{:S(2)}) collective-permute-start(bf16[256,1536]{1,0:T(8,128)(2,1)} %collective-permute-done.41.refs_4_.refs_12_), channel_id=1, source_target_pairs={{0,8},{8,0},{1,9},{9,1},{2,10},{10,2},{3,11},{11,3},{4,12},{12,4},... | collective-permute-start | bytes 2359304 | tf_op jit(solution)/shard_map/ppermute | solution.py:40
  324.2 39.6 %collective-permute-start.52 = (bf16[2,256,1536]{2,1,0:T(8,128)(2,1)}, bf16[2,256,1536]{2,1,0:T(8,128)(2,1)}, u32[]{:S(2)}, u32[]{:S(2)}) collective-permute-start(bf16[2,256,1536]{2,1,0:T(8,128)(2,1)} %get-tuple-element.483), channel_id=1, source_target_pairs={{0,8},{8,0},{1,9},{9,1},{2,10},{10,2},{3,11},{11,3},{4,12},{12,4},... | collective-permute-start | bytes 4718600 | tf_op jit(solution)/shard_map/ppermute | solution.py:40
  324.4 39.4 %collective-permute-start.53 = (bf16[256,1664]{1,0:T(8,128)(2,1)}, bf16[256,1664]{1,0:T(8,128)(2,1)}, u32[]{:S(2)}, u32[]{:S(2)}) collective-permute-start(bf16[256,1664]{1,0:T(8,128)(2,1)} %collective-permute-done.39.refs_0_.refs_12_), channel_id=1, source_target_pairs={{0,16},{16,0},{1,17},{17,1},{2,18},{18,2},{3,19},{19,3},{4,20},{20... | collective-permute-start | bytes 2555912 | tf_op jit(solution)/shard_map/ppermute | solution.py:40
  326.1 37.7 %collective-permute-start.49 = (bf16[256,1536]{1,0:T(8,128)(2,1)}, bf16[256,1536]{1,0:T(8,128)(2,1)}, u32[]{:S(2)}, u32[]{:S(2)}) collective-permute-start(bf16[256,1536]{1,0:T(8,128)(2,1)} %fusion.13), channel_id=1, source_target_pairs={{0,16},{16,0},{1,17},{17,1},{2,18},{18,2},{3,19},{19,3},{4,20},{20... | collective-permute-start | bytes 2359304 | tf_op jit(solution)/shard_map/ppermute | solution.py:40
  363.4 50.7 %collective-permute-start.59 = (bf16[256,1536]{1,0:T(8,128)(2,1)S(1)}, bf16[256,1536]{1,0:T(8,128)(2,1)}, u32[]{:S(2)}, u32[]{:S(2)}) collective-permute-start(bf16[256,1536]{1,0:T(8,128)(2,1)S(1)} %get-tuple-element.774), channel_id=1, source_target_pairs={{0,16},{16,0},{1,17},{17,1},{2,18},{18,2},{3,19},{19,3},{4,20},{20... | collective-permute-start | bytes 2359304 | tf_op jit(solution)/shard_map/ppermute | solution.py:40
  373.9 40.3 %collective-permute-start.60 = (bf16[2,256,1536]{2,1,0:T(8,128)(2,1)}, bf16[2,256,1536]{2,1,0:T(8,128)(2,1)}, u32[]{:S(2)}, u32[]{:S(2)}) collective-permute-start(bf16[2,256,1536]{2,1,0:T(8,128)(2,1)} %get-tuple-element.506), channel_id=1, source_target_pairs={{0,8},{8,0},{1,9},{9,1},{2,10},{10,2},{3,11},{11,3},{4,12},{12,4},... | collective-permute-start | bytes 4718600 | tf_op jit(solution)/shard_map/ppermute | solution.py:40
  374.3 39.8 %collective-permute-start.61 = (bf16[256,1536]{1,0:T(8,128)(2,1)}, bf16[256,1536]{1,0:T(8,128)(2,1)}, u32[]{:S(2)}, u32[]{:S(2)}) collective-permute-start(bf16[256,1536]{1,0:T(8,128)(2,1)} %fusion.19), channel_id=1, source_target_pairs={{0,16},{16,0},{1,17},{17,1},{2,18},{18,2},{3,19},{19,3},{4,20},{20... | collective-permute-start | bytes 2359304 | tf_op jit(solution)/shard_map/ppermute | solution.py:40
  375.6 38.6 %collective-permute-start.62 = (bf16[256,1536]{1,0:T(8,128)(2,1)}, bf16[256,1536]{1,0:T(8,128)(2,1)}, u32[]{:S(2)}, u32[]{:S(2)}) collective-permute-start(bf16[256,1536]{1,0:T(8,128)(2,1)} %add_convert_fusion.27), channel_id=1, source_target_pairs={{0,2},{2,4},{4,6},{6,0},{1,3},{3,5},{5,7},{7,1},{8,10},{10,12},{12... | collective-permute-start | bytes 2359304 | tf_op jit(solution)/shard_map/ppermute | solution.py:40
  377.9 37.6 %collective-permute-start.58 = (bf16[256,1536]{1,0:T(8,128)(2,1)}, bf16[256,1536]{1,0:T(8,128)(2,1)}, u32[]{:S(2)}, u32[]{:S(2)}) collective-permute-start(bf16[256,1536]{1,0:T(8,128)(2,1)} %fusion.18), channel_id=1, source_target_pairs={{0,16},{16,0},{1,17},{17,1},{2,18},{18,2},{3,19},{19,3},{4,20},{20... | collective-permute-start | bytes 2359304 | tf_op jit(solution)/shard_map/ppermute | solution.py:40
  428.7 29.8 %collective-permute-start.65 = (bf16[256,1536]{1,0:T(8,128)(2,1)}, bf16[256,1536]{1,0:T(8,128)(2,1)}, u32[]{:S(2)}, u32[]{:S(2)}) collective-permute-start(bf16[256,1536]{1,0:T(8,128)(2,1)} %get-tuple-element.538), channel_id=1, source_target_pairs={{0,16},{16,0},{1,17},{17,1},{2,18},{18,2},{3,19},{19,3},{4,20},{20... | collective-permute-start | bytes 2359304 | tf_op jit(solution)/shard_map/ppermute | solution.py:40
  428.9 29.5 %collective-permute-start.66 = (bf16[256,1536]{1,0:T(8,128)(2,1)}, bf16[256,1536]{1,0:T(8,128)(2,1)}, u32[]{:S(2)}, u32[]{:S(2)}) collective-permute-start(bf16[256,1536]{1,0:T(8,128)(2,1)} %add_convert_fusion.23), channel_id=1, source_target_pairs={{0,2},{2,4},{4,6},{6,0},{1,3},{3,5},{5,7},{7,1},{8,10},{10,12},{12... | collective-permute-start | bytes 2359304 | tf_op jit(solution)/shard_map/ppermute | solution.py:40
  430.1 28.3 %collective-permute-start.67 = (bf16[2,256,1536]{2,1,0:T(8,128)(2,1)}, bf16[2,256,1536]{2,1,0:T(8,128)(2,1)}, u32[]{:S(2)}, u32[]{:S(2)}) collective-permute-start(bf16[2,256,1536]{2,1,0:T(8,128)(2,1)} %get-tuple-element.540), channel_id=1, source_target_pairs={{0,8},{8,0},{1,9},{9,1},{2,10},{10,2},{3,11},{11,3},{4,12},{12,4},... | collective-permute-start | bytes 4718600 | tf_op jit(solution)/shard_map/ppermute | solution.py:40
  430.8 26.7 %collective-permute-start.68 = (f32[4,40,256]{2,1,0:T(8,128)S(1)}, f32[4,40,256]{2,1,0:T(8,128)}, u32[]{:S(2)}, u32[]{:S(2)}) collective-permute-start(f32[4,40,256]{2,1,0:T(8,128)S(1)} %slice_bitcast_fusion.6), channel_id=1, source_target_pairs={{0,16},{16,0},{1,17},{17,1},{2,18},{18,2},{3,19},{19,3},{4,20},{20... | collective-permute-start | bytes 491528 | tf_op jit(solution)/shard_map/ppermute | solution.py:40
  466.0 38.1 %collective-permute-start.69 = (bf16[256,1536]{1,0:T(8,128)(2,1)}, bf16[256,1536]{1,0:T(8,128)(2,1)}, u32[]{:S(2)}, u32[]{:S(2)}) collective-permute-start(bf16[256,1536]{1,0:T(8,128)(2,1)} %add_convert_fusion.15), channel_id=1, source_target_pairs={{0,2},{2,4},{4,6},{6,0},{1,3},{3,5},{5,7},{7,1},{8,10},{10,12},{12... | collective-permute-start | bytes 2359304 | tf_op jit(solution)/shard_map/ppermute | solution.py:40
  466.3 37.8 %collective-permute-start.70 = (bf16[256,1536]{1,0:T(8,128)(2,1)}, bf16[256,1536]{1,0:T(8,128)(2,1)}, u32[]{:S(2)}, u32[]{:S(2)}) collective-permute-start(bf16[256,1536]{1,0:T(8,128)(2,1)} %get-tuple-element.564), channel_id=1, source_target_pairs={{0,16},{16,0},{1,17},{17,1},{2,18},{18,2},{3,19},{19,3},{4,20},{20... | collective-permute-start | bytes 2359304 | tf_op jit(solution)/shard_map/ppermute | solution.py:40
  466.7 37.4 %collective-permute-start.71 = (bf16[256,1536]{1,0:T(8,128)(2,1)}, bf16[256,1536]{1,0:T(8,128)(2,1)}, u32[]{:S(2)}, u32[]{:S(2)}) collective-permute-start(bf16[256,1536]{1,0:T(8,128)(2,1)} %add_convert_fusion.17), channel_id=1, source_target_pairs={{0,2},{2,4},{4,6},{6,0},{1,3},{3,5},{5,7},{7,1},{8,10},{10,12},{12... | collective-permute-start | bytes 2359304 | tf_op jit(solution)/shard_map/ppermute | solution.py:40
  467.5 36.6 %collective-permute-start.75 = (bf16[2,192,1280]{2,1,0:T(8,128)(2,1)}, bf16[2,192,1280]{2,1,0:T(8,128)(2,1)}, u32[]{:S(2)}, u32[]{:S(2)}) collective-permute-start(bf16[2,192,1280]{2,1,0:T(8,128)(2,1)} %get-tuple-element.567), channel_id=1, source_target_pairs={{0,1},{1,0},{2,3},{3,2},{4,5},{5,4},{6,7},{7,6},{8,9},{9,8},{10,11... | collective-permute-start | bytes 2949128 | tf_op jit(solution)/shard_map/ppermute | solution.py:40
  469.0 34.5 %collective-permute-start.74 = (f32[40,256]{1,0:T(8,128)S(1)}, f32[40,256]{1,0:T(8,128)S(1)}, u32[]{:S(2)}, u32[]{:S(2)}) collective-permute-start(f32[40,256]{1,0:T(8,128)S(1)} %bitcast_add_fusion.3), channel_id=1, source_target_pairs={{0,2},{2,4},{4,6},{6,0},{1,3},{3,5},{5,7},{7,1},{8,10},{10,12},{12... | collective-permute-start | bytes 122888 | tf_op jit(solution)/shard_map/ppermute | solution.py:40
  551.6 26.7 %collective-permute-start.81 = (bf16[2,4,48,1536]{3,2,1,0:T(8,128)(2,1)}, bf16[2,4,48,1536]{3,2,1,0:T(8,128)(2,1)}, u32[]{:S(2)}, u32[]{:S(2)}) collective-permute-start(bf16[2,4,48,1536]{3,2,1,0:T(8,128)(2,1)} %get-tuple-element.612), channel_id=1, source_target_pairs={{0,16},{16,0},{1,17},{17,1},{2,18},{18,2},{3,19},{19,3},{4,20},{20... | collective-permute-start | bytes 3538952 | tf_op jit(solution)/shard_map/ppermute | solution.py:40
  553.8 43.0 %collective-permute-start.83 = (bf16[2,192,1280]{2,1,0:T(8,128)(2,1)}, bf16[2,192,1280]{2,1,0:T(8,128)(2,1)}, u32[]{:S(2)}, u32[]{:S(2)}) collective-permute-start(bf16[2,192,1280]{2,1,0:T(8,128)(2,1)} %get-tuple-element.616), channel_id=1, source_target_pairs={{0,1},{1,0},{2,3},{3,2},{4,5},{5,4},{6,7},{7,6},{8,9},{9,8},{10,11... | collective-permute-start | bytes 2949128 | tf_op jit(solution)/shard_map/ppermute | solution.py:40
  554.5 42.2 %collective-permute-start.84 = (bf16[256,1536]{1,0:T(8,128)(2,1)}, bf16[256,1536]{1,0:T(8,128)(2,1)}, u32[]{:S(2)}, u32[]{:S(2)}) collective-permute-start(bf16[256,1536]{1,0:T(8,128)(2,1)} %add_convert_fusion.8), channel_id=1, source_target_pairs={{0,2},{2,4},{4,6},{6,0},{1,3},{3,5},{5,7},{7,1},{8,10},{10,12},{12... | collective-permute-start | bytes 2359304 | tf_op jit(solution)/shard_map/ppermute | solution.py:40
  554.5 60.9 %collective-permute-start.85 = (bf16[256,1536]{1,0:T(8,128)(2,1)}, bf16[256,1536]{1,0:T(8,128)(2,1)}, u32[]{:S(2)}, u32[]{:S(2)}) collective-permute-start(bf16[256,1536]{1,0:T(8,128)(2,1)} %get-tuple-element.626), channel_id=1, source_target_pairs={{0,16},{16,0},{1,17},{17,1},{2,18},{18,2},{3,19},{19,3},{4,20},{20... | collective-permute-start | bytes 2359304 | tf_op jit(solution)/shard_map/ppermute | solution.py:40
  555.7 62.5 %all-to-all-start.2 = ((bf16[4,192,1280]{2,1,0:T(8,128)(2,1)}), bf16[4,192,1280]{2,1,0:T(8,128)(2,1)}, u32[]{:S(2)}, u32[]{:S(2)}) async-start(bf16[4,192,1280]{2,1,0:T(8,128)(2,1)} %pad_maximum_fusion), calls=%async_computation.2 | async-start | bytes 3932160 | tf_op jit(solution)/shard_map/all_to_all | solution.py:930
  594.7 57.6 %collective-permute-start.88 = (bf16[4,48,1536]{2,1,0:T(8,128)(2,1)}, bf16[4,48,1536]{2,1,0:T(8,128)(2,1)}, u32[]{:S(2)}, u32[]{:S(2)}) collective-permute-start(bf16[4,48,1536]{2,1,0:T(8,128)(2,1)} %get-tuple-element.777), channel_id=1, source_target_pairs={{0,1},{1,0},{2,3},{3,2},{4,5},{5,4},{6,7},{7,6},{8,9},{9,8},{10,11... | collective-permute-start | bytes 1769480 | tf_op jit(solution)/shard_map/ppermute | solution.py:40
  618.2 33.8 %collective-permute-start.86 = (bf16[2,4,2,48,768]{4,3,2,1,0:T(8,128)(2,1)}, bf16[2,4,2,48,768]{4,3,2,1,0:T(8,128)(2,1)S(1)}, u32[]{:S(2)}, u32[]{:S(2)}) collective-permute-start(bf16[2,4,2,48,768]{4,3,2,1,0:T(8,128)(2,1)} %get-tuple-element.654), channel_id=1, source_target_pairs={{0,16},{16,0},{1,17},{17,1},{2,18},{18,2},{3,19},{19,3},{4,20},{20... | collective-permute-start | bytes 3538952 | tf_op jit(solution)/shard_map/ppermute | solution.py:40
  619.4 30.7 %collective-permute-start.87 = (bf16[2,4,2,48,640]{4,3,2,1,0:T(8,128)(2,1)}, bf16[2,4,2,48,640]{4,3,2,1,0:T(8,128)(2,1)}, u32[]{:S(2)}, u32[]{:S(2)}) collective-permute-start(bf16[2,4,2,48,640]{4,3,2,1,0:T(8,128)(2,1)} %get-tuple-element.656), channel_id=1, source_target_pairs={{0,1},{1,0},{2,3},{3,2},{4,5},{5,4},{6,7},{7,6},{8,9},{9,8},{10,11... | collective-permute-start | bytes 2949128 | tf_op jit(solution)/shard_map/ppermute | solution.py:40
  620.2 48.7 %all-to-all-start.3 = ((bf16[4,192,1280]{2,1,0:T(8,128)(2,1)}), bf16[4,192,1280]{2,1,0:T(8,128)(2,1)S(1)}, u32[]{:S(2)}, u32[]{:S(2)}) async-start(bf16[4,192,1280]{2,1,0:T(8,128)(2,1)} %pad_maximum_fusion.1), calls=%async_computation.3 | async-start | bytes 3932160 | tf_op jit(solution)/shard_map/all_to_all | solution.py:981
  653.4 58.2 %collective-permute-start.101 = (bf16[10,64,1536]{2,1,0:T(8,128)(2,1)}, bf16[10,64,1536]{2,1,0:T(8,128)(2,1)}, u32[]{:S(2)}, u32[]{:S(2)}) collective-permute-start(bf16[10,64,1536]{2,1,0:T(8,128)(2,1)} %get-tuple-element.686), channel_id=1, source_target_pairs={{0,1},{1,0},{2,3},{3,2},{4,5},{5,4},{6,7},{7,6},{8,9},{9,8},{10,11... | collective-permute-start | bytes 5898248 | tf_op jit(solution)/shard_map/ppermute | solution.py:40
  (159 other events, 1653.5 us)

commit v5 on v4

--- a/solution.py
+++ b/solution.py
@@ -510,15 +510,13 @@
     return jnp.concatenate([rows[:, HEAD_SIZE * h : HEAD_SIZE * (h + 1)] for h in heads], axis=0)
 
 
-def probabilities(query, keys, allowed):
+def masked_scores(query, keys, allowed):
     scores = dot(query, keys, ((1,), (1,))) * (1.0 / math.sqrt(HEAD_SIZE))
-    scores = jnp.where(allowed, scores, -1000000000.0)
-    shifted = jnp.exp(scores - jnp.max(scores, axis=-1, keepdims=True))
-    return shifted / jnp.sum(shifted, axis=-1, keepdims=True)
+    return jnp.where(allowed, scores, -1000000000.0)
 
 
 def attention_kernel(
-    qk_ref, value_ref, cos_ref, sin_ref, column_ref, row_ref, query_ref, key_ref, mixed_ref
+    qk_ref, value_ref, cos_ref, sin_ref, column_ref, row_ref, query_ref, key_ref, mixed_ref, log_ref
 ):
     width = query_ref.shape[1]
     block = query_ref.shape[0]
@@ -526,14 +524,23 @@
     query_ref[...] = rotated[:, :width]
     key_ref[...] = rotated[:, width:]
     allowed = allowed_pairs(column_ref, row_ref)
+    lane = lax.broadcasted_iota(jnp.int32, (block, LANES), 1)
+    logs = jnp.zeros((block, LANES), F32)
     for group in range(key_ref.shape[1] // HEAD_SIZE):
         here = slice(HEAD_SIZE * group, HEAD_SIZE * (group + 1))
         query = group_rows(query_ref[...], group)
-        probs = probabilities(query, key_ref[:, here], allowed)
-        mixed = dot(probs.astype(BF16), value_ref[:, here]).astype(BF16)
+        scores = masked_scores(query, key_ref[:, here], allowed)
+        row_max = jnp.max(scores, axis=-1, keepdims=True)
+        shifted = jnp.exp(scores - row_max)
+        row_total = jnp.sum(shifted, axis=-1, keepdims=True)
+        log_total = row_max + jnp.log(row_total)
+        mixed = dot((shifted / row_total).astype(BF16), value_ref[:, here]).astype(BF16)
         for i in range(QUERY_PER_GROUP):
-            start = HEAD_SIZE * (group * QUERY_PER_GROUP + i)
-            mixed_ref[:, start : start + HEAD_SIZE] = mixed[block * i : block * (i + 1)]
+            head = group * QUERY_PER_GROUP + i
+            rows = slice(block * i, block * (i + 1))
+            mixed_ref[:, HEAD_SIZE * head : HEAD_SIZE * (head + 1)] = mixed[rows]
+            logs = jnp.where(lane == head, log_total[rows], logs)
+    log_ref[...] = logs
 
 
 def attention_back_kernel(
@@ -541,6 +548,7 @@
     key_ref,
     value_ref,
     grad_ref,
+    log_ref,
     cos_ref,
     sin_ref,
     column_ref,
@@ -557,7 +565,9 @@
         here = slice(HEAD_SIZE * group, HEAD_SIZE * (group + 1))
         query = group_rows(query_ref[...], group)
         grad_mixed = group_rows(grad_ref[...], group)
-        probs = probabilities(query, key_ref[:, here], allowed)
+        heads = [group * QUERY_PER_GROUP + i for i in range(QUERY_PER_GROUP)]
+        log_total = jnp.concatenate([log_ref[:, head : head + 1] for head in heads], axis=0)
+        probs = jnp.exp(masked_scores(query, key_ref[:, here], allowed) - log_total)
         grad_probs = dot(grad_mixed, value_ref[:, here], ((1,), (1,)))
         grad_value_ref[:, here] = dot(probs.astype(BF16), grad_mixed, ((0,), (0,))).astype(BF16)
         spread = jnp.sum(probs * grad_probs, axis=-1, keepdims=True)
@@ -582,8 +592,8 @@
         grid=(rows // block,),
         in_specs=[by_row(a.shape[1]) for a in list(arrays) + list(tables[:3])]
         + [pl.BlockSpec((1,) + tables[3].shape[1:], lambda i: (i, 0, 0))],
-        out_specs=[by_row(width) for width in widths],
-        out_shape=[jax.ShapeDtypeStruct((rows, width), BF16) for width in widths],
+        out_specs=[by_row(width) for width, _ in widths],
+        out_shape=[jax.ShapeDtypeStruct((rows, width), kind) for width, kind in widths],
         scratch_shapes=scratch,
         compiler_params=pltpu.CompilerParams(vmem_limit_bytes=VMEM_BYTES // 2),
         cost_estimate=pl.CostEstimate(
@@ -730,10 +740,10 @@
         jnp.broadcast_to(segment.reshape(-1, 1), (blocks * block, block)),
         jnp.broadcast_to(segment[:, None, :], (blocks, 8, block)),
     )
-    query, keys, mixed = attention_call(
+    query, keys, mixed, logs = attention_call(
         attention_kernel,
         [qk_pre, values],
-        [q_width, kv_width, q_width],
+        [(q_width, BF16), (kv_width, BF16), (q_width, BF16), (LANES, F32)],
         tables,
         block,
         [],
@@ -847,7 +857,7 @@
         last_results = parts[:2]
 
     total = plus(moved["step"], grads_sum[2])
-    grads_sum[0] = end_y(grads_c[0], moved["grad_zero"])
+    zero_hop = moved["grad_zero"]
     results_sum[1] = end_y(results_c[1], moved["result_one"])
     spread = jnp.stack(grads_gates).reshape(z_size, 2, y_size, E, count)
     spread = ring_sum([spread[:, 0], spread[:, 1]], "c", F32)
@@ -874,16 +884,18 @@
     grad_hidden, total, results_sum, results_c, first_grads, result_three = sync(
         grad_hidden, total, results_sum, results_c, first_grads, result_three
     )
-    second_grads, step, result_two, result_step, grad_gates, one = sync(
+    second_grads, step, result_two, result_step, grad_gates, one, zero_hop, zero_parts = sync(
         in_grads(1),
         ring_step(total, "z"),
         hops_y(results_c[2]),
         ring_step(results_sum[1], "z"),
         ring_sum([spread[i] for i in range(z_size)], "z", F32),
         ring_step(first_grads[2], "x"),
+        zero_hop,
+        grads_c[0],
     )
     grad_gates = with_layout_constraint(grad_gates, Layout((0, 1))).T
-    grad_experts = plus(step, grads_sum[0], F32)
+    grad_experts = plus(step, end_y(zero_parts, zero_hop), F32)
     result_total = plus(result_step, end_y(results_c[2], result_two))
     grad_experts, first_grads, second_grads, results_c, result_total, result_three = sync(
         grad_experts, first_grads, second_grads, results_c, result_total, result_three
@@ -934,8 +946,8 @@
     result_zero = hops_y(results_c[0])
     grad_qk_pre, grad_value_pre = attention_call(
         attention_back_kernel,
-        [query, keys, values, grad_mixed],
-        [q_width + kv_width, kv_width],
+        [query, keys, values, grad_mixed, logs],
+        [(q_width + kv_width, BF16), (kv_width, BF16)],
         tables,
         block,
         [pltpu.VMEM((block, q_width + kv_width), F32)],

time: 732 us -> 728 us (level)
    unnamed x215 -> x217, local copies, waits for them, and re-layouts: 14.9 us -> 18 us
  transfers between devices with their start and end apart: 106 -> 106, of which waited for: 35 -> 35; matrix products, arithmetic and copies ran while one was open for 17% -> 16% of each run, Pallas kernels for 38% -> 37%
where the time goes in v5:
time: 728 us; the launch traced here: 721 us
  Pallas kernels  273 us (38%)
  waiting for transfers between devices  180 us (25%)
  starting transfers between devices  112 us (15%)
  other arithmetic  85.4 us (12%)
  local copies, waits for them, and re-layouts  45.8 us (6%)
  matrix products  22.5 us (3%)
    ppermute x102, waiting for transfers between devices, ring_step(): return lax.ppermute(array, axis, [(i, (i + 1) % size) for i in range(size)])  176 us
    pallas_call x4, Pallas kernels, run_experts(): pl.pallas_call(functools.partial(experts_kernel, counts, steps, x_size),...  144 us
    ppermute x102, starting transfers between devices, ring_step(): return lax.ppermute(array, axis, [(i, (i + 1) % size) for i in range(size)])  94.7 us
    pallas_call x3, Pallas kernels, expert_grads(): pl.pallas_call(functools.partial(expert_grads_kernel, len(whole), len(col...  77 us
    convert_element_type x20, other arithmetic, plus(): return (first.astype(F32) + second.astype(F32)).astype(kind)  43.3 us
    dot_general x12, matrix products, dot(): lax.dot_general(left, right, (dims, ((), ())), preferred_element_type=F32)  22.5 us
    unnamed x217, local copies, waits for them, and re-layouts  18 us
    pallas_call x4, Pallas kernels, move(): pl.pallas_call(functools.partial(move_kernel, moves, len(sources), len(sh...  17.1 us
  transfers between devices with their start and end apart: 106, of which 35 were waited for; matrix products, arithmetic and copies ran while one was open for 16% of the time, Pallas kernels for 37%

profile of v5, /device:TPU:1, one launch (start us, length us, event | category | flops | bytes accessed | tf_op | source)
XLA Modules:
  0.0 721.3 jit_solution(16735810908510483616)
XLA Ops:
  15.8 4.5 pack_experts.2
  20.3 4.6 pack_experts.3
  24.9 6.4 collective-permute-done.2
  32.5 10.6 %collective-permute-done.8 = bf16[2,48,2176]{2,1,0:T(8,128)(2,1)S(1)} collective-permute-done((bf16[2,48,2176]{2,1,0:T(8,128)(2,1)S(1)}, bf16[2,48,2176]{2,1,0:T(8,128)(2,1)S(1)}, u32[]{:S(2)}, u32[]{:S(2)}) %collective-permute-start.8) | collective-permute-done | bytes 417824 | tf_op jit(solution)/shard_map/ppermute | solution.py:40
  44.9 7.8 %collective-permute-done.7.refs_12_ = bf16[2,2,48,1024]{3,2,1,0:T(8,128)(2,1)S(1)} collective-permute-done((bf16[2,2,48,1024]{3,2,1,0:T(8,128)(2,1)S(1)}, bf16[2,2,48,1024]{3,2,1,0:T(8,128)(2,1)S(1)}, u32[]{:S(2)}, u32[]{:S(2)}) %collective-permute-start.7) | collective-permute-done | bytes 393248 | tf_op jit(solution)/shard_map/ppermute | solution.py:40
  52.7 13.2 %collective-permute-done.6.refs_1_ = bf16[2,2,48,1152]{3,2,1,0:T(8,128)(2,1)S(1)} collective-permute-done((bf16[2,2,48,1152]{3,2,1,0:T(8,128)(2,1)S(1)}, bf16[2,2,48,1152]{3,2,1,0:T(8,128)(2,1)S(1)}, u32[]{:S(2)}, u32[]{:S(2)}) %collective-permute-start.6) | collective-permute-done | bytes 442400 | tf_op jit(solution)/shard_map/ppermute | solution.py:40
  66.7 4.6 all-to-all-start
  76.0 6.9 collective-permute-done.13.refs_9_
  82.9 8.4 %collective-permute-done.14.refs_13_ = bf16[2,2,48,1024]{3,2,1,0:T(8,128)(2,1)} collective-permute-done((bf16[2,2,48,1024]{3,2,1,0:T(8,128)(2,1)}, bf16[2,2,48,1024]{3,2,1,0:T(8,128)(2,1)}, u32[]{:S(2)}, u32[]{:S(2)}) %collective-permute-start.14) | collective-permute-done | bytes 393248 | tf_op jit(solution)/shard_map/ppermute | solution.py:40
  95.3 6.9 collective-permute-done.16.refs_14_
  106.6 4.2 collective-permute-done.19.refs_11_
  110.7 8.0 %collective-permute-done.20.refs_15_ = bf16[2,2,48,1024]{3,2,1,0:T(8,128)(2,1)S(1)} collective-permute-done((bf16[2,2,48,1024]{3,2,1,0:T(8,128)(2,1)S(1)}, bf16[2,2,48,1024]{3,2,1,0:T(8,128)(2,1)S(1)}, u32[]{:S(2)}, u32[]{:S(2)}) %collective-permute-start.20) | collective-permute-done | bytes 393248 | tf_op jit(solution)/shard_map/ppermute | solution.py:40
  120.4 4.7 all-to-all-start.1
  125.1 5.9 place_weights.1
  141.3 4.8 collective-permute-start.22
  151.3 6.2 attention.1
  166.1 8.1 %collective-permute-done.21.refs_9_ = bf16[4,192,1280]{2,1,0:T(8,128)(2,1)} collective-permute-done((bf16[4,192,1280]{2,1,0:T(8,128)(2,1)}, bf16[4,192,1280]{2,1,0:T(8,128)(2,1)}, u32[]{:S(2)}, u32[]{:S(2)}) %collective-permute-start.21) | collective-permute-done | bytes 1966112 | tf_op jit(solution)/shard_map/ppermute | solution.py:40
  175.9 5.8 collective-permute-start.25
  196.8 31.4 %collective-permute-done.30.refs_11_ = bf16[4,192,1280]{2,1,0:T(8,128)(2,1)} collective-permute-done((bf16[4,192,1280]{2,1,0:T(8,128)(2,1)}, bf16[4,192,1280]{2,1,0:T(8,128)(2,1)}, u32[]{:S(2)}, u32[]{:S(2)}) %collective-permute-start.30) | collective-permute-done | bytes 1966112 | tf_op jit(solution)/shard_map/ppermute | solution.py:40
  233.5 36.2 %experts.4 = (bf16[2,256,1536]{2,1,0:T(8,128)(2,1)}, bf16[2,256,1536]{2,1,0:T(8,128)(2,1)}, bf16[2,256,1536]{2,1,0:T(8,128)(2,1)}, bf16[2,256,1536]{2,1,0:T(8,12...) custom-call(s32[3]{0:T(128)} %pad_add_fusion.2.place_ref, ...), custom_call_target="tpu_custom_call" | custom-call | flops 24159191040 | bytes 31457280 | tf_op jit(solution)/shard_map/experts/pallas_call | solution.py:344
  278.8 36.1 %experts.5 = (bf16[2,256,1536]{2,1,0:T(8,128)(2,1)}, bf16[2,256,1536]{2,1,0:T(8,128)(2,1)}, bf16[2,256,1536]{2,1,0:T(8,128)(2,1)}, bf16[2,256,1536]{2,1,0:T(8,12...) custom-call(s32[3]{0:T(128)} %pad_add_fusion.2.place_ref, ...), custom_call_target="tpu_custom_call" | custom-call | flops 24159191040 | bytes 31457280 | tf_op jit(solution)/shard_map/experts/pallas_call | solution.py:344
  316.6 3.5 fusion.15
  326.8 36.1 %experts.6 = (bf16[2,256,1536]{2,1,0:T(8,128)(2,1)}, bf16[2,256,1536]{2,1,0:T(8,128)(2,1)}, bf16[2,256,1536]{2,1,0:T(8,128)(2,1)}, bf16[2,256,1536]{2,1,0:T(8,12...) custom-call(s32[3]{0:T(128)} %pad_add_fusion.2.place_ref, ...), custom_call_target="tpu_custom_call" | custom-call | flops 24159191040 | bytes 31457280 | tf_op jit(solution)/shard_map/experts/pallas_call | solution.py:344
  364.4 3.5 fusion.23
  377.5 36.0 %experts.7 = (bf16[2,256,1536]{2,1,0:T(8,128)(2,1)}, bf16[2,256,1536]{2,1,0:T(8,128)(2,1)}, bf16[2,256,1536]{2,1,0:T(8,128)(2,1)}, bf16[2,256,1536]{2,1,0:T(8,12...) custom-call(s32[3]{0:T(128)} %pad_add_fusion.2.place_ref, ...), custom_call_target="tpu_custom_call" | custom-call | flops 24159191040 | bytes 31457280 | tf_op jit(solution)/shard_map/experts/pallas_call | solution.py:344
  432.0 25.5 %expert_grads.3 = (bf16[2,192,1280]{2,1,0:T(8,128)(2,1)}, bf16[2,192,1280]{2,1,0:T(8,128)(2,1)}, bf16[2,192,1280]{2,1,0:T(8,128)(2,1)}, bf16[2,192,1280]{2,1,0:T(8,128)(2,1)}) custom-call(s32[2]{0:T(128)} %pad_add_fusion.1.place_ref, bf16[256,1664]{1,0:T(8,128)(2,1)} %concatenate.52.refs_0_, bf16[256,1664]{1,0:T(8,128)(2,1)} %collective-permute-done.28.refs_1_, ...), custom_call_target="tpu_custom_call" | custom-call | flops 16106127360 | bytes 23068672 | tf_op jit(solution)/shard_map/expert_grads/pallas_call | solution.py:443
  458.6 3.7 collective-permute-done.72
  470.6 25.5 %expert_grads.4 = (bf16[2,192,1280]{2,1,0:T(8,128)(2,1)}, bf16[2,192,1280]{2,1,0:T(8,128)(2,1)}, bf16[2,192,1280]{2,1,0:T(8,128)(2,1)}, bf16[2,192,1280]{2,1,0:T(8,128)(2,1)}) custom-call(s32[2]{0:T(128)} %pad_add_fusion.1.place_ref, bf16[256,1664]{1,0:T(8,128)(2,1)} %concatenate.52.refs_0_, bf16[256,1664]{1,0:T(8,128)(2,1)} %collective-permute-done.28.refs_1_, ...), custom_call_target="tpu_custom_call" | custom-call | flops 16106127360 | bytes 23068672 | tf_op jit(solution)/shard_map/expert_grads/pallas_call | solution.py:443
  496.2 6.3 collective-permute-done.74
  502.6 3.1 convert_add_fusion.1
  525.4 11.8 %collective-permute-done.78 = bf16[256,1536]{1,0:T(8,128)(2,1)S(1)} collective-permute-done((bf16[256,1536]{1,0:T(8,128)(2,1)S(1)}, bf16[256,1536]{1,0:T(8,128)(2,1)S(1)}, u32[]{:S(2)}, u32[]{:S(2)}) %collective-permute-start.78) | collective-permute-done | bytes 786464 | tf_op jit(solution)/shard_map/ppermute | solution.py:40
  539.2 3.6 pick_weights.3
  551.5 4.5 all-to-all-start.2
  556.0 9.5 %attention_back.1 = (bf16[512,1024]{1,0:T(8,128)(2,1)S(1)}, bf16[512,256]{1,0:T(8,128)(2,1)S(1)}) custom-call(bf16[512,768]{1,0:T(8,128)(2,1)S(1)} %get-tuple-element.407.query_ref, bf16[512,256]{1,0:T(8,128)(2,1)S(1)} %get-tuple-element.408.key_ref, bf16[512,256]{1,0:T(8,128)(2,1)S(1)} %copy-done.7, ...), custom_call_target="tpu_custom_call" | custom-call | flops 805306368 | bytes 8388608 | tf_op jit(solution)/shard_map/attention_back/pallas_call | solution.py:590
  565.5 4.9 collective-permute-done.80
  570.4 4.2 collective-permute-done.81
  579.0 3.6 collective-permute-start.82
  586.0 3.5 convolution_convert_fusion
  598.4 3.6 pick_weights.4
  604.0 4.0 pick_weights.5
  608.0 3.6 fusion.9
  616.0 3.8 all-to-all-start.3
  619.8 26.1 %expert_grads.5 = (bf16[10,64,1536]{2,1,0:T(8,128)(2,1)}, bf16[10,64,1536]{2,1,0:T(8,128)(2,1)}) custom-call(s32[2]{0:T(128)} %pad_add_fusion.1.place_ref, bf16[256,1536]{1,0:T(8,128)(2,1)} %bitcast.261, bf16[256,1536]{1,0:T(8,128)(2,1)} %collective-permute-done.5.refs_5_.refs_1_, bf16[256,1536]{1,0:T(8,128)(2,1)} %copy-done.96, ...), custom_call_target="tpu_custom_call" | custom-call | flops 16106127360 | bytes 23068672 | tf_op jit(solution)/shard_map/expert_grads/pallas_call | solution.py:443
  652.0 8.3 %collective-permute-done.90 = bf16[4,2,48,640]{3,2,1,0:T(8,128)(2,1)S(1)} collective-permute-done((bf16[4,2,48,640]{3,2,1,0:T(8,128)(2,1)S(1)}, bf16[4,2,48,640]{3,2,1,0:T(8,128)(2,1)S(1)}, u32[]{:S(2)}, u32[]{:S(2)}) %collective-permute-start.90) | collective-permute-done | bytes 491552 | tf_op jit(solution)/shard_map/ppermute | solution.py:40
  674.2 4.9 unpack_experts.2
  701.2 6.2 collective-permute-start.100
  707.4 4.0 convert_add_fusion
  711.4 4.8 unpack_experts.3
  (560 shorter events, 235.0 us)
Async XLA Ops:
  0.7 30.6 %collective-permute-start.4 = (bf16[256,1536]{1,0:T(8,128)(2,1)}, bf16[256,1536]{1,0:T(8,128)(2,1)}, u32[]{:S(2)}, u32[]{:S(2)}) collective-permute-start(bf16[256,1536]{1,0:T(8,128)(2,1)} %bitcast.258), channel_id=1, source_target_pairs={{0,2},{2,4},{4,6},{6,0},{1,3},{3,5},{5,7},{7,1},{8,10},{10,12},{12... | collective-permute-start | bytes 2359304 | tf_op jit(solution)/shard_map/ppermute | solution.py:40
  2.9 28.5 %collective-permute-start.5 = (bf16[256,1536]{1,0:T(8,128)(2,1)}, bf16[256,1536]{1,0:T(8,128)(2,1)}, u32[]{:S(2)}, u32[]{:S(2)}) collective-permute-start(bf16[256,1536]{1,0:T(8,128)(2,1)} %bitcast.259), channel_id=1, source_target_pairs={{0,16},{16,0},{1,17},{17,1},{2,18},{18,2},{3,19},{19,3},{4,20},{20... | collective-permute-start | bytes 2359304 | tf_op jit(solution)/shard_map/ppermute | solution.py:40
  12.3 54.4 %collective-permute-start.10 = (bf16[10,64,1536]{2,1,0:T(8,128)(2,1)}, bf16[10,64,1536]{2,1,0:T(8,128)(2,1)}, u32[]{:S(2)}, u32[]{:S(2)}) collective-permute-start(bf16[10,64,1536]{2,1,0:T(8,128)(2,1)} %refs_12_.3), channel_id=1, source_target_pairs={{0,1},{1,0},{2,3},{3,2},{4,5},{5,4},{6,7},{7,6},{8,9},{9,8},{10,11... | collective-permute-start | bytes 5898248 | tf_op jit(solution)/shard_map/ppermute | solution.py:40
  31.5 34.5 %collective-permute-start.6 = (bf16[2,2,48,1152]{3,2,1,0:T(8,128)(2,1)S(1)}, bf16[2,2,48,1152]{3,2,1,0:T(8,128)(2,1)S(1)}, u32[]{:S(2)}, u32[]{:S(2)}) collective-permute-start(bf16[2,2,48,1152]{3,2,1,0:T(8,128)(2,1)S(1)} %fusion.33.refs_0_), channel_id=1, source_target_pairs={{0,1},{1,0},{2,3},{3,2},{4,5},{5,4},{6,7},{7,6},{8,9},{9,8},{10,11... | collective-permute-start | bytes 1327112 | tf_op jit(solution)/shard_map/ppermute | solution.py:40
  66.7 53.7 %all-to-all-start = ((bf16[4,192,1280]{2,1,0:T(8,128)(2,1)}), bf16[4,192,1280]{2,1,0:T(8,128)(2,1)}, u32[]{:S(2)}, u32[]{:S(2)}) async-start(bf16[4,192,1280]{2,1,0:T(8,128)(2,1)} %pack_experts.2), calls=%async_computation | async-start | bytes 3932160 | tf_op jit(solution)/shard_map/all_to_all | solution.py:706
  120.4 53.8 %all-to-all-start.1 = ((bf16[4,192,1280]{2,1,0:T(8,128)(2,1)}), bf16[4,192,1280]{2,1,0:T(8,128)(2,1)}, u32[]{:S(2)}, u32[]{:S(2)}) async-start(bf16[4,192,1280]{2,1,0:T(8,128)(2,1)} %pack_experts.3), calls=%async_computation.1 | async-start | bytes 3932160 | tf_op jit(solution)/shard_map/all_to_all | solution.py:716
  134.3 39.9 %collective-permute-start.21 = (bf16[4,192,1280]{2,1,0:T(8,128)(2,1)}, bf16[4,192,1280]{2,1,0:T(8,128)(2,1)}, u32[]{:S(2)}, u32[]{:S(2)}) collective-permute-start(bf16[4,192,1280]{2,1,0:T(8,128)(2,1)} %all-to-all-done.refs_8_), channel_id=1, source_target_pairs={{0,1},{1,0},{2,3},{3,2},{4,5},{5,4},{6,7},{7,6},{8,9},{9,8},{10,11... | collective-permute-start | bytes 5898248 | tf_op jit(solution)/shard_map/ppermute | solution.py:40
  183.9 44.3 %collective-permute-start.30 = (bf16[4,192,1280]{2,1,0:T(8,128)(2,1)}, bf16[4,192,1280]{2,1,0:T(8,128)(2,1)}, u32[]{:S(2)}, u32[]{:S(2)}) collective-permute-start(bf16[4,192,1280]{2,1,0:T(8,128)(2,1)} %all-to-all-done.1.refs_10_), channel_id=1, source_target_pairs={{0,1},{1,0},{2,3},{3,2},{4,5},{5,4},{6,7},{7,6},{8,9},{9,8},{10,11... | collective-permute-start | bytes 5898248 | tf_op jit(solution)/shard_map/ppermute | solution.py:40
  193.9 34.4 %collective-permute-start.28 = (bf16[256,1664]{1,0:T(8,128)(2,1)}, bf16[256,1664]{1,0:T(8,128)(2,1)}, u32[]{:S(2)}, u32[]{:S(2)}) collective-permute-start(bf16[256,1664]{1,0:T(8,128)(2,1)} %concatenate.52.refs_0_), channel_id=1, source_target_pairs={{0,16},{16,0},{1,17},{17,1},{2,18},{18,2},{3,19},{19,3},{4,20},{20... | collective-permute-start | bytes 2555912 | tf_op jit(solution)/shard_map/ppermute | solution.py:40
  194.1 34.1 %collective-permute-start.29 = (bf16[256,1664]{1,0:T(8,128)(2,1)}, bf16[256,1664]{1,0:T(8,128)(2,1)}, u32[]{:S(2)}, u32[]{:S(2)}) collective-permute-start(bf16[256,1664]{1,0:T(8,128)(2,1)} %concatenate.52.refs_0_), channel_id=1, source_target_pairs={{0,2},{2,4},{4,6},{6,0},{1,3},{3,5},{5,7},{7,1},{8,10},{10,12},{12... | collective-permute-start | bytes 2555912 | tf_op jit(solution)/shard_map/ppermute | solution.py:40
  195.6 32.6 %collective-permute-start.31 = (bf16[256,1664]{1,0:T(8,128)(2,1)}, bf16[256,1664]{1,0:T(8,128)(2,1)}, u32[]{:S(2)}, u32[]{:S(2)}) collective-permute-start(bf16[256,1664]{1,0:T(8,128)(2,1)} %concatenate.52.refs_0_), channel_id=1, source_target_pairs={{0,8},{8,0},{1,9},{9,1},{2,10},{10,2},{3,11},{11,3},{4,12},{12,4},... | collective-permute-start | bytes 2555912 | tf_op jit(solution)/shard_map/ppermute | solution.py:40
  230.1 39.5 %collective-permute-start.34 = (bf16[256,1536]{1,0:T(8,128)(2,1)}, bf16[256,1536]{1,0:T(8,128)(2,1)}, u32[]{:S(2)}, u32[]{:S(2)}) collective-permute-start(bf16[256,1536]{1,0:T(8,128)(2,1)} %collective-permute-done.4.refs_4_), channel_id=1, source_target_pairs={{0,2},{2,4},{4,6},{6,0},{1,3},{3,5},{5,7},{7,1},{8,10},{10,12},{12... | collective-permute-start | bytes 2359304 | tf_op jit(solution)/shard_map/ppermute | solution.py:40
  231.6 38.1 %collective-permute-start.33 = (bf16[256,1664]{1,0:T(8,128)(2,1)}, bf16[256,1664]{1,0:T(8,128)(2,1)}, u32[]{:S(2)}, u32[]{:S(2)}) collective-permute-start(bf16[256,1664]{1,0:T(8,128)(2,1)} %collective-permute-done.29.refs_0_.refs_4_), channel_id=1, source_target_pairs={{0,2},{2,4},{4,6},{6,0},{1,3},{3,5},{5,7},{7,1},{8,10},{10,12},{12... | collective-permute-start | bytes 2555912 | tf_op jit(solution)/shard_map/ppermute | solution.py:40
  233.3 36.4 %collective-permute-start.35 = (bf16[256,1664]{1,0:T(8,128)(2,1)}, bf16[256,1664]{1,0:T(8,128)(2,1)}, u32[]{:S(2)}, u32[]{:S(2)}) collective-permute-start(bf16[256,1664]{1,0:T(8,128)(2,1)} %collective-permute-done.29.refs_0_.refs_4_), channel_id=1, source_target_pairs={{0,16},{16,0},{1,17},{17,1},{2,18},{18,2},{3,19},{19,3},{4,20},{20... | collective-permute-start | bytes 2555912 | tf_op jit(solution)/shard_map/ppermute | solution.py:40
  271.1 43.7 %collective-permute-start.40 = (bf16[256,1536]{1,0:T(8,128)(2,1)}, bf16[256,1536]{1,0:T(8,128)(2,1)}, u32[]{:S(2)}, u32[]{:S(2)}) collective-permute-start(bf16[256,1536]{1,0:T(8,128)(2,1)} %collective-permute-done.34.refs_4_.refs_8_), channel_id=1, source_target_pairs={{0,16},{16,0},{1,17},{17,1},{2,18},{18,2},{3,19},{19,3},{4,20},{20... | collective-permute-start | bytes 2359304 | tf_op jit(solution)/shard_map/ppermute | solution.py:40
  272.4 42.4 %collective-permute-start.41 = (bf16[256,1536]{1,0:T(8,128)(2,1)}, bf16[256,1536]{1,0:T(8,128)(2,1)}, u32[]{:S(2)}, u32[]{:S(2)}) collective-permute-start(bf16[256,1536]{1,0:T(8,128)(2,1)} %collective-permute-done.34.refs_4_.refs_8_), channel_id=1, source_target_pairs={{0,2},{2,4},{4,6},{6,0},{1,3},{3,5},{5,7},{7,1},{8,10},{10,12},{12... | collective-permute-start | bytes 2359304 | tf_op jit(solution)/shard_map/ppermute | solution.py:40
  275.2 39.6 %collective-permute-start.39 = (bf16[256,1664]{1,0:T(8,128)(2,1)}, bf16[256,1664]{1,0:T(8,128)(2,1)}, u32[]{:S(2)}, u32[]{:S(2)}) collective-permute-start(bf16[256,1664]{1,0:T(8,128)(2,1)} %collective-permute-done.33.refs_0_.refs_8_), channel_id=1, source_target_pairs={{0,2},{2,4},{4,6},{6,0},{1,3},{3,5},{5,7},{7,1},{8,10},{10,12},{12... | collective-permute-start | bytes 2555912 | tf_op jit(solution)/shard_map/ppermute | solution.py:40
  276.6 38.3 %collective-permute-start.43 = (bf16[256,1664]{1,0:T(8,128)(2,1)}, bf16[256,1664]{1,0:T(8,128)(2,1)}, u32[]{:S(2)}, u32[]{:S(2)}) collective-permute-start(bf16[256,1664]{1,0:T(8,128)(2,1)} %collective-permute-done.33.refs_0_.refs_8_), channel_id=1, source_target_pairs={{0,16},{16,0},{1,17},{17,1},{2,18},{18,2},{3,19},{19,3},{4,20},{20... | collective-permute-start | bytes 2555912 | tf_op jit(solution)/shard_map/ppermute | solution.py:40
  277.8 37.1 %collective-permute-start.42 = (bf16[2,256,1536]{2,1,0:T(8,128)(2,1)}, bf16[2,256,1536]{2,1,0:T(8,128)(2,1)}, u32[]{:S(2)}, u32[]{:S(2)}) collective-permute-start(bf16[2,256,1536]{2,1,0:T(8,128)(2,1)} %get-tuple-element.465), channel_id=1, source_target_pairs={{0,8},{8,0},{1,9},{9,1},{2,10},{10,2},{3,11},{11,3},{4,12},{12,4},... | collective-permute-start | bytes 4718600 | tf_op jit(solution)/shard_map/ppermute | solution.py:40
  322.1 40.7 %collective-permute-start.50 = (bf16[256,1536]{1,0:T(8,128)(2,1)}, bf16[256,1536]{1,0:T(8,128)(2,1)}, u32[]{:S(2)}, u32[]{:S(2)}) collective-permute-start(bf16[256,1536]{1,0:T(8,128)(2,1)} %collective-permute-done.40.refs_5_.refs_9_), channel_id=1, source_target_pairs={{0,2},{2,4},{4,6},{6,0},{1,3},{3,5},{5,7},{7,1},{8,10},{10,12},{12... | collective-permute-start | bytes 2359304 | tf_op jit(solution)/shard_map/ppermute | solution.py:40
  323.3 40.0 %collective-permute-start.51 = (bf16[256,1536]{1,0:T(8,128)(2,1)}, bf16[256,1536]{1,0:T(8,128)(2,1)}, u32[]{:S(2)}, u32[]{:S(2)}) collective-permute-start(bf16[256,1536]{1,0:T(8,128)(2,1)} %collective-permute-done.41.refs_4_.refs_12_), channel_id=1, source_target_pairs={{0,8},{8,0},{1,9},{9,1},{2,10},{10,2},{3,11},{11,3},{4,12},{12,4},... | collective-permute-start | bytes 2359304 | tf_op jit(solution)/shard_map/ppermute | solution.py:40
  323.5 39.7 %collective-permute-start.52 = (bf16[2,256,1536]{2,1,0:T(8,128)(2,1)}, bf16[2,256,1536]{2,1,0:T(8,128)(2,1)}, u32[]{:S(2)}, u32[]{:S(2)}) collective-permute-start(bf16[2,256,1536]{2,1,0:T(8,128)(2,1)} %get-tuple-element.487), channel_id=1, source_target_pairs={{0,8},{8,0},{1,9},{9,1},{2,10},{10,2},{3,11},{11,3},{4,12},{12,4},... | collective-permute-start | bytes 4718600 | tf_op jit(solution)/shard_map/ppermute | solution.py:40
  323.8 39.5 %collective-permute-start.53 = (bf16[256,1664]{1,0:T(8,128)(2,1)}, bf16[256,1664]{1,0:T(8,128)(2,1)}, u32[]{:S(2)}, u32[]{:S(2)}) collective-permute-start(bf16[256,1664]{1,0:T(8,128)(2,1)} %collective-permute-done.39.refs_0_.refs_12_), channel_id=1, source_target_pairs={{0,16},{16,0},{1,17},{17,1},{2,18},{18,2},{3,19},{19,3},{4,20},{20... | collective-permute-start | bytes 2555912 | tf_op jit(solution)/shard_map/ppermute | solution.py:40
  325.6 37.7 %collective-permute-start.49 = (bf16[256,1536]{1,0:T(8,128)(2,1)}, bf16[256,1536]{1,0:T(8,128)(2,1)}, u32[]{:S(2)}, u32[]{:S(2)}) collective-permute-start(bf16[256,1536]{1,0:T(8,128)(2,1)} %fusion.13), channel_id=1, source_target_pairs={{0,16},{16,0},{1,17},{17,1},{2,18},{18,2},{3,19},{19,3},{4,20},{20... | collective-permute-start | bytes 2359304 | tf_op jit(solution)/shard_map/ppermute | solution.py:40
  362.9 50.6 %collective-permute-start.59 = (bf16[256,1536]{1,0:T(8,128)(2,1)}, bf16[256,1536]{1,0:T(8,128)(2,1)}, u32[]{:S(2)}, u32[]{:S(2)}) collective-permute-start(bf16[256,1536]{1,0:T(8,128)(2,1)} %get-tuple-element.782), channel_id=1, source_target_pairs={{0,16},{16,0},{1,17},{17,1},{2,18},{18,2},{3,19},{19,3},{4,20},{20... | collective-permute-start | bytes 2359304 | tf_op jit(solution)/shard_map/ppermute | solution.py:40
  373.2 40.3 %collective-permute-start.60 = (bf16[2,256,1536]{2,1,0:T(8,128)(2,1)}, bf16[2,256,1536]{2,1,0:T(8,128)(2,1)}, u32[]{:S(2)}, u32[]{:S(2)}) collective-permute-start(bf16[2,256,1536]{2,1,0:T(8,128)(2,1)} %get-tuple-element.510), channel_id=1, source_target_pairs={{0,8},{8,0},{1,9},{9,1},{2,10},{10,2},{3,11},{11,3},{4,12},{12,4},... | collective-permute-start | bytes 4718600 | tf_op jit(solution)/shard_map/ppermute | solution.py:40
  373.6 39.8 %collective-permute-start.61 = (bf16[256,1536]{1,0:T(8,128)(2,1)}, bf16[256,1536]{1,0:T(8,128)(2,1)}, u32[]{:S(2)}, u32[]{:S(2)}) collective-permute-start(bf16[256,1536]{1,0:T(8,128)(2,1)} %fusion.19), channel_id=1, source_target_pairs={{0,16},{16,0},{1,17},{17,1},{2,18},{18,2},{3,19},{19,3},{4,20},{20... | collective-permute-start | bytes 2359304 | tf_op jit(solution)/shard_map/ppermute | solution.py:40
  374.9 38.6 %collective-permute-start.62 = (bf16[256,1536]{1,0:T(8,128)(2,1)}, bf16[256,1536]{1,0:T(8,128)(2,1)}, u32[]{:S(2)}, u32[]{:S(2)}) collective-permute-start(bf16[256,1536]{1,0:T(8,128)(2,1)} %add_convert_fusion.27), channel_id=1, source_target_pairs={{0,2},{2,4},{4,6},{6,0},{1,3},{3,5},{5,7},{7,1},{8,10},{10,12},{12... | collective-permute-start | bytes 2359304 | tf_op jit(solution)/shard_map/ppermute | solution.py:40
  377.2 38.0 %collective-permute-start.58 = (bf16[256,1536]{1,0:T(8,128)(2,1)}, bf16[256,1536]{1,0:T(8,128)(2,1)}, u32[]{:S(2)}, u32[]{:S(2)}) collective-permute-start(bf16[256,1536]{1,0:T(8,128)(2,1)} %fusion.18), channel_id=1, source_target_pairs={{0,16},{16,0},{1,17},{17,1},{2,18},{18,2},{3,19},{19,3},{4,20},{20... | collective-permute-start | bytes 2359304 | tf_op jit(solution)/shard_map/ppermute | solution.py:40
  428.6 28.9 %collective-permute-start.65 = (bf16[256,1536]{1,0:T(8,128)(2,1)}, bf16[256,1536]{1,0:T(8,128)(2,1)}, u32[]{:S(2)}, u32[]{:S(2)}) collective-permute-start(bf16[256,1536]{1,0:T(8,128)(2,1)} %get-tuple-element.542), channel_id=1, source_target_pairs={{0,16},{16,0},{1,17},{17,1},{2,18},{18,2},{3,19},{19,3},{4,20},{20... | collective-permute-start | bytes 2359304 | tf_op jit(solution)/shard_map/ppermute | solution.py:40
  428.9 28.6 %collective-permute-start.66 = (bf16[256,1536]{1,0:T(8,128)(2,1)}, bf16[256,1536]{1,0:T(8,128)(2,1)}, u32[]{:S(2)}, u32[]{:S(2)}) collective-permute-start(bf16[256,1536]{1,0:T(8,128)(2,1)} %add_convert_fusion.23), channel_id=1, source_target_pairs={{0,2},{2,4},{4,6},{6,0},{1,3},{3,5},{5,7},{7,1},{8,10},{10,12},{12... | collective-permute-start | bytes 2359304 | tf_op jit(solution)/shard_map/ppermute | solution.py:40
  430.1 27.4 %collective-permute-start.67 = (bf16[2,256,1536]{2,1,0:T(8,128)(2,1)}, bf16[2,256,1536]{2,1,0:T(8,128)(2,1)}, u32[]{:S(2)}, u32[]{:S(2)}) collective-permute-start(bf16[2,256,1536]{2,1,0:T(8,128)(2,1)} %get-tuple-element.544), channel_id=1, source_target_pairs={{0,8},{8,0},{1,9},{9,1},{2,10},{10,2},{3,11},{11,3},{4,12},{12,4},... | collective-permute-start | bytes 4718600 | tf_op jit(solution)/shard_map/ppermute | solution.py:40
  430.7 26.7 %collective-permute-start.68 = (f32[4,40,256]{2,1,0:T(8,128)S(1)}, f32[4,40,256]{2,1,0:T(8,128)S(1)}, u32[]{:S(2)}, u32[]{:S(2)}) collective-permute-start(f32[4,40,256]{2,1,0:T(8,128)S(1)} %slice_bitcast_fusion.6), channel_id=1, source_target_pairs={{0,16},{16,0},{1,17},{17,1},{2,18},{18,2},{3,19},{19,3},{4,20},{20... | collective-permute-start | bytes 491528 | tf_op jit(solution)/shard_map/ppermute | solution.py:40
  465.1 37.5 %collective-permute-start.69 = (bf16[256,1536]{1,0:T(8,128)(2,1)}, bf16[256,1536]{1,0:T(8,128)(2,1)}, u32[]{:S(2)}, u32[]{:S(2)}) collective-permute-start(bf16[256,1536]{1,0:T(8,128)(2,1)} %add_convert_fusion.15), channel_id=1, source_target_pairs={{0,2},{2,4},{4,6},{6,0},{1,3},{3,5},{5,7},{7,1},{8,10},{10,12},{12... | collective-permute-start | bytes 2359304 | tf_op jit(solution)/shard_map/ppermute | solution.py:40
  465.4 37.1 %collective-permute-start.70 = (bf16[256,1536]{1,0:T(8,128)(2,1)}, bf16[256,1536]{1,0:T(8,128)(2,1)}, u32[]{:S(2)}, u32[]{:S(2)}) collective-permute-start(bf16[256,1536]{1,0:T(8,128)(2,1)} %get-tuple-element.568), channel_id=1, source_target_pairs={{0,16},{16,0},{1,17},{17,1},{2,18},{18,2},{3,19},{19,3},{4,20},{20... | collective-permute-start | bytes 2359304 | tf_op jit(solution)/shard_map/ppermute | solution.py:40
  465.8 36.7 %collective-permute-start.71 = (bf16[256,1536]{1,0:T(8,128)(2,1)}, bf16[256,1536]{1,0:T(8,128)(2,1)}, u32[]{:S(2)}, u32[]{:S(2)}) collective-permute-start(bf16[256,1536]{1,0:T(8,128)(2,1)} %add_convert_fusion.17), channel_id=1, source_target_pairs={{0,2},{2,4},{4,6},{6,0},{1,3},{3,5},{5,7},{7,1},{8,10},{10,12},{12... | collective-permute-start | bytes 2359304 | tf_op jit(solution)/shard_map/ppermute | solution.py:40
  466.6 36.0 %collective-permute-start.75 = (bf16[2,192,1280]{2,1,0:T(8,128)(2,1)}, bf16[2,192,1280]{2,1,0:T(8,128)(2,1)}, u32[]{:S(2)}, u32[]{:S(2)}) collective-permute-start(bf16[2,192,1280]{2,1,0:T(8,128)(2,1)} %get-tuple-element.571), channel_id=1, source_target_pairs={{0,1},{1,0},{2,3},{3,2},{4,5},{5,4},{6,7},{7,6},{8,9},{9,8},{10,11... | collective-permute-start | bytes 2949128 | tf_op jit(solution)/shard_map/ppermute | solution.py:40
  468.0 34.5 %collective-permute-start.74 = (f32[40,256]{1,0:T(8,128)S(1)}, f32[40,256]{1,0:T(8,128)S(1)}, u32[]{:S(2)}, u32[]{:S(2)}) collective-permute-start(f32[40,256]{1,0:T(8,128)S(1)} %bitcast_add_fusion.3), channel_id=1, source_target_pairs={{0,2},{2,4},{4,6},{6,0},{1,3},{3,5},{5,7},{7,1},{8,10},{10,12},{12... | collective-permute-start | bytes 122888 | tf_op jit(solution)/shard_map/ppermute | solution.py:40
  548.0 26.7 %collective-permute-start.81 = (bf16[2,4,48,1536]{3,2,1,0:T(8,128)(2,1)}, bf16[2,4,48,1536]{3,2,1,0:T(8,128)(2,1)}, u32[]{:S(2)}, u32[]{:S(2)}) collective-permute-start(bf16[2,4,48,1536]{3,2,1,0:T(8,128)(2,1)} %get-tuple-element.620), channel_id=1, source_target_pairs={{0,16},{16,0},{1,17},{17,1},{2,18},{18,2},{3,19},{19,3},{4,20},{20... | collective-permute-start | bytes 3538952 | tf_op jit(solution)/shard_map/ppermute | solution.py:40
  549.5 43.5 %collective-permute-start.83 = (bf16[2,192,1280]{2,1,0:T(8,128)(2,1)}, bf16[2,192,1280]{2,1,0:T(8,128)(2,1)}, u32[]{:S(2)}, u32[]{:S(2)}) collective-permute-start(bf16[2,192,1280]{2,1,0:T(8,128)(2,1)} %get-tuple-element.624), channel_id=1, source_target_pairs={{0,1},{1,0},{2,3},{3,2},{4,5},{5,4},{6,7},{7,6},{8,9},{9,8},{10,11... | collective-permute-start | bytes 2949128 | tf_op jit(solution)/shard_map/ppermute | solution.py:40
  550.3 42.8 %collective-permute-start.84 = (bf16[256,1536]{1,0:T(8,128)(2,1)}, bf16[256,1536]{1,0:T(8,128)(2,1)}, u32[]{:S(2)}, u32[]{:S(2)}) collective-permute-start(bf16[256,1536]{1,0:T(8,128)(2,1)} %add_convert_fusion.8), channel_id=1, source_target_pairs={{0,2},{2,4},{4,6},{6,0},{1,3},{3,5},{5,7},{7,1},{8,10},{10,12},{12... | collective-permute-start | bytes 2359304 | tf_op jit(solution)/shard_map/ppermute | solution.py:40
  550.3 61.4 %collective-permute-start.85 = (bf16[256,1536]{1,0:T(8,128)(2,1)}, bf16[256,1536]{1,0:T(8,128)(2,1)}, u32[]{:S(2)}, u32[]{:S(2)}) collective-permute-start(bf16[256,1536]{1,0:T(8,128)(2,1)} %get-tuple-element.634), channel_id=1, source_target_pairs={{0,16},{16,0},{1,17},{17,1},{2,18},{18,2},{3,19},{19,3},{4,20},{20... | collective-permute-start | bytes 2359304 | tf_op jit(solution)/shard_map/ppermute | solution.py:40
  551.5 62.5 %all-to-all-start.2 = ((bf16[4,192,1280]{2,1,0:T(8,128)(2,1)}), bf16[4,192,1280]{2,1,0:T(8,128)(2,1)}, u32[]{:S(2)}, u32[]{:S(2)}) async-start(bf16[4,192,1280]{2,1,0:T(8,128)(2,1)} %pad_maximum_fusion), calls=%async_computation.2 | async-start | bytes 3932160 | tf_op jit(solution)/shard_map/all_to_all | solution.py:942
  591.0 57.0 %collective-permute-start.88 = (bf16[4,48,1536]{2,1,0:T(8,128)(2,1)}, bf16[4,48,1536]{2,1,0:T(8,128)(2,1)}, u32[]{:S(2)}, u32[]{:S(2)}) collective-permute-start(bf16[4,48,1536]{2,1,0:T(8,128)(2,1)} %get-tuple-element.785), channel_id=1, source_target_pairs={{0,1},{1,0},{2,3},{3,2},{4,5},{5,4},{6,7},{7,6},{8,9},{9,8},{10,11... | collective-permute-start | bytes 1769480 | tf_op jit(solution)/shard_map/ppermute | solution.py:40
  614.0 33.8 %collective-permute-start.86 = (bf16[2,4,2,48,768]{4,3,2,1,0:T(8,128)(2,1)}, bf16[2,4,2,48,768]{4,3,2,1,0:T(8,128)(2,1)S(1)}, u32[]{:S(2)}, u32[]{:S(2)}) collective-permute-start(bf16[2,4,2,48,768]{4,3,2,1,0:T(8,128)(2,1)} %get-tuple-element.662), channel_id=1, source_target_pairs={{0,16},{16,0},{1,17},{17,1},{2,18},{18,2},{3,19},{19,3},{4,20},{20... | collective-permute-start | bytes 3538952 | tf_op jit(solution)/shard_map/ppermute | solution.py:40
  615.2 30.7 %collective-permute-start.87 = (bf16[2,4,2,48,640]{4,3,2,1,0:T(8,128)(2,1)}, bf16[2,4,2,48,640]{4,3,2,1,0:T(8,128)(2,1)}, u32[]{:S(2)}, u32[]{:S(2)}) collective-permute-start(bf16[2,4,2,48,640]{4,3,2,1,0:T(8,128)(2,1)} %get-tuple-element.664), channel_id=1, source_target_pairs={{0,1},{1,0},{2,3},{3,2},{4,5},{5,4},{6,7},{7,6},{8,9},{9,8},{10,11... | collective-permute-start | bytes 2949128 | tf_op jit(solution)/shard_map/ppermute | solution.py:40
  616.0 48.7 %all-to-all-start.3 = ((bf16[4,192,1280]{2,1,0:T(8,128)(2,1)}), bf16[4,192,1280]{2,1,0:T(8,128)(2,1)S(1)}, u32[]{:S(2)}, u32[]{:S(2)}) async-start(bf16[4,192,1280]{2,1,0:T(8,128)(2,1)} %pad_maximum_fusion.1), calls=%async_computation.3 | async-start | bytes 3932160 | tf_op jit(solution)/shard_map/all_to_all | solution.py:993
  649.2 58.2 %collective-permute-start.101 = (bf16[10,64,1536]{2,1,0:T(8,128)(2,1)}, bf16[10,64,1536]{2,1,0:T(8,128)(2,1)}, u32[]{:S(2)}, u32[]{:S(2)}) collective-permute-start(bf16[10,64,1536]{2,1,0:T(8,128)(2,1)} %get-tuple-element.694), channel_id=1, source_target_pairs={{0,1},{1,0},{2,3},{3,2},{4,5},{5,4},{6,7},{7,6},{8,9},{9,8},{10,11... | collective-permute-start | bytes 5898248 | tf_op jit(solution)/shard_map/ppermute | solution.py:40
  (160 other events, 1946.6 us)
